TPU v7x, 32 devices: a whole 2x2x4 slice. The times are simulated.
32 devices in a mesh: groups: 2 (over x), expert: 4 (over y, core), dp: 4 (over z).
Axes of the slice: x: 2, y: 2, z: 4, core: 2. Of those that a mesh axis runs over, the one named last changes fastest.
Arguments:
- tokens: bfloat16 [4096, 2048], P(('groups', 'expert', 'dp')), parts along dimension 0, may hold values from -6 to 6
- route_ids: int32 [4096, 2], P(('groups', 'expert', 'dp')), parts along dimension 0, may hold values from 0 to 3, all different within a row; in each aligned block of 128 rows (0 to 127, 128 to 255, ...) at most 128 rows name the same one
- route_probs: bfloat16 [4096, 2], P(('groups', 'expert', 'dp')), parts along dimension 0, may hold values from 0.049804688 to 1
- cotangent: bfloat16 [4096, 2048], P(('groups', 'expert', 'dp')), parts along dimension 0, may hold values from -6 to 6
- w_gate_up: bfloat16 [4, 2, 384, 2048], P('expert', None, 'dp'), may hold values from -0.125 to 0.125
- w_down: bfloat16 [4, 384, 2048], P('expert', 'dp'), may hold values from -0.3125 to 0.3125
Outputs:
- grad_tokens: bfloat16 [4096, 2048], P(('groups', 'expert', 'dp')), parts along dimension 0
- grad_gate_up: float32 [8, 2, 384, 2048], P(('groups', 'expert'), None, 'dp'), parts along dimension 0
- grad_down: float32 [8, 384, 2048], P(('groups', 'expert'), 'dp'), parts along dimension 0
There are 2 independent parts, one for each index of `groups`. A program takes and returns all parts, laid end to end along the dimension named above; an argument that names none is the same for every part. Nothing has to cross between parts.
Inputs may be any that keep to these rules, and one draw needn't show every extreme that they name: `route_ids`: each row names 2 different experts; among the 128 rows of one device no expert is named by more than 128 rows.
All inputs are finite; a program needn't handle non-finite values.
Results may differ from a plain program's by a relative error of at most 0.0095.
Values may be sent and summed in bfloat16 or wider, within the bound.
No kernel may reach another device: no remote copies, remote signals or barrier semaphores. Data moves between devices by JAX's collectives and lax.ppermute only.
A program may use at most 128 MiB of HBM per device.

v0:
```python
import jax
import jax.numpy as jnp
from jax import lax
from jax.sharding import PartitionSpec as P


def passed_along(block, axis, distance):
    devices = range(lax.axis_size(axis))
    route = [((i - distance) % len(devices), i) for i in devices]
    return lax.ppermute(block, axis, route)


def expert_pass(state, weights, expert, rows):
    accum, all_gate_up, all_down = state
    gate_up = weights[0][0]
    down = weights[1][0]
    rows_x, rows_dy, rows_probs, rows_ids = rows
    topk = rows_ids.shape[1]
    total = rows_ids.shape[0] * topk
    table = (total + 127) // 128 * 128
    mask = rows_ids.reshape(-1) == expert
    flags = mask.astype(jnp.int32)
    position = jnp.cumsum(flags) - 1
    count = jnp.sum(flags)
    target = jnp.where(mask, position, table)
    pair_index = jnp.arange(total, dtype=jnp.int32)
    table_rows = jnp.zeros((table,), jnp.int32).at[target].set(pair_index // topk, mode="drop")
    table_weight = (
        jnp.zeros((table,), jnp.float32)
        .at[target]
        .set(rows_probs.reshape(-1).astype(jnp.float32), mode="drop")
    )
    block_total = (count + 127) // 128

    def one_block(index, inner):
        accum, part_gate_up, part_down = inner
        start = index * 128
        slot_rows = lax.dynamic_slice_in_dim(table_rows, start, 128)
        slot_weight = lax.dynamic_slice_in_dim(table_weight, start, 128)
        block_x = rows_x[slot_rows]
        block_dy = rows_dy[slot_rows]
        projected = jnp.einsum("rd,chd->crh", block_x, gate_up, preferred_element_type=jnp.float32)
        gate_act = projected[0]
        up_act = projected[1]
        sigma = jax.nn.sigmoid(gate_act)
        silu_gate = gate_act * sigma
        weighted = (slot_weight[:, None] * silu_gate * up_act).astype(jnp.bfloat16)
        back_hidden = slot_weight[:, None] * jnp.einsum(
            "rd,hd->rh", block_dy, down, preferred_element_type=jnp.float32
        )
        gate_grad = (back_hidden * up_act * sigma * (1.0 + gate_act * (1.0 - sigma))).astype(
            jnp.bfloat16
        )
        up_grad = (back_hidden * silu_gate).astype(jnp.bfloat16)
        both = jnp.stack([gate_grad, up_grad])
        part_down = part_down + jnp.einsum(
            "rh,rd->hd", weighted, block_dy, preferred_element_type=jnp.float32
        )
        part_gate_up = part_gate_up + jnp.einsum(
            "crh,rd->chd", both, block_x, preferred_element_type=jnp.float32
        )
        contrib = jnp.einsum("crh,chd->rd", both, gate_up, preferred_element_type=jnp.float32)
        accum = accum.at[slot_rows].add(contrib)
        return (accum, part_gate_up, part_down)

    begin = (accum, jnp.zeros(gate_up.shape, jnp.float32), jnp.zeros(down.shape, jnp.float32))
    accum, part_gate_up, part_down = lax.fori_loop(0, block_total, one_block, begin)
    all_gate_up = lax.dynamic_update_index_in_dim(all_gate_up, part_gate_up, expert, 0)
    all_down = lax.dynamic_update_index_in_dim(all_down, part_down, expert, 0)
    return (accum, all_gate_up, all_down)


def body(tokens, route_ids, route_probs, cotangent, w_gate_up, w_down):
    rows_x, rows_dy, rows_probs = (
        lax.all_gather(tokens, "dp", axis=0, tiled=True),
        lax.all_gather(cotangent, "dp", axis=0, tiled=True),
        lax.all_gather(route_probs, "dp", axis=0, tiled=True),
    )
    rows_ids = lax.all_gather(route_ids, "dp", axis=0, tiled=True)
    rows = (rows_x, rows_dy, rows_probs, rows_ids)
    owners = lax.axis_size("expert")
    owner_pos = lax.axis_index("expert")
    hid_block = w_down.shape[1]
    width = rows_x.shape[1]
    state = (
        jnp.zeros((rows_x.shape[0], width), jnp.float32),
        jnp.zeros((owners, 2, hid_block, width), jnp.float32),
        jnp.zeros((owners, hid_block, width), jnp.float32),
    )
    weights = (w_gate_up, w_down)

    def turn(step, carry):
        state, held = carry
        state = expert_pass(state, held, jnp.mod(owner_pos - step, owners), rows)
        held = passed_along((held[0], held[1]), "expert", 1)
        return (state, held)

    state, held = lax.fori_loop(0, owners - 1, turn, (state, weights))
    state = expert_pass(state, held, jnp.mod(owner_pos - (owners - 1), owners), rows)
    accum, all_gate_up, all_down = state
    grad_gate_up, grad_down = (
        lax.psum_scatter(
            all_gate_up.astype(jnp.bfloat16), "expert", scatter_dimension=0, tiled=True
        ).astype(jnp.float32),
        lax.psum_scatter(
            all_down.astype(jnp.bfloat16), "expert", scatter_dimension=0, tiled=True
        ).astype(jnp.float32),
    )
    grad_tokens = lax.psum_scatter(
        accum.astype(jnp.bfloat16), "dp", scatter_dimension=0, tiled=True
    )
    return (grad_tokens, grad_gate_up, grad_down)


def solution(mesh):
    placed = (
        P(("groups", "expert", "dp"), None),
        P(("groups", "expert", "dp"), None),
        P(("groups", "expert", "dp"), None),
        P(("groups", "expert", "dp"), None),
        P("expert", None, "dp", None),
        P("expert", "dp", None),
    )
    return jax.shard_map(
        body,
        mesh=mesh,
        in_specs=placed,
        out_specs=(
            P(("groups", "expert", "dp"), None),
            P(("groups", "expert"), None, "dp", None),
            P(("groups", "expert"), "dp", None),
        ),
        check_vma=False,
    )
```

profile of v0, /device:TPU:0, one launch (start us, length us, event | category | flops | bytes accessed | tf_op | source)
XLA Modules:
  0.0 587.0 jit_solution(6757494915766360064)
XLA Ops:
  12.1 16.4 %all_gather.12 = s32[512,2]{1,0:T(8,128)S(1)} all-gather(s32[128,2]{1,0:T(8,128)S(1)} %copy.10), channel_id=1, replica_groups=mesh['groups'=2,'expert'=4,'dp'=4] {'dp'}, dimensions={0}, use_global_device_ids=true | all-gather | bytes 5120 | tf_op jit(solution)/shard_map/all_gather | solution.py:79
  30.2 14.8 %all_gather.13 = bf16[512,2]{1,0:T(8,128)(2,1)S(1)} all-gather(bf16[128,2]{1,0:T(8,128)(2,1)S(1)} %copy.11), channel_id=1, replica_groups=mesh['groups'=2,'expert'=4,'dp'=4] {'dp'}, dimensions={0}, use_global_device_ids=true | all-gather | bytes 2560 | tf_op jit(solution)/shard_map/all_gather | solution.py:77
  46.8 4.9 scatter_custom_fusion.4
  51.7 4.9 scatter_custom_fusion.5
  56.6 6.4 %all-gather.3.cloned.1.call-done = bf16[512,2048]{1,0:T(8,128)(2,1)} async-done(((bf16[128,2048]{1,0:T(8,128)(2,1)}), bf16[512,2048]{1,0:T(8,128)(2,1)}) %all-gather.3.cloned.1.call-update) | async-done | bytes 2097168 | tf_op jit(solution)/shard_map/all_gather | solution.py:76
  62.9 46.3 %all-gather.5.cloned.1.call-done = bf16[512,2048]{1,0:T(8,128)(2,1)} async-done(((bf16[128,2048]{1,0:T(8,128)(2,1)}), bf16[512,2048]{1,0:T(8,128)(2,1)}) %all-gather.5.cloned.1.call-update) | async-done | bytes 2097168 | tf_op jit(solution)/shard_map/all_gather | solution.py:75
  115.1 236.5 %while.90 = (s32[]{:T(128)}, f32[512,2048]{1,0:T(8,128)}, bf16[4,2,96,2048]{3,2,1,0:T(8,128)(2,1)}, bf16[4,96,2048]{2,1,0:T(8,128)(2,1)}, bf16[1,2,96,2048]{3,2,...) while((s32[]{:T(128)}, f32[512,2048]{1,0:T(8,128)}, ...), condition=%wide.wide.region_9.10_spmd, body=%wide.wide.region_0.9_spmd.sunk | while | flops 403962336 | bytes 51832844 | solution.py:98
  122.9 4.3 scatter_custom_fusion.23
  127.2 4.5 scatter_custom_fusion.24
  134.0 42.7 %while.91 = (s32[]{:T(128)}, f32[512,2048]{1,0:T(8,128)}, f32[2,96,2048]{2,1,0:T(8,128)}, f32[96,2048]{1,0:T(8,128)}, s32[]{:T(128)}, /*index=5*/s32[1024]{0:T(1...) while((s32[]{:T(128)}, f32[512,2048]{1,0:T(8,128)}, ...), condition=%wide.region_8.8_spmd, body=%wide.region_6.7_spmd.sunk | while | flops 403813760 | bytes 21888456 | solution.py:67
  134.1 3.3 gather_fusion.2
  141.8 2.5 convolution_bitcast_fusion.11
  144.3 6.9 %scatter_fusion.1 = f32[512,2048]{1,0:T(8,128)} fusion(f32[512,2048]{1,0:T(8,128)} %get-tuple-element.835, s32[128]{0:T(128)} %copy-done.9, f32[128,2048]{1,0:T(8,128)} %convolution_bitcast_fusion.11), kind=kCustom, calls=%fused_computation.4.clone.1 | custom fusion | flops 262144 | bytes 3146240 | tf_op jit(solution)/shard_map/while/body/eval_jaxpr/while/body/scatter-add | solution.py:63
  151.2 3.0 convolution_add_fusion.10
  155.5 3.3 gather_fusion.2
  163.2 2.5 convolution_bitcast_fusion.11
  165.6 6.9 %scatter_fusion.1 = f32[512,2048]{1,0:T(8,128)} fusion(f32[512,2048]{1,0:T(8,128)} %get-tuple-element.835, s32[128]{0:T(128)} %copy-done.9, f32[128,2048]{1,0:T(8,128)} %convolution_bitcast_fusion.11), kind=kCustom, calls=%fused_computation.4.clone.1 | custom fusion | flops 262144 | bytes 3146240 | tf_op jit(solution)/shard_map/while/body/eval_jaxpr/while/body/scatter-add | solution.py:63
  172.5 3.0 convolution_add_fusion.10
  176.7 2.6 bitcast_dynamic-update-slice_fusion.8
  187.4 4.3 scatter_custom_fusion.23
  191.7 4.5 scatter_custom_fusion.24
  198.5 85.5 %while.91 = (s32[]{:T(128)}, f32[512,2048]{1,0:T(8,128)}, f32[2,96,2048]{2,1,0:T(8,128)}, f32[96,2048]{1,0:T(8,128)}, s32[]{:T(128)}, /*index=5*/s32[1024]{0:T(1...) while((s32[]{:T(128)}, f32[512,2048]{1,0:T(8,128)}, ...), condition=%wide.region_8.8_spmd, body=%wide.region_6.7_spmd.sunk | while | flops 403813760 | bytes 21888456 | solution.py:67
  198.6 3.3 gather_fusion.2
  206.3 2.5 convolution_bitcast_fusion.11
  208.8 6.9 %scatter_fusion.1 = f32[512,2048]{1,0:T(8,128)} fusion(f32[512,2048]{1,0:T(8,128)} %get-tuple-element.835, s32[128]{0:T(128)} %copy-done.9, f32[128,2048]{1,0:T(8,128)} %convolution_bitcast_fusion.11), kind=kCustom, calls=%fused_computation.4.clone.1 | custom fusion | flops 262144 | bytes 3146240 | tf_op jit(solution)/shard_map/while/body/eval_jaxpr/while/body/scatter-add | solution.py:63
  215.7 3.0 convolution_add_fusion.10
  220.0 3.3 gather_fusion.2
  227.7 2.5 convolution_bitcast_fusion.11
  230.1 6.9 %scatter_fusion.1 = f32[512,2048]{1,0:T(8,128)} fusion(f32[512,2048]{1,0:T(8,128)} %get-tuple-element.835, s32[128]{0:T(128)} %copy-done.9, f32[128,2048]{1,0:T(8,128)} %convolution_bitcast_fusion.11), kind=kCustom, calls=%fused_computation.4.clone.1 | custom fusion | flops 262144 | bytes 3146240 | tf_op jit(solution)/shard_map/while/body/eval_jaxpr/while/body/scatter-add | solution.py:63
  237.0 3.0 convolution_add_fusion.10
  241.3 3.3 gather_fusion.2
  249.0 2.5 convolution_bitcast_fusion.11
  251.5 6.9 %scatter_fusion.1 = f32[512,2048]{1,0:T(8,128)} fusion(f32[512,2048]{1,0:T(8,128)} %get-tuple-element.835, s32[128]{0:T(128)} %copy-done.9, f32[128,2048]{1,0:T(8,128)} %convolution_bitcast_fusion.11), kind=kCustom, calls=%fused_computation.4.clone.1 | custom fusion | flops 262144 | bytes 3146240 | tf_op jit(solution)/shard_map/while/body/eval_jaxpr/while/body/scatter-add | solution.py:63
  258.4 3.0 convolution_add_fusion.10
  262.7 3.3 gather_fusion.2
  270.4 2.5 convolution_bitcast_fusion.11
  272.9 6.9 %scatter_fusion.1 = f32[512,2048]{1,0:T(8,128)} fusion(f32[512,2048]{1,0:T(8,128)} %get-tuple-element.835, s32[128]{0:T(128)} %copy-done.9, f32[128,2048]{1,0:T(8,128)} %convolution_bitcast_fusion.11), kind=kCustom, calls=%fused_computation.4.clone.1 | custom fusion | flops 262144 | bytes 3146240 | tf_op jit(solution)/shard_map/while/body/eval_jaxpr/while/body/scatter-add | solution.py:63
  279.8 3.0 convolution_add_fusion.10
  284.0 2.6 bitcast_dynamic-update-slice_fusion.8
  294.0 4.3 scatter_custom_fusion.23
  298.3 4.5 scatter_custom_fusion.24
  305.1 42.7 %while.91 = (s32[]{:T(128)}, f32[512,2048]{1,0:T(8,128)}, f32[2,96,2048]{2,1,0:T(8,128)}, f32[96,2048]{1,0:T(8,128)}, s32[]{:T(128)}, /*index=5*/s32[1024]{0:T(1...) while((s32[]{:T(128)}, f32[512,2048]{1,0:T(8,128)}, ...), condition=%wide.region_8.8_spmd, body=%wide.region_6.7_spmd.sunk | while | flops 403813760 | bytes 21888456 | solution.py:67
  305.2 3.3 gather_fusion.2
  312.9 2.5 convolution_bitcast_fusion.11
  315.4 6.9 %scatter_fusion.1 = f32[512,2048]{1,0:T(8,128)} fusion(f32[512,2048]{1,0:T(8,128)} %get-tuple-element.835, s32[128]{0:T(128)} %copy-done.9, f32[128,2048]{1,0:T(8,128)} %convolution_bitcast_fusion.11), kind=kCustom, calls=%fused_computation.4.clone.1 | custom fusion | flops 262144 | bytes 3146240 | tf_op jit(solution)/shard_map/while/body/eval_jaxpr/while/body/scatter-add | solution.py:63
  322.3 3.0 convolution_add_fusion.10
  326.6 3.3 gather_fusion.2
  334.3 2.5 convolution_bitcast_fusion.11
  336.8 6.9 %scatter_fusion.1 = f32[512,2048]{1,0:T(8,128)} fusion(f32[512,2048]{1,0:T(8,128)} %get-tuple-element.835, s32[128]{0:T(128)} %copy-done.9, f32[128,2048]{1,0:T(8,128)} %convolution_bitcast_fusion.11), kind=kCustom, calls=%fused_computation.4.clone.1 | custom fusion | flops 262144 | bytes 3146240 | tf_op jit(solution)/shard_map/while/body/eval_jaxpr/while/body/scatter-add | solution.py:63
  343.7 3.0 convolution_add_fusion.10
  347.9 2.6 bitcast_dynamic-update-slice_fusion.8
  353.9 44.2 %while.88 = (s32[]{:T(128)}, f32[512,2048]{1,0:T(8,128)}, f32[2,96,2048]{2,1,0:T(8,128)}, f32[96,2048]{1,0:T(8,128)}, s32[]{:T(128)}, /*index=5*/s32[1024]{0:T(1...) while((s32[]{:T(128)}, f32[512,2048]{1,0:T(8,128)}, ...), condition=%wide.region_17.18_spmd, body=%wide.region_15.17_spmd.sunk | while | flops 403813760 | bytes 21816580 | solution.py:67
  354.7 3.3 gather_fusion
  364.9 6.9 %scatter_fusion = f32[512,2048]{1,0:T(8,128)} fusion(f32[512,2048]{1,0:T(8,128)} %get-tuple-element.952, s32[128]{0:T(128)S(1)} %compare_select_fusion.8, f32[128,2048]{1,0:T(8,128)} %convolution_bitcast_fusion.9), kind=kCustom, calls=%fused_computation.7.clone.1 | custom fusion | flops 262144 | bytes 3146240 | tf_op jit(solution)/shard_map/while/body/scatter-add | solution.py:63
  371.8 3.0 convolution_add_fusion.8
  376.8 3.3 gather_fusion
  384.6 2.4 convolution_bitcast_fusion.9
  387.0 6.9 %scatter_fusion = f32[512,2048]{1,0:T(8,128)} fusion(f32[512,2048]{1,0:T(8,128)} %get-tuple-element.952, s32[128]{0:T(128)S(1)} %compare_select_fusion.8, f32[128,2048]{1,0:T(8,128)} %convolution_bitcast_fusion.9), kind=kCustom, calls=%fused_computation.7.clone.1 | custom fusion | flops 262144 | bytes 3146240 | tf_op jit(solution)/shard_map/while/body/scatter-add | solution.py:63
  393.9 3.0 convolution_add_fusion.8
  401.3 3.9 convert_element_type.92
  405.2 88.1 %reduce-scatter.8.cloned.1.call-done = bf16[1,96,2048]{2,1,0:T(8,128)(2,1)} async-done(((bf16[4,96,2048]{2,1,0:T(8,128)(2,1)}), bf16[1,96,2048]{2,1,0:T(8,128)(2,1)}) %reduce-scatter.8.cloned.1.call-update) | async-done | bytes 393232 | tf_op jit(solution)/shard_map/reduce_scatter | solution.py:105
  495.3 38.6 %reduce-scatter.6.cloned.1.call-done = bf16[1,2,96,2048]{3,2,1,0:T(8,128)(2,1)} async-done(((bf16[4,2,96,2048]{3,2,1,0:T(8,128)(2,1)}), bf16[1,2,96,2048]{3,2,1,0:T(8,128)(2,1)}) %reduce-scatter.6.cloned.1.call-update) | async-done | bytes 786448 | tf_op jit(solution)/shard_map/reduce_scatter | solution.py:102
  533.9 2.5 convert_element_type.94
  536.4 44.1 %reduce-scatter.4.cloned.1.call-done = bf16[128,2048]{1,0:T(8,128)(2,1)} async-done(((bf16[512,2048]{1,0:T(8,128)(2,1)}), bf16[128,2048]{1,0:T(8,128)(2,1)}) %reduce-scatter.4.cloned.1.call-update) | async-done | bytes 524304 | tf_op jit(solution)/shard_map/reduce_scatter | solution.py:109
  (346 shorter events, 110.3 us)
Async XLA Ops:
  7.2 4.8 copy-start.17
  7.2 22.9 %copy-start.18 = (bf16[128,2]{0,1:T(2,128)(2,1)S(1)}, bf16[128,2]{0,1:T(2,128)(2,1)}, u32[]{:S(2)}) copy-start(bf16[128,2]{0,1:T(2,128)(2,1)} %param.14) | copy-start | bytes 1540
  7.2 55.7 %all-gather.3.cloned.1.call-start = ((), (), s32[]{:S(2)}) async-start(), calls=%async_computation.3 | async-start | bytes 2621440 | tf_op jit(solution)/shard_map/all_gather | solution.py:76
  11.1 98.1 %all-gather.5.cloned.1.call-start = ((), (), s32[]{:S(2)}) async-start(), calls=%async_computation.4 | async-start | bytes 2621440 | tf_op jit(solution)/shard_map/all_gather | solution.py:75
  11.9 481.5 %reduce-scatter.8.cloned.1.call-start = ((), (), s32[]{:S(2)}) async-start(), calls=%async_computation.7 | async-start | bytes 1966080 | tf_op jit(solution)/shard_map/reduce_scatter | solution.py:105
  45.1 66.6 %copy-start.10 = (bf16[512,2]{1,0:T(8,128)(2,1)}, bf16[512,2]{1,0:T(8,128)(2,1)S(1)}, u32[]{:S(2)}) copy-start(bf16[512,2]{1,0:T(8,128)(2,1)S(1)} %all_gather.13) | copy-start | bytes 6148
  111.7 3.4 copy-start
  117.2 62.2 %collective-permute-start = (bf16[1,2,96,2048]{3,2,1,0:T(8,128)(2,1)}, bf16[1,2,96,2048]{3,2,1,0:T(8,128)(2,1)}, u32[]{:S(2)}, u32[]{:S(2)}) collective-permute-start(bf16[1,2,96,2048]{3,2,1,0:T(8,128)(2,1)} %copy.38), channel_id=1, source_target_pairs={{12,0},{0,4},{4,8},{8,12},{13,1},{1,5},{5,9},{9,13},{14,2},{2,6},{... | collective-permute-start | bytes 2359304 | tf_op jit(solution)/shard_map/while/body/eval_jaxpr/ppermute | solution.py:10
  118.9 60.4 %collective-permute-start.1 = (bf16[1,96,2048]{2,1,0:T(8,128)(2,1)}, bf16[1,96,2048]{2,1,0:T(8,128)(2,1)}, u32[]{:S(2)}, u32[]{:S(2)}) collective-permute-start(bf16[1,96,2048]{2,1,0:T(8,128)(2,1)} %copy.39), channel_id=1, source_target_pairs={{12,0},{0,4},{4,8},{8,12},{13,1},{1,5},{5,9},{9,13},{14,2},{2,6},{... | collective-permute-start | bytes 1179656 | tf_op jit(solution)/shard_map/while/body/eval_jaxpr/ppermute | solution.py:10
  134.0 3.4 copy-start.13
  134.0 5.9 copy-start.15
  134.1 3.3 copy-start.9
  151.2 3.0 copy-start.1
  151.2 3.0 copy-start.12
  155.4 3.4 copy-start.13
  155.4 5.9 %copy-start.15 = (f32[1024]{0:T(1024)}, f32[1024]{0:T(1024)S(1)}, u32[]{:S(2)}) copy-start(f32[1024]{0:T(1024)S(1)} %get-tuple-element.855) | copy-start | bytes 12292 | tf_op jit(solution)/shard_map/while/body/eval_jaxpr/while
  155.5 3.3 copy-start.9
  172.5 3.0 copy-start.1
  172.5 3.0 copy-start.12
  176.7 2.6 copy-start.3
  176.7 2.6 copy-start.7
  182.6 104.1 %collective-permute-start = (bf16[1,2,96,2048]{3,2,1,0:T(8,128)(2,1)}, bf16[1,2,96,2048]{3,2,1,0:T(8,128)(2,1)}, u32[]{:S(2)}, u32[]{:S(2)}) collective-permute-start(bf16[1,2,96,2048]{3,2,1,0:T(8,128)(2,1)} %copy.38), channel_id=1, source_target_pairs={{12,0},{0,4},{4,8},{8,12},{13,1},{1,5},{5,9},{9,13},{14,2},{2,6},{... | collective-permute-start | bytes 2359304 | tf_op jit(solution)/shard_map/while/body/eval_jaxpr/ppermute | solution.py:10
  184.3 102.3 %collective-permute-start.1 = (bf16[1,96,2048]{2,1,0:T(8,128)(2,1)}, bf16[1,96,2048]{2,1,0:T(8,128)(2,1)}, u32[]{:S(2)}, u32[]{:S(2)}) collective-permute-start(bf16[1,96,2048]{2,1,0:T(8,128)(2,1)} %copy.39), channel_id=1, source_target_pairs={{12,0},{0,4},{4,8},{8,12},{13,1},{1,5},{5,9},{9,13},{14,2},{2,6},{... | collective-permute-start | bytes 1179656 | tf_op jit(solution)/shard_map/while/body/eval_jaxpr/ppermute | solution.py:10
  198.5 3.4 copy-start.13
  198.5 5.9 copy-start.15
  198.6 3.3 copy-start.9
  215.7 3.0 copy-start.1
  215.7 3.0 copy-start.12
  219.9 3.4 copy-start.13
  219.9 5.9 %copy-start.15 = (f32[1024]{0:T(1024)}, f32[1024]{0:T(1024)S(1)}, u32[]{:S(2)}) copy-start(f32[1024]{0:T(1024)S(1)} %get-tuple-element.855) | copy-start | bytes 12292 | tf_op jit(solution)/shard_map/while/body/eval_jaxpr/while
  220.0 3.3 copy-start.9
  237.0 3.0 copy-start.1
  237.0 3.0 copy-start.12
  241.2 3.4 copy-start.13
  241.2 5.9 %copy-start.15 = (f32[1024]{0:T(1024)}, f32[1024]{0:T(1024)S(1)}, u32[]{:S(2)}) copy-start(f32[1024]{0:T(1024)S(1)} %get-tuple-element.855) | copy-start | bytes 12292 | tf_op jit(solution)/shard_map/while/body/eval_jaxpr/while
  241.3 3.3 copy-start.9
  258.4 3.0 copy-start.1
  258.4 3.0 copy-start.12
  262.6 3.4 copy-start.13
  262.6 5.9 %copy-start.15 = (f32[1024]{0:T(1024)}, f32[1024]{0:T(1024)S(1)}, u32[]{:S(2)}) copy-start(f32[1024]{0:T(1024)S(1)} %get-tuple-element.855) | copy-start | bytes 12292 | tf_op jit(solution)/shard_map/while/body/eval_jaxpr/while
  262.7 3.3 copy-start.9
  279.8 3.0 copy-start.1
  279.8 3.0 copy-start.12
  284.0 2.6 copy-start.3
  284.0 2.6 copy-start.7
  289.8 60.7 %collective-permute-start = (bf16[1,2,96,2048]{3,2,1,0:T(8,128)(2,1)}, bf16[1,2,96,2048]{3,2,1,0:T(8,128)(2,1)}, u32[]{:S(2)}, u32[]{:S(2)}) collective-permute-start(bf16[1,2,96,2048]{3,2,1,0:T(8,128)(2,1)} %copy.38), channel_id=1, source_target_pairs={{12,0},{0,4},{4,8},{8,12},{13,1},{1,5},{5,9},{9,13},{14,2},{2,6},{... | collective-permute-start | bytes 2359304 | tf_op jit(solution)/shard_map/while/body/eval_jaxpr/ppermute | solution.py:10
  291.6 58.9 %collective-permute-start.1 = (bf16[1,96,2048]{2,1,0:T(8,128)(2,1)}, bf16[1,96,2048]{2,1,0:T(8,128)(2,1)}, u32[]{:S(2)}, u32[]{:S(2)}) collective-permute-start(bf16[1,96,2048]{2,1,0:T(8,128)(2,1)} %copy.39), channel_id=1, source_target_pairs={{12,0},{0,4},{4,8},{8,12},{13,1},{1,5},{5,9},{9,13},{14,2},{2,6},{... | collective-permute-start | bytes 1179656 | tf_op jit(solution)/shard_map/while/body/eval_jaxpr/ppermute | solution.py:10
  305.1 3.4 copy-start.13
  305.1 5.9 copy-start.15
  305.2 3.3 copy-start.9
  322.3 3.0 copy-start.1
  322.3 3.0 copy-start.12
  326.5 3.4 copy-start.13
  326.5 5.9 %copy-start.15 = (f32[1024]{0:T(1024)}, f32[1024]{0:T(1024)S(1)}, u32[]{:S(2)}) copy-start(f32[1024]{0:T(1024)S(1)} %get-tuple-element.855) | copy-start | bytes 12292 | tf_op jit(solution)/shard_map/while/body/eval_jaxpr/while
  326.6 3.3 copy-start.9
  343.7 3.0 copy-start.1
  343.7 3.0 copy-start.12
  347.9 2.6 copy-start.3
  347.9 2.6 copy-start.7
  371.8 3.0 copy-start.5
  393.9 3.0 copy-start.5
  398.1 2.1 copy-start.4
  400.2 133.7 %reduce-scatter.6.cloned.1.call-start = ((), (), s32[]{:S(2)}) async-start(), calls=%async_computation.6 | async-start | bytes 3932160 | tf_op jit(solution)/shard_map/reduce_scatter | solution.py:102
  401.3 179.2 %reduce-scatter.4.cloned.1.call-start = ((), (), s32[]{:S(2)}) async-start(), calls=%async_computation.5 | async-start | bytes 2621440 | tf_op jit(solution)/shard_map/reduce_scatter | solution.py:109
  (37 other events, 35.5 us)
Sparse Core Ops, SparseCore 0:
  11.3 51.6 all-gather.2
  64.5 44.6 all-gather.4
  400.3 93.0 reduce-scatter.7
  495.9 37.9 reduce-scatter.5
  536.6 43.8 reduce-scatter.3
where the time goes:
time: 580 us; the launch traced here: 587 us
  waiting for transfers between devices  224 us (39%)
  local copies, waits for them, and re-layouts  142 us (24%)
  matrix products  85.5 us (15%)
  other arithmetic  83.9 us (14%)
  blocking collectives  31.3 us (5%)
  between operations  14.6 us (3%)
    reduce_scatter x1, waiting for transfers between devices, body(): lax.psum_scatter(all_down.astype(jnp.bfloat16), 'expert', scatter_dimensi...  88.1 us
    scatter-add x10, other arithmetic, one_block(): accum = accum.at[slot_rows].add(contrib)  68.9 us
    all_gather x1, waiting for transfers between devices, body(): lax.all_gather(tokens, 'dp', axis=0, tiled=True)  46.3 us
    reduce_scatter x1, waiting for transfers between devices, body(): lax.psum_scatter(accum.astype(jnp.bfloat16), 'dp', scatter_dimension=0, t...  44.1 us
    reduce_scatter x1, waiting for transfers between devices, body(): lax.psum_scatter(all_gate_up.astype(jnp.bfloat16), 'expert', scatter_dime...  38.6 us
    gather x10, local copies, waits for them, and re-layouts, one_block(): block_x = rows_x[slot_rows]  33 us
    dot_general x10, matrix products, one_block(): jnp.einsum('crh,rd->chd', both, block_x, preferred_element_type=jnp.float32)  30.2 us
    dot_general x10, matrix products, one_block(): jnp.einsum('crh,chd->rd', both, gate_up, preferred_element_type=jnp.float32)  24.6 us
  transfers between devices with their start and end apart: 11, of which 5 were waited for; matrix products, arithmetic and copies ran while one was open for 40% of the time, Pallas kernels for 0%

commit v1 on v0

v1 whole, which is shorter than its diff:
```python
import jax
import jax.numpy as jnp
from jax import lax
from jax.sharding import PartitionSpec as P


def ring_pairs(count):
    order = [0] + list(range(1, count, 2)) + list(range(2, count, 2))[::-1]
    return [(order[i], order[(i + 1) % count]) for i in range(count)]


def onward(block):
    return lax.ppermute(block, "dp", ring_pairs(lax.axis_size("dp")))


def swapped(block, bit):
    return lax.ppermute(block, "expert", [(i, i ^ bit) for i in range(lax.axis_size("expert"))])


def bits_of(count):
    return [1 << i for i in range(count.bit_length() - 1)]


def all_experts(block):
    held = {0: block}
    for bit in bits_of(lax.axis_size("expert"))[::-1]:
        held.update({k | bit: swapped(v, bit) for k, v in list(held.items())})
    return [held[k] for k in range(len(held))]


def summed_to_owner(terms):
    left = {k: v for k, v in enumerate(terms)}
    for bit in bits_of(len(terms)):
        stay = [k for k in left if not k & bit]
        got = {k: swapped(left[k | bit], bit) for k in stay[::-1]}
        left = {k: left[k].astype(jnp.float32) + got[k].astype(jnp.float32) for k in stay}
        if len(left) > 1:
            left = {k: v.astype(jnp.bfloat16) for k, v in left.items()}
    return left[0]


def f32_dot(spec, a, b):
    return jnp.einsum(spec, a, b, preferred_element_type=jnp.float32)


def hidden_terms(x, dy, prob, gate, up, down):
    gate_act = f32_dot("rd,hd->rh", x, gate)
    up_act = f32_dot("rd,hd->rh", x, up)
    back = f32_dot("rd,hd->rh", dy, down)
    hid = gate.shape[0] // prob.shape[0]
    weight = jnp.repeat(prob.T.astype(jnp.float32), hid, axis=1)
    sigma = jax.nn.sigmoid(gate_act)
    silu_gate = gate_act * sigma
    weighted = (weight * silu_gate * up_act).astype(jnp.bfloat16)
    back = weight * back
    gate_grad = (back * up_act * sigma * (1.0 + gate_act * (1.0 - sigma))).astype(jnp.bfloat16)
    up_grad = (back * silu_gate).astype(jnp.bfloat16)
    contrib = f32_dot("rh,hd->rd", gate_grad, gate) + f32_dot("rh,hd->rd", up_grad, up)
    return weighted, gate_grad, up_grad, contrib.astype(jnp.bfloat16)


def body(tokens, route_ids, route_probs, cotangent, w_gate_up, w_down):
    turns = lax.axis_size("dp")
    experts = lax.axis_size("expert")
    here = lax.axis_index("expert")
    hid, width = w_down.shape[1:]
    names = jnp.arange(experts, dtype=jnp.int32) ^ here
    prob = jnp.sum(
        jnp.where(route_ids[None] == names[:, None, None], route_probs[None], 0), axis=2
    ).astype(jnp.bfloat16)

    slabs = [(tokens, cotangent, prob)]
    for _ in range(turns - 1):
        slabs.append(tuple(onward(v) for v in slabs[-1]))
    block = jnp.concatenate([w_gate_up.reshape(2 * hid, width), w_down.reshape(hid, width)])
    blocks = all_experts(block)
    gate = jnp.concatenate([b[:hid] for b in blocks])
    up = jnp.concatenate([b[hid : 2 * hid] for b in blocks])
    down = jnp.concatenate([b[2 * hid :] for b in blocks])

    parts = [hidden_terms(x, dy, pr, gate, up, down) for x, dy, pr in slabs]
    acc = parts[1][3]
    for i in range(2, turns + 1):
        acc = onward(acc)
        acc = (acc.astype(jnp.float32) + parts[i % turns][3].astype(jnp.float32)).astype(jnp.bfloat16)

    all_x = jnp.concatenate([s[0] for s in slabs])
    all_dy = jnp.concatenate([s[1] for s in slabs])
    weighted, gate_grad, up_grad = (jnp.concatenate([p[i] for p in parts]) for i in range(3))
    grad_down = f32_dot("rh,rd->hd", weighted, all_dy).astype(jnp.bfloat16)
    grad_gate = f32_dot("rh,rd->hd", gate_grad, all_x).astype(jnp.bfloat16)
    grad_up = f32_dot("rh,rd->hd", up_grad, all_x).astype(jnp.bfloat16)
    terms = []
    for k in range(experts):
        at = slice(k * hid, (k + 1) * hid)
        terms.append(jnp.concatenate([grad_gate[at], grad_up[at], grad_down[at]]))
    total = summed_to_owner(terms)
    return (
        acc,
        total[: 2 * hid].reshape(1, 2, hid, width),
        total[2 * hid :].reshape(1, hid, width),
    )


def solution(mesh):
    placed = (
        P(("groups", "expert", "dp"), None),
        P(("groups", "expert", "dp"), None),
        P(("groups", "expert", "dp"), None),
        P(("groups", "expert", "dp"), None),
        P("expert", None, "dp", None),
        P("expert", "dp", None),
    )
    return jax.shard_map(
        body,
        mesh=mesh,
        in_specs=placed,
        out_specs=(
            P(("groups", "expert", "dp"), None),
            P(("groups", "expert"), None, "dp", None),
            P(("groups", "expert"), "dp", None),
        ),
        check_vma=False,
    )
```

time: 580 us -> 155 us (0.27); the launches traced: 587 us -> 154 us
  local copies, waits for them, and re-layouts: 142 us -> 11.5 us
  waiting for transfers between devices: 224 us -> 99.9 us
  other arithmetic: 83.9 us -> 4 us
  matrix products: 85.5 us -> 23.6 us
  blocking collectives: 31.3 us -> 0 us
  between operations: 14.6 us -> 1.12 us
  starting transfers between devices: 2.47 us -> 13.8 us
    reduce_scatter x3 -> x0, waiting for transfers between devices: 171 us -> none  [the longest x1 88.1 us: body(): lax.psum_scatter(all_down.astype(jnp.bfloat16), 'expert', scatter_dimensi...]
    ppermute x6 -> x18, waiting for transfers between devices: 0.02 us -> 99.9 us  [the longest x12 99.9 us: onward(): return lax.ppermute(block, 'dp', ring_pairs(lax.axis_size('dp')))]
    scatter-add x10 -> x0, other arithmetic: 68.9 us -> none  [one_block(): accum = accum.at[slot_rows].add(contrib)]
    dot_general x50 -> x23, matrix products: 85.5 us -> 23.6 us  [f32_dot(): return jnp.einsum(spec, a, b, preferred_element_type=jnp.float32)]
    all_gather x2 -> x0, waiting for transfers between devices: 52.7 us -> none  [the longest x1 46.3 us: body(): lax.all_gather(tokens, 'dp', axis=0, tiled=True)]
    gather x20 -> x0, local copies, waits for them, and re-layouts: 42.4 us -> none  [the longest x10 33 us: one_block(): block_x = rows_x[slot_rows]]
    scatter x8 -> x0, local copies, waits for them, and re-layouts: 36.1 us -> none  [the longest x4 18.3 us: expert_pass(): table_weight = jnp.zeros((table,), jnp.float32).at[target].set(rows_probs...]
    all_gather x2 -> x0, blocking collectives: 31.3 us -> none  [the longest x1 16.4 us: body(): rows_ids = lax.all_gather(route_ids, 'dp', axis=0, tiled=True)]
  transfers between devices with their start and end apart: 11 -> 18, of which waited for: 5 -> 8; matrix products, arithmetic and copies ran while one was open for 40% -> 16% of each run, Pallas kernels for 0% -> 0%
where the time goes in v1:
time: 155 us; the launch traced here: 154 us
  waiting for transfers between devices  99.9 us (64%)
  matrix products  23.6 us (15%)
  starting transfers between devices  13.8 us (9%)
  local copies, waits for them, and re-layouts  11.5 us (7%)
  other arithmetic  4 us (3%)
    ppermute x12, waiting for transfers between devices, onward(): return lax.ppermute(block, 'dp', ring_pairs(lax.axis_size('dp')))  99.9 us
    dot_general x23, matrix products, f32_dot(): return jnp.einsum(spec, a, b, preferred_element_type=jnp.float32)  23.6 us
    ppermute x12, starting transfers between devices, onward(): return lax.ppermute(block, 'dp', ring_pairs(lax.axis_size('dp')))  9.85 us
    ppermute x6, starting transfers between devices, swapped(): lax.ppermute(block, 'expert', [(i, i ^ bit) for i in range(lax.axis_size(...  3.96 us
    slice x4, local copies, waits for them, and re-layouts, body(): up = jnp.concatenate([b[hid:2 * hid] for b in blocks])  3.55 us
  transfers between devices with their start and end apart: 18, of which 8 were waited for; matrix products, arithmetic and copies ran while one was open for 16% of the time, Pallas kernels for 0%

profile of v1, /device:TPU:0, one launch (start us, length us, event | category | flops | bytes accessed | tf_op | source)
XLA Modules:
  0.0 153.9 jit_solution(8982013521971083826)
XLA Ops:
  0.7 2.5 %pad_maximum_fusion.3 = bf16[288,2048]{1,0:T(8,128)(2,1)} fusion(bf16[96,2048]{1,0:T(8,128)(2,1)} %bitcast.89, bf16[192,2048]{1,0:T(8,128)(2,1)} %bitcast.83), kind=kLoop, calls=%fused_computation.33 | loop fusion | flops 2359296 | bytes 2359296 | tf_op jit(solution)/shard_map/concatenate | solution.py:75
  3.2 3.0 %collective-permute-start.2 = (bf16[288,2048]{1,0:T(8,128)(2,1)}, bf16[288,2048]{1,0:T(8,128)(2,1)}, u32[]{:S(2)}, u32[]{:S(2)}) collective-permute-start(bf16[288,2048]{1,0:T(8,128)(2,1)} %pad_maximum_fusion.3), channel_id=1, source_target_pairs={{0,8},{4,12},{8,0},{12,4},{1,9},{5,13},{9,1},{13,5},{2,10},{6,14},... | collective-permute-start | bytes 3538952 | tf_op jit(solution)/shard_map/ppermute | solution.py:17
  6.1 0.1 fusion.49
  6.2 1.6 %collective-permute-start = (bf16[4,128]{1,0:T(4,128)(2,1)S(1)}, bf16[4,128]{1,0:T(4,128)(2,1)S(1)}, u32[]{:S(2)}, u32[]{:S(2)}) collective-permute-start(bf16[4,128]{1,0:T(4,128)(2,1)S(1)} %fusion.49), channel_id=1, source_target_pairs={{0,1},{1,3},{3,2},{2,0},{4,5},{5,7},{7,6},{6,4},{8,9},{9,11},{11,1... | collective-permute-start | bytes 3080 | tf_op jit(solution)/shard_map/ppermute | solution.py:13
  7.8 2.6 %collective-permute-start.4 = (bf16[128,2048]{1,0:T(8,128)(2,1)}, bf16[128,2048]{1,0:T(8,128)(2,1)}, u32[]{:S(2)}, u32[]{:S(2)}) collective-permute-start(bf16[128,2048]{1,0:T(8,128)(2,1)} %param.9), channel_id=1, source_target_pairs={{0,1},{1,3},{3,2},{2,0},{4,5},{5,7},{7,6},{6,4},{8,9},{9,11},{11,1... | collective-permute-start | bytes 1572872 | tf_op jit(solution)/shard_map/ppermute | solution.py:13
  10.4 0.4 collective-permute-start.5
  10.9 0.8 slice_bitcast_fusion.2
  11.7 0.8 copy.24
  12.6 0.3 collective-permute-start.7
  12.9 0.1 copy.21
  13.1 21.3 %collective-permute-done.7 = bf16[4,128]{1,0:T(4,128)(2,1)S(1)} collective-permute-done((bf16[4,128]{1,0:T(4,128)(2,1)S(1)}, bf16[4,128]{1,0:T(4,128)(2,1)S(1)}, u32[]{:S(2)}, u32[]{:S(2)}) %collective-permute-start.7) | collective-permute-done | bytes 1056 | tf_op jit(solution)/shard_map/ppermute | solution.py:13
  34.3 1.7 %collective-permute-start.11 = (bf16[4,128]{1,0:T(4,128)(2,1)S(1)}, bf16[4,128]{1,0:T(4,128)(2,1)S(1)}, u32[]{:S(2)}, u32[]{:S(2)}) collective-permute-start(bf16[4,128]{1,0:T(4,128)(2,1)S(1)} %collective-permute-done.7), channel_id=1, source_target_pairs={{0,1},{1,3},{3,2},{2,0},{4,5},{5,7},{7,6},{6,4},{8,9},{9,11},{11,1... | collective-permute-start | bytes 3080 | tf_op jit(solution)/shard_map/ppermute | solution.py:13
  36.0 1.4 collective-permute-start.8
  37.5 0.8 copy.22
  38.3 0.5 collective-permute-done.11
  38.8 0.8 copy.23
  39.6 1.1 constant_dynamic-update-slice_fusion.2
  40.7 11.4 %collective-permute-done.8 = bf16[128,2048]{1,0:T(8,128)(2,1)} collective-permute-done((bf16[128,2048]{1,0:T(8,128)(2,1)}, bf16[128,2048]{1,0:T(8,128)(2,1)}, u32[]{:S(2)}, u32[]{:S(2)}) %collective-permute-start.8) | collective-permute-done | bytes 524320 | tf_op jit(solution)/shard_map/ppermute | solution.py:13
  52.1 0.5 collective-permute-start.12
  52.5 10.8 %collective-permute-done.9 = bf16[128,2048]{1,0:T(8,128)(2,1)} collective-permute-done((bf16[128,2048]{1,0:T(8,128)(2,1)}, bf16[128,2048]{1,0:T(8,128)(2,1)}, u32[]{:S(2)}, u32[]{:S(2)}) %collective-permute-start.9) | collective-permute-done | bytes 524320 | tf_op jit(solution)/shard_map/ppermute | solution.py:13
  63.3 0.5 collective-permute-start.13
  63.8 1.1 constant_dynamic-update-slice_fusion.1
  65.0 1.3 fusion.57
  66.3 1.3 fusion.56
  67.6 16.1 %collective-permute-done.13 = bf16[128,2048]{1,0:T(8,128)(2,1)S(1)} collective-permute-done((bf16[128,2048]{1,0:T(8,128)(2,1)}, bf16[128,2048]{1,0:T(8,128)(2,1)S(1)}, u32[]{:S(2)}, u32[]{:S(2)}) %collective-permute-start.13) | collective-permute-done | bytes 524320 | tf_op jit(solution)/shard_map/ppermute | solution.py:13
  83.8 0.1 fusion.58
  84.0 1.7 %fusion.20 = f32[128,384]{1,0:T(8,128)S(1)} fusion(f32[128,384]{1,0:T(8,128)S(1)} %copy-done.4, bf16[128,2048]{1,0:T(8,128)(2,1)} %param.9, bf16[96,2048]{1,0:T(8,128)(2,1)S(1)} %get-tuple-element.23, bf16[96,2048]{1,0:T(8,128)(2,1)S(1)} %get-tuple-element.20, bf16[96,2048]{1,0:T(8,128)(2,1)S(1)} %get-tuple-element.17, bf16[96,2048]{1,0:T(8,128)(2,1)S(1)} %bitcast.90), kind=kOutput, calls=%fused_computation.39 | convolution fusion | flops 207667200 | bytes 2490368 | tf_op jit(solution)/shard_map/rd,hd->rh/dot_general | solution.py:43
  85.7 0.6 convolution_bitcast_fusion
  86.3 1.7 %convolution_bitcast_fusion.6 = f32[128,384]{1,0:T(8,128)S(1)} fusion(bf16[128,2048]{1,0:T(8,128)(2,1)} %collective-permute-done.9, bf16[96,2048]{1,0:T(8,128)(2,1)S(1)} %get-tuple-element.22, bf16[96,2048]{1,0:T(8,128)(2,1)S(1)} %get-tuple-element.19, bf16[96,2048]{1,0:T(8,128)(2,1)S(1)} %get-tuple-element.16, bf16[96,2048]{1,0:T(8,128)(2,1)S(1)} %copy-done.3), kind=kOutput, calls=%fused_computation.44 | convolution fusion | flops 207618048 | bytes 2293760 | tf_op jit(solution)/shard_map/rd,hd->rh/dot_general | solution.py:43
  88.0 0.6 convolution_bitcast_fusion.3
  88.6 1.7 %convolution_bitcast_fusion.9 = f32[128,384]{1,0:T(8,128)S(1)} fusion(bf16[128,2048]{1,0:T(8,128)(2,1)} %collective-permute-done.5, bf16[96,2048]{1,0:T(8,128)(2,1)S(1)} %get-tuple-element.22, bf16[96,2048]{1,0:T(8,128)(2,1)S(1)} %get-tuple-element.19, bf16[96,2048]{1,0:T(8,128)(2,1)S(1)} %get-tuple-element.16, bf16[96,2048]{1,0:T(8,128)(2,1)S(1)} %copy-done.3), kind=kOutput, calls=%fused_computation.48 | convolution fusion | flops 207618048 | bytes 2293760 | tf_op jit(solution)/shard_map/rd,hd->rh/dot_general | solution.py:43
  90.3 1.7 %fusion.22 = f32[128,384]{1,0:T(8,128)S(1)} fusion(f32[128,384]{1,0:T(8,128)S(1)} %copy-done.5, bf16[128,2048]{1,0:T(8,128)(2,1)} %collective-permute-done.8, bf16[96,2048]{1,0:T(8,128)(2,1)S(1)} %get-tuple-element.23, bf16[96,2048]{1,0:T(8,128)(2,1)S(1)} %get-tuple-element.20, bf16[96,2048]{1,0:T(8,128)(2,1)S(1)} %get-tuple-element.17, ...), kind=kOutput, calls=%fused_computation.47 | convolution fusion | flops 207667200 | bytes 2490368 | tf_op jit(solution)/shard_map/rd,hd->rh/dot_general | solution.py:43
  91.9 1.7 %fusion.23 = f32[128,384]{1,0:T(8,128)S(1)} fusion(f32[128,384]{1,0:T(8,128)S(1)} %copy.21, bf16[128,2048]{1,0:T(8,128)(2,1)} %collective-permute-done.4, bf16[96,2048]{1,0:T(8,128)(2,1)S(1)} %get-tuple-element.23, bf16[96,2048]{1,0:T(8,128)(2,1)S(1)} %get-tuple-element.20, bf16[96,2048]{1,0:T(8,128)(2,1)S(1)} %get-tuple-element.17, ...), kind=kOutput, calls=%fused_computation.51 | convolution fusion | flops 207667200 | bytes 2490368 | tf_op jit(solution)/shard_map/rd,hd->rh/dot_general | solution.py:43
  93.6 0.2 pad_maximum_fusion.1
  93.8 0.6 multiply_convert_fusion.3
  94.4 0.3 copy-done.6
  94.7 0.6 fusion.21
  95.3 1.7 %multiply_convert_fusion.1 = (bf16[128,384]{1,0:T(8,128)(2,1)S(1)}, bf16[128,384]{1,0:T(8,128)(2,1)S(1)}, bf16[128,384]{1,0:T(8,128)(2,1)S(1)}) fusion(f32[128,384]{1,0:T(8,128)S(1)} %copy-done.5, f32[128,384]{1,0:T(8,128)S(1)} %convolution_bitcast_fusion.6, f32[128,384]{1,0:T(8,128)S(1)} %fusion.22, bf16[384,2048]{1,0:T(8,128)(2,1)S(1)} %pad_maximum_fusion.1, ...), kind=kOutput, calls=%fused_computation.77 | convolution fusion | flops 202113024 | bytes 2981888 | tf_op jit(solution)/shard_map/rd,hd->rh/dot_general | solution.py:43
  97.0 0.6 multiply_convert_fusion
  97.6 1.7 %multiply_convert_fusion.2 = (bf16[128,384]{1,0:T(8,128)(2,1)S(1)}, bf16[128,384]{1,0:T(8,128)(2,1)S(1)}, bf16[128,384]{1,0:T(8,128)(2,1)S(1)}) fusion(f32[128,384]{1,0:T(8,128)S(1)} %copy.21, f32[128,384]{1,0:T(8,128)S(1)} %convolution_bitcast_fusion.9, f32[128,384]{1,0:T(8,128)S(1)} %fusion.23, bf16[384,2048]{1,0:T(8,128)(2,1)S(1)} %pad_maximum_fusion.1, ...), kind=kOutput, calls=%fused_computation.78 | convolution fusion | flops 202113024 | bytes 2981888 | tf_op jit(solution)/shard_map/rd,hd->rh/dot_general | solution.py:43
  99.3 2.4 %convolution_convert_fusion = bf16[384,2048]{1,0:T(8,128)(2,1)S(1)} fusion(bf16[128,2048]{1,0:T(8,128)(2,1)S(1)} %collective-permute-done.12, bf16[128,2048]{1,0:T(8,128)(2,1)} %collective-permute-done.8, bf16[128,2048]{1,0:T(8,128)(2,1)} %collective-permute-done.4, bf16[128,2048]{1,0:T(8,128)(2,1)} %param.9, bf16[128,384]{1,0:T(8,128)(2,1)S(1)} %get-tuple-element.35, ...), kind=kOutput, calls=%fused_computation | convolution fusion | flops 816054272 | bytes 4063232 | tf_op jit(solution)/shard_map/rh,rd->hd/dot_general | solution.py:43
  101.7 0.2 fusion.55
  101.9 1.0 convolution_convert_fusion.1
  102.9 1.0 convolution_convert_fusion.2
  103.9 0.4 fusion.53
  104.5 0.4 fusion.59
  104.9 0.5 fusion
  105.4 0.8 collective-permute-start.6
  106.1 0.1 pad_maximum_fusion.4
  106.3 0.3 collective-permute-start.15
  106.5 0.4 fusion.60
  107.0 13.9 %collective-permute-done.6 = bf16[128,2048]{1,0:T(8,128)(2,1)S(1)} collective-permute-done((bf16[128,2048]{1,0:T(8,128)(2,1)S(1)}, bf16[128,2048]{1,0:T(8,128)(2,1)S(1)}, u32[]{:S(2)}, u32[]{:S(2)}) %collective-permute-start.6) | collective-permute-done | bytes 524320 | tf_op jit(solution)/shard_map/ppermute | solution.py:13
  120.8 0.5 fusion.4
  121.4 0.5 add_convert_fusion
  121.9 0.6 collective-permute-start.17
  122.4 0.4 fusion.61
  122.9 12.9 %collective-permute-done.10 = bf16[128,2048]{1,0:T(8,128)(2,1)S(1)} collective-permute-done((bf16[128,2048]{1,0:T(8,128)(2,1)S(1)}, bf16[128,2048]{1,0:T(8,128)(2,1)S(1)}, u32[]{:S(2)}, u32[]{:S(2)}) %collective-permute-start.10) | collective-permute-done | bytes 524320 | tf_op jit(solution)/shard_map/ppermute | solution.py:13
  135.8 0.5 fusion.8
  136.4 0.4 fusion.62
  136.8 13.1 %collective-permute-done.14 = bf16[128,2048]{1,0:T(8,128)(2,1)S(1)} collective-permute-done((bf16[128,2048]{1,0:T(8,128)(2,1)S(1)}, bf16[128,2048]{1,0:T(8,128)(2,1)S(1)}, u32[]{:S(2)}, u32[]{:S(2)}) %collective-permute-start.14) | collective-permute-done | bytes 524320 | tf_op jit(solution)/shard_map/ppermute | solution.py:13
  149.9 1.3 fusion.12
  151.2 0.6 convert_add_fusion
  151.8 0.9 slice_bitcast_fusion
  152.7 1.2 slice.129
  (45 shorter events, 0.6 us)
Async XLA Ops:
  0.6 10.2 %copy-start = (bf16[1,2,96,2048]{3,2,1,0:T(8,128)(2,1)S(1)}, bf16[1,2,96,2048]{3,2,1,0:T(8,128)(2,1)}, u32[]{:S(2)}) copy-start(bf16[1,2,96,2048]{3,2,1,0:T(8,128)(2,1)} %param.10) | copy-start | bytes 2359300
  0.6 5.5 %copy-start.8 = (bf16[128,2]{0,1:T(2,128)(2,1)S(1)}, bf16[128,2]{0,1:T(2,128)(2,1)}, u32[]{:S(2)}) copy-start(bf16[128,2]{0,1:T(2,128)(2,1)} %param.8) | copy-start | bytes 1540
  0.7 5.5 %copy-start.7 = (s32[128,2]{0,1:T(2,128)S(1)}, s32[128,2]{0,1:T(2,128)}, u32[]{:S(2)}) copy-start(s32[128,2]{0,1:T(2,128)} %param.7) | copy-start | bytes 3076
  0.7 9.8 %copy-start.1 = (bf16[128,2048]{1,0:T(8,128)(2,1)S(1)}, bf16[128,2048]{1,0:T(8,128)(2,1)}, u32[]{:S(2)}) copy-start(bf16[128,2048]{1,0:T(8,128)(2,1)} %param.6) | copy-start | bytes 1572868
  3.2 61.7 %collective-permute-start.2 = (bf16[288,2048]{1,0:T(8,128)(2,1)}, bf16[288,2048]{1,0:T(8,128)(2,1)}, u32[]{:S(2)}, u32[]{:S(2)}) collective-permute-start(bf16[288,2048]{1,0:T(8,128)(2,1)} %pad_maximum_fusion.3), channel_id=1, source_target_pairs={{0,8},{4,12},{8,0},{12,4},{1,9},{5,13},{9,1},{13,5},{2,10},{6,14},... | collective-permute-start | bytes 3538952 | tf_op jit(solution)/shard_map/ppermute | solution.py:17
  6.1 60.2 %collective-permute-start.1 = (bf16[288,2048]{1,0:T(8,128)(2,1)}, bf16[288,2048]{1,0:T(8,128)(2,1)}, u32[]{:S(2)}, u32[]{:S(2)}) collective-permute-start(bf16[288,2048]{1,0:T(8,128)(2,1)} %pad_maximum_fusion.3), channel_id=1, source_target_pairs={{0,4},{4,0},{8,12},{12,8},{1,5},{5,1},{9,13},{13,9},{2,6},{6,2},{1... | collective-permute-start | bytes 3538952 | tf_op jit(solution)/shard_map/ppermute | solution.py:17
  6.2 6.3 %collective-permute-start = (bf16[4,128]{1,0:T(4,128)(2,1)S(1)}, bf16[4,128]{1,0:T(4,128)(2,1)S(1)}, u32[]{:S(2)}, u32[]{:S(2)}) collective-permute-start(bf16[4,128]{1,0:T(4,128)(2,1)S(1)} %fusion.49), channel_id=1, source_target_pairs={{0,1},{1,3},{3,2},{2,0},{4,5},{5,7},{7,6},{6,4},{8,9},{9,11},{11,1... | collective-permute-start | bytes 3080 | tf_op jit(solution)/shard_map/ppermute | solution.py:13
  7.8 28.2 %collective-permute-start.4 = (bf16[128,2048]{1,0:T(8,128)(2,1)}, bf16[128,2048]{1,0:T(8,128)(2,1)}, u32[]{:S(2)}, u32[]{:S(2)}) collective-permute-start(bf16[128,2048]{1,0:T(8,128)(2,1)} %param.9), channel_id=1, source_target_pairs={{0,1},{1,3},{3,2},{2,0},{4,5},{5,7},{7,6},{6,4},{8,9},{9,11},{11,1... | collective-permute-start | bytes 1572872 | tf_op jit(solution)/shard_map/ppermute | solution.py:13
  10.4 26.9 %collective-permute-start.5 = (bf16[128,2048]{1,0:T(8,128)(2,1)S(1)}, bf16[128,2048]{1,0:T(8,128)(2,1)}, u32[]{:S(2)}, u32[]{:S(2)}) collective-permute-start(bf16[128,2048]{1,0:T(8,128)(2,1)S(1)} %copy-done.1), channel_id=1, source_target_pairs={{0,1},{1,3},{3,2},{2,0},{4,5},{5,7},{7,6},{6,4},{8,9},{9,11},{11,1... | collective-permute-start | bytes 1572872 | tf_op jit(solution)/shard_map/ppermute | solution.py:13
  12.6 21.8 %collective-permute-start.7 = (bf16[4,128]{1,0:T(4,128)(2,1)S(1)}, bf16[4,128]{1,0:T(4,128)(2,1)S(1)}, u32[]{:S(2)}, u32[]{:S(2)}) collective-permute-start(bf16[4,128]{1,0:T(4,128)(2,1)S(1)} %collective-permute-done), channel_id=1, source_target_pairs={{0,1},{1,3},{3,2},{2,0},{4,5},{5,7},{7,6},{6,4},{8,9},{9,11},{11,1... | collective-permute-start | bytes 3080 | tf_op jit(solution)/shard_map/ppermute | solution.py:13
  34.3 4.5 %collective-permute-start.11 = (bf16[4,128]{1,0:T(4,128)(2,1)S(1)}, bf16[4,128]{1,0:T(4,128)(2,1)S(1)}, u32[]{:S(2)}, u32[]{:S(2)}) collective-permute-start(bf16[4,128]{1,0:T(4,128)(2,1)S(1)} %collective-permute-done.7), channel_id=1, source_target_pairs={{0,1},{1,3},{3,2},{2,0},{4,5},{5,7},{7,6},{6,4},{8,9},{9,11},{11,1... | collective-permute-start | bytes 3080 | tf_op jit(solution)/shard_map/ppermute | solution.py:13
  36.0 16.1 %collective-permute-start.8 = (bf16[128,2048]{1,0:T(8,128)(2,1)}, bf16[128,2048]{1,0:T(8,128)(2,1)}, u32[]{:S(2)}, u32[]{:S(2)}) collective-permute-start(bf16[128,2048]{1,0:T(8,128)(2,1)} %collective-permute-done.4), channel_id=1, source_target_pairs={{0,1},{1,3},{3,2},{2,0},{4,5},{5,7},{7,6},{6,4},{8,9},{9,11},{11,1... | collective-permute-start | bytes 1572872 | tf_op jit(solution)/shard_map/ppermute | solution.py:13
  37.4 25.9 %collective-permute-start.9 = (bf16[128,2048]{1,0:T(8,128)(2,1)}, bf16[128,2048]{1,0:T(8,128)(2,1)}, u32[]{:S(2)}, u32[]{:S(2)}) collective-permute-start(bf16[128,2048]{1,0:T(8,128)(2,1)} %collective-permute-done.5), channel_id=1, source_target_pairs={{0,1},{1,3},{3,2},{2,0},{4,5},{5,7},{7,6},{6,4},{8,9},{9,11},{11,1... | collective-permute-start | bytes 1572872 | tf_op jit(solution)/shard_map/ppermute | solution.py:13
  52.1 42.3 %collective-permute-start.12 = (bf16[128,2048]{1,0:T(8,128)(2,1)}, bf16[128,2048]{1,0:T(8,128)(2,1)S(1)}, u32[]{:S(2)}, u32[]{:S(2)}) collective-permute-start(bf16[128,2048]{1,0:T(8,128)(2,1)} %collective-permute-done.8), channel_id=1, source_target_pairs={{0,1},{1,3},{3,2},{2,0},{4,5},{5,7},{7,6},{6,4},{8,9},{9,11},{11,1... | collective-permute-start | bytes 1572872 | tf_op jit(solution)/shard_map/ppermute | solution.py:13
  63.3 20.4 %collective-permute-start.13 = (bf16[128,2048]{1,0:T(8,128)(2,1)}, bf16[128,2048]{1,0:T(8,128)(2,1)S(1)}, u32[]{:S(2)}, u32[]{:S(2)}) collective-permute-start(bf16[128,2048]{1,0:T(8,128)(2,1)} %collective-permute-done.9), channel_id=1, source_target_pairs={{0,1},{1,3},{3,2},{2,0},{4,5},{5,7},{7,6},{6,4},{8,9},{9,11},{11,1... | collective-permute-start | bytes 1572872 | tf_op jit(solution)/shard_map/ppermute | solution.py:13
  64.9 18.9 %collective-permute-start.3 = (bf16[288,2048]{1,0:T(8,128)(2,1)}, bf16[288,2048]{1,0:T(8,128)(2,1)S(1)}, u32[]{:S(2)}, u32[]{:S(2)}) collective-permute-start(bf16[288,2048]{1,0:T(8,128)(2,1)} %collective-permute-done.2), channel_id=1, source_target_pairs={{0,4},{4,0},{8,12},{12,8},{1,5},{5,1},{9,13},{13,9},{2,6},{6,2},{1... | collective-permute-start | bytes 3538952 | tf_op jit(solution)/shard_map/ppermute | solution.py:17
  67.6 16.3 %copy-start.2 = (bf16[1,96,2048]{2,1,0:T(8,128)(2,1)S(1)}, bf16[1,96,2048]{2,1,0:T(8,128)(2,1)}, u32[]{:S(2)}) copy-start(bf16[1,96,2048]{2,1,0:T(8,128)(2,1)} %param.11) | copy-start | bytes 1179652
  67.6 16.3 %copy-start.4 = (f32[128,384]{1,0:T(8,128)S(1)}, f32[128,384]{1,0:T(8,128)}, u32[]{:S(2)}) copy-start(f32[128,384]{1,0:T(8,128)} %copy.24) | copy-start | bytes 589828
  83.9 1.7 %copy-start.3 = (bf16[96,2048]{1,0:T(8,128)(2,1)S(1)}, bf16[96,2048]{1,0:T(8,128)(2,1)}, u32[]{:S(2)}) copy-start(bf16[96,2048]{1,0:T(8,128)(2,1)} %get-tuple-element.25) | copy-start | bytes 1179652
  88.6 1.7 %copy-start.5 = (f32[128,384]{1,0:T(8,128)S(1)}, f32[128,384]{1,0:T(8,128)}, u32[]{:S(2)}) copy-start(f32[128,384]{1,0:T(8,128)} %copy.22) | copy-start | bytes 589828
  93.8 0.9 copy-start.6
  104.4 17.0 %collective-permute-start.16 = (bf16[288,2048]{1,0:T(8,128)(2,1)S(1)}, bf16[288,2048]{1,0:T(8,128)(2,1)S(1)}, u32[]{:S(2)}, u32[]{:S(2)}) collective-permute-start(bf16[288,2048]{1,0:T(8,128)(2,1)S(1)} %pad_maximum_fusion.5), channel_id=1, source_target_pairs={{0,4},{4,0},{8,12},{12,8},{1,5},{5,1},{9,13},{13,9},{2,6},{6,2},{1... | collective-permute-start | bytes 3538952 | tf_op jit(solution)/shard_map/ppermute | solution.py:17
  105.4 15.5 %collective-permute-start.6 = (bf16[128,2048]{1,0:T(8,128)(2,1)S(1)}, bf16[128,2048]{1,0:T(8,128)(2,1)S(1)}, u32[]{:S(2)}, u32[]{:S(2)}) collective-permute-start(bf16[128,2048]{1,0:T(8,128)(2,1)S(1)} %fusion), channel_id=1, source_target_pairs={{0,1},{1,3},{3,2},{2,0},{4,5},{5,7},{7,6},{6,4},{8,9},{9,11},{11,1... | collective-permute-start | bytes 1572872 | tf_op jit(solution)/shard_map/ppermute | solution.py:13
  106.3 44.9 %collective-permute-start.15 = (bf16[288,2048]{1,0:T(8,128)(2,1)S(1)}, bf16[288,2048]{1,0:T(8,128)(2,1)S(1)}, u32[]{:S(2)}, u32[]{:S(2)}) collective-permute-start(bf16[288,2048]{1,0:T(8,128)(2,1)S(1)} %pad_maximum_fusion.4), channel_id=1, source_target_pairs={{0,4},{4,0},{8,12},{12,8},{1,5},{5,1},{9,13},{13,9},{2,6},{6,2},{1... | collective-permute-start | bytes 3538952 | tf_op jit(solution)/shard_map/ppermute | solution.py:17
  121.3 14.5 %collective-permute-start.10 = (bf16[128,2048]{1,0:T(8,128)(2,1)S(1)}, bf16[128,2048]{1,0:T(8,128)(2,1)S(1)}, u32[]{:S(2)}, u32[]{:S(2)}) collective-permute-start(bf16[128,2048]{1,0:T(8,128)(2,1)S(1)} %fusion.4), channel_id=1, source_target_pairs={{0,1},{1,3},{3,2},{2,0},{4,5},{5,7},{7,6},{6,4},{8,9},{9,11},{11,1... | collective-permute-start | bytes 1572872 | tf_op jit(solution)/shard_map/ppermute | solution.py:13
  121.9 29.3 %collective-permute-start.17 = (bf16[288,2048]{1,0:T(8,128)(2,1)S(1)}, bf16[288,2048]{1,0:T(8,128)(2,1)S(1)}, u32[]{:S(2)}, u32[]{:S(2)}) collective-permute-start(bf16[288,2048]{1,0:T(8,128)(2,1)S(1)} %add_convert_fusion), channel_id=1, source_target_pairs={{0,8},{4,12},{8,0},{12,4},{1,9},{5,13},{9,1},{13,5},{2,10},{6,14},... | collective-permute-start | bytes 3538952 | tf_op jit(solution)/shard_map/ppermute | solution.py:17
  136.3 13.6 %collective-permute-start.14 = (bf16[128,2048]{1,0:T(8,128)(2,1)S(1)}, bf16[128,2048]{1,0:T(8,128)(2,1)S(1)}, u32[]{:S(2)}, u32[]{:S(2)}) collective-permute-start(bf16[128,2048]{1,0:T(8,128)(2,1)S(1)} %fusion.8), channel_id=1, source_target_pairs={{0,1},{1,3},{3,2},{2,0},{4,5},{5,7},{7,6},{6,4},{8,9},{9,11},{11,1... | collective-permute-start | bytes 1572872 | tf_op jit(solution)/shard_map/ppermute | solution.py:13

commit v2 on v1

v2 whole, which is shorter than its diff:
```python
import functools

import jax
import jax.numpy as jnp
from jax import lax
from jax.experimental import pallas as pl
from jax.experimental.pallas import tpu as pltpu
from jax.sharding import PartitionSpec as P

BF16 = jnp.bfloat16
F32 = jnp.float32


def ring_pairs(count, turns):
    order = [0] + list(range(1, count, 2)) + list(range(2, count, 2))[::-1]
    return [(order[i], order[(i + turns) % count]) for i in range(count)]


def onward(block, turns=1):
    return lax.ppermute(block, "dp", ring_pairs(lax.axis_size("dp"), turns))


def swapped(block, bit):
    return lax.ppermute(block, "expert", [(i, i ^ bit) for i in range(lax.axis_size("expert"))])


def bits_of(count):
    return [1 << i for i in range(count.bit_length() - 1)]


def all_experts(block):
    held = {0: block}
    for bit in bits_of(lax.axis_size("expert"))[::-1]:
        held.update({k | bit: swapped(v, bit) for k, v in list(held.items())})
    return [held[k] for k in range(len(held))]


def summed_to_owner(terms):
    left, sent = dict(enumerate(terms)), None
    for bit in bits_of(len(terms)):
        stay = [k for k in left if not k & bit]
        got = {k: swapped(left[k | bit], bit) for k in stay[::-1]}
        left = {k: left[k].astype(F32) + got[k].astype(F32) for k in stay}
        if len(left) > 1:
            left = {k: v.astype(BF16) for k, v in left.items()}
            sent = left[max(left)]
    return left[0], sent


def call(kernel, outs, *args, flops=0, scratch=()):
    total = sum(a.size * a.dtype.itemsize for a in (*args, *outs))
    return pl.pallas_call(
        kernel,
        out_shape=list(outs),
        in_specs=[pl.BlockSpec(memory_space=pltpu.VMEM)] * len(args),
        out_specs=[pl.BlockSpec(memory_space=pltpu.VMEM)] * len(outs),
        scratch_shapes=list(scratch),
        compiler_params=pltpu.CompilerParams(vmem_limit_bytes=40 * 1024 * 1024),
        cost_estimate=pl.CostEstimate(flops=flops, bytes_accessed=total, transcendentals=0),
    )(*args)


def dot_nt(a, b):
    return lax.dot_general(a, b, (((1,), (1,)), ((), ())), preferred_element_type=F32)


def dot_tn(a, b):
    return lax.dot_general(a, b, (((0,), (0,)), ((), ())), preferred_element_type=F32)


def dot_nn(a, b):
    return jnp.dot(a, b, preferred_element_type=F32)


def grads_of(gate_act, up_act, back, weight):
    sigma = jax.nn.sigmoid(gate_act)
    silu_gate = gate_act * sigma
    weighted = weight * silu_gate * up_act
    back = weight * back
    gate_grad = back * up_act * sigma * (1.0 + gate_act * (1.0 - sigma))
    return gate_grad.astype(BF16), (back * silu_gate).astype(BF16), weighted.astype(BF16)


def spread(refs, *counts):
    at, groups = 0, []
    for count in counts:
        groups.append(refs[at : at + count])
        at += count
    return *groups, refs[at:]


def put_contrib(both, gate_up, contrib):
    wide2, width = gate_up[0].shape
    step = min(512, width)
    for at in range(0, width, step):
        cols = slice(at, at + step)
        total = None
        for k, block in enumerate(gate_up):
            term = dot_tn(both[k * wide2 : (k + 1) * wide2, :], block[:, cols])
            total = term if total is None else total + term
        contrib[:, cols] = total.astype(BF16)


def put_weight_grads(ks, xs, dys, both, hid, gate_up, down):
    wide, width = down[0].shape
    count = xs[0].shape[0]
    step = min(512, width)
    for n, k in enumerate(ks):
        for acts, rows, out, size in ((hid, dys, down[n], wide), (both, xs, gate_up[n], 2 * wide)):
            left = jnp.concatenate([a[k * size : (k + 1) * size, :] for a in acts], axis=1)
            for at in range(0, width, step):
                cols = slice(at, at + step)
                right = jnp.concatenate([r[:count, cols] for r in rows], axis=0)
                out[:, cols] = dot_nn(left, right).astype(BF16)


def weights_of(dyp, experts, rows):
    width = dyp.shape[1]
    per = width // rows
    packed = dyp[rows:, :].astype(F32)
    return [
        packed[k // per : k // per + 1, k % per * rows : (k % per + 1) * rows] for k in range(experts)
    ]


def slab_kernel(experts, *refs):
    (x, dyp), gate_up, down, (both, hid, contrib) = spread(refs, 2, experts, experts)
    rows, wide = x.shape[0], down[0].shape[0]
    weights = weights_of(dyp, experts, rows)
    for k in range(experts):
        acts = dot_nt(gate_up[k][...], x[...])
        back = dot_nt(down[k][...], dyp[:rows, :])
        gate_grad, up_grad, weighted = grads_of(acts[:wide], acts[wide:], back, weights[k])
        both[2 * k * wide : (2 * k + 1) * wide, :] = gate_grad
        both[(2 * k + 1) * wide : (2 * k + 2) * wide, :] = up_grad
        hid[k * wide : (k + 1) * wide, :] = weighted
    put_contrib(both, gate_up, contrib)


def acts_kernel(experts, *refs):
    (x,), gate_up, (acts,) = spread(refs, 1, experts)
    wide = gate_up[0].shape[0] // 2
    for k in range(experts):
        acts[2 * k * wide : 2 * (k + 1) * wide, :] = dot_nt(gate_up[k][...], x[...])


def far_kernel(experts, slabs, ks, *refs):
    (acts,), down, xs, dys, both, hid, outs = spread(
        refs, 1, experts, slabs, slabs, slabs - 1, slabs - 1
    )
    (last, last_hid), out_gate_up, out_down, _ = spread(outs, 2, len(ks), len(ks))
    rows, wide = xs[0].shape[0], down[0].shape[0]
    weights = weights_of(dys[-1], experts, rows)
    for k in range(experts):
        back = dot_nt(down[k][...], dys[-1][:rows, :])
        gate_act = acts[2 * k * wide : (2 * k + 1) * wide, :]
        up_act = acts[(2 * k + 1) * wide : (2 * k + 2) * wide, :]
        gate_grad, up_grad, weighted = grads_of(gate_act, up_act, back, weights[k])
        last[2 * k * wide : (2 * k + 1) * wide, :] = gate_grad
        last[(2 * k + 1) * wide : (2 * k + 2) * wide, :] = up_grad
        last_hid[k * wide : (k + 1) * wide, :] = weighted
    put_weight_grads(ks, xs, dys, (*both, last), (*hid, last_hid), out_gate_up, out_down)


def near_kernel(experts, slabs, ks, *refs):
    gate_up, xs, dys, both, hid, outs = spread(refs, experts, slabs, slabs, slabs, slabs)
    (contrib,), out_gate_up, out_down, _ = spread(outs, 1, len(ks), len(ks))
    put_weight_grads(ks, xs, dys, both, hid, out_gate_up, out_down)
    put_contrib(both[-1], gate_up, contrib)


def shape(rows, cols, kind=BF16):
    return jax.ShapeDtypeStruct((rows, cols), kind)


def after(value, *others):
    return lax.optimization_barrier((value, *others))[0]


def body(tokens, route_ids, route_probs, cotangent, w_gate_up, w_down):
    turns = lax.axis_size("dp")
    experts = lax.axis_size("expert")
    here = lax.axis_index("expert")
    wide, width = w_down.shape[1:]
    names = jnp.arange(experts, dtype=jnp.int32) ^ here

    rows = tokens.shape[0]
    prob = jnp.sum(
        jnp.where(route_ids[None] == names[:, None, None], route_probs[None], 0), axis=2
    ).astype(BF16)
    packed = jnp.zeros((-(-prob.size // (8 * width)) * 8 * width,), BF16).at[: prob.size].set(prob.reshape(-1))
    xs, dys = [tokens], [jnp.concatenate([cotangent, packed.reshape(-1, width)])]
    for _ in range(turns - 1):
        xs.append(onward(xs[-1]))
        dys.append(onward(dys[-1]))
    gate_up = all_experts(w_gate_up.reshape(2 * wide, width))
    down = all_experts(w_down.reshape(wide, width))

    slabs, units = len(xs), experts * wide
    unit_flops = 2 * rows * width * units
    both, hid, contrib = [], [], []
    for x, dyp in zip(xs[:-1], dys):
        b, h, c = call(
            functools.partial(slab_kernel, experts),
            (shape(2 * units, rows), shape(units, rows), shape(rows, width)),
            x, dyp, *gate_up, *down,
            flops=5 * unit_flops,
        )
        both.append(b)
        hid.append(h)
        contrib.append(c)
    (acts,) = call(
        functools.partial(acts_kernel, experts),
        (shape(2 * units, rows, F32),),
        xs[-1], *gate_up,
        flops=2 * unit_flops,
    )

    far = tuple(range(experts // 2, experts))[::-1]
    near = tuple(range(experts // 2))[::-1]
    grads = [shape(2 * wide, width)] * len(far) + [shape(wide, width)] * len(far)
    b, h, *got_far = call(
        functools.partial(far_kernel, experts, slabs, far),
        (shape(2 * units, rows), shape(units, rows), *grads),
        acts, *down, *xs, *dys, *both, *hid,
        flops=3 * slabs * unit_flops // 2 + unit_flops,
    )
    both.append(b)
    hid.append(h)
    c, *got_near = call(
        functools.partial(near_kernel, experts, slabs, near),
        (shape(rows, width), *grads),
        *gate_up, *xs, *dys, *both, *hid,
        flops=3 * slabs * unit_flops // 2 + 2 * unit_flops,
    )
    contrib.append(c)
    terms_gate_up = dict(zip(far + near, got_far[: len(far)] + got_near[: len(near)]))
    terms_down = dict(zip(far + near, got_far[len(far) :] + got_near[len(near) :]))
    grad_down, sent_down = summed_to_owner([terms_down[k] for k in range(experts)])
    grad_gate_up, sent_gate_up = summed_to_owner([terms_gate_up[k] for k in range(experts)])

    half = width // 2
    done = []
    for cols in (slice(0, half), slice(half, width)):
        part = onward(after(contrib[1 % slabs][:, cols], xs[-1]))
        part = after(part, sent_gate_up, sent_down)
        for i in range(2, slabs + 1):
            if i > 2:
                part = onward(part)
            part = (part.astype(F32) + contrib[i % slabs][:, cols].astype(F32)).astype(BF16)
        done.append(part)
    acc = jnp.concatenate(done, axis=1)
    return acc, grad_gate_up.reshape(1, 2, wide, width), grad_down.reshape(1, wide, width)


def solution(mesh):
    placed = (
        P(("groups", "expert", "dp"), None),
        P(("groups", "expert", "dp"), None),
        P(("groups", "expert", "dp"), None),
        P(("groups", "expert", "dp"), None),
        P("expert", None, "dp", None),
        P("expert", "dp", None),
    )
    return jax.shard_map(
        body,
        mesh=mesh,
        in_specs=placed,
        out_specs=(
            P(("groups", "expert", "dp"), None),
            P(("groups", "expert"), None, "dp", None),
            P(("groups", "expert"), "dp", None),
        ),
        check_vma=False,
    )
```

time: 155 us -> 130 us (0.84)
  matrix products: 23.6 us -> 0 us
  waiting for transfers between devices: 99.9 us -> 79.6 us
  starting transfers between devices: 13.8 us -> 30.8 us
  Pallas kernels: 0 us -> 12.1 us
  local copies, waits for them, and re-layouts: 11.5 us -> 1.16 us
    ppermute x12, waiting for transfers between devices: 99.9 us -> 72.4 us  [onward(): return lax.ppermute(block, 'dp', ring_pairs(lax.axis_size('dp'), turns))]
    dot_general x23 -> x0, matrix products: 23.6 us -> none  [f32_dot(): return jnp.einsum(spec, a, b, preferred_element_type=jnp.float32)]
    ppermute x12, starting transfers between devices: 9.85 us -> 23.2 us  [onward(): return lax.ppermute(block, 'dp', ring_pairs(lax.axis_size('dp'), turns))]
    pallas_call x0 -> x6, Pallas kernels: none -> 12.1 us  [call(): pl.pallas_call(kernel, out_shape=list(outs), in_specs=[pl.BlockSpec(memor...]
    ppermute x6 -> x12, waiting for transfers between devices: 0.02 us -> 7.16 us  [swapped(): lax.ppermute(block, 'expert', [(i, i ^ bit) for i in range(lax.axis_size(...]
    slice x7 -> x1, local copies, waits for them, and re-layouts: 5.37 us -> 0.03 us  [body(): part = onward(after(contrib[1 % slabs][:, cols], xs[-1]))]
    ppermute x6 -> x12, starting transfers between devices: 3.96 us -> 7.6 us  [swapped(): lax.ppermute(block, 'expert', [(i, i ^ bit) for i in range(lax.axis_size(...]
    reshape x5 -> x1, local copies, waits for them, and re-layouts: 3.51 us -> 0.02 us  [body(): packed.reshape(-1, width)]
  transfers between devices with their start and end apart: 18 -> 24, of which waited for: 8 -> 14; matrix products, arithmetic and copies ran while one was open for 16% -> 3% of each run, Pallas kernels for 0% -> 8%
where the time goes in v2:
time: 130 us
  waiting for transfers between devices  79.6 us (61%)
  starting transfers between devices  30.8 us (24%)
  Pallas kernels  12.1 us (9%)
  other arithmetic  5.08 us (4%)
    ppermute x12, waiting for transfers between devices, onward(): return lax.ppermute(block, 'dp', ring_pairs(lax.axis_size('dp'), turns))  72.4 us
    ppermute x12, starting transfers between devices, onward(): return lax.ppermute(block, 'dp', ring_pairs(lax.axis_size('dp'), turns))  23.2 us
    pallas_call x6, Pallas kernels, call(): pl.pallas_call(kernel, out_shape=list(outs), in_specs=[pl.BlockSpec(memor...  12.1 us
    ppermute x12, starting transfers between devices, swapped(): lax.ppermute(block, 'expert', [(i, i ^ bit) for i in range(lax.axis_size(...  7.6 us
    ppermute x12, waiting for transfers between devices, swapped(): lax.ppermute(block, 'expert', [(i, i ^ bit) for i in range(lax.axis_size(...  7.16 us
  transfers between devices with their start and end apart: 24, of which 14 were waited for; matrix products, arithmetic and copies ran while one was open for 3% of the time, Pallas kernels for 8%

profile of v2, /device:TPU:0, one launch (start us, length us, event | category | flops | bytes accessed | tf_op | source)
XLA Modules:
  0.0 129.6 jit_solution(3347533070376875114)
XLA Ops:
  0.6 0.0 copy-start
  0.6 3.1 %collective-permute-start = (bf16[128,2048]{1,0:T(8,128)(2,1)}, bf16[128,2048]{1,0:T(8,128)(2,1)S(1)}, u32[]{:S(2)}, u32[]{:S(2)}) collective-permute-start(bf16[128,2048]{1,0:T(8,128)(2,1)} %refs_4_.1), channel_id=1, source_target_pairs={{0,1},{1,3},{3,2},{2,0},{4,5},{5,7},{7,6},{6,4},{8,9},{9,11},{11,1... | collective-permute-start | bytes 1572872 | tf_op jit(solution)/shard_map/ppermute | solution.py:20
  3.7 1.5 %collective-permute-start.3 = (bf16[192,2048]{1,0:T(8,128)(2,1)}, bf16[192,2048]{1,0:T(8,128)(2,1)S(1)}, u32[]{:S(2)}, u32[]{:S(2)}) collective-permute-start(bf16[192,2048]{1,0:T(8,128)(2,1)} %bitcast.6), channel_id=1, source_target_pairs={{0,8},{4,12},{8,0},{12,4},{1,9},{5,13},{9,1},{13,5},{2,10},{6,14},... | collective-permute-start | bytes 2359304 | tf_op jit(solution)/shard_map/ppermute | solution.py:24
  5.2 1.1 constant_dynamic-update-slice_fusion.1
  6.3 0.8 fusion
  7.1 2.6 %collective-permute-start.1 = (bf16[136,2048]{1,0:T(8,128)(2,1)S(1)}, bf16[136,2048]{1,0:T(8,128)(2,1)S(1)}, u32[]{:S(2)}, u32[]{:S(2)}) collective-permute-start(bf16[136,2048]{1,0:T(8,128)(2,1)S(1)} %constant_dynamic-update-slice_fusion.refs_1_.refs_9_.refs_8_), channel_id=1, source_target_pairs={{0,1},{1,3},{3,2},{2,0},{4,5},{5,7},{7,6},{6,4},{8,9},{9,11},{11,1... | collective-permute-start | bytes 1671176 | tf_op jit(solution)/shard_map/ppermute | solution.py:20
  9.8 0.0 collective-permute-start.2
  9.8 7.9 %collective-permute-done.refs_0_.refs_6_.refs_5_ = bf16[128,2048]{1,0:T(8,128)(2,1)S(1)} collective-permute-done((bf16[128,2048]{1,0:T(8,128)(2,1)}, bf16[128,2048]{1,0:T(8,128)(2,1)S(1)}, u32[]{:S(2)}, u32[]{:S(2)}) %collective-permute-start) | collective-permute-done | bytes 524320 | tf_op jit(solution)/shard_map/ppermute | solution.py:20
  17.7 1.3 collective-permute-start.8
  19.0 10.7 %collective-permute-done.1.refs_1_.refs_10_.refs_9_ = bf16[136,2048]{1,0:T(8,128)(2,1)S(1)} collective-permute-done((bf16[136,2048]{1,0:T(8,128)(2,1)S(1)}, bf16[136,2048]{1,0:T(8,128)(2,1)S(1)}, u32[]{:S(2)}, u32[]{:S(2)}) %collective-permute-start.1) | collective-permute-done | bytes 557088 | tf_op jit(solution)/shard_map/ppermute | solution.py:20
  29.6 1.2 collective-permute-start.11
  30.8 0.0 collective-permute-done.3.refs_4_.refs_3_.refs_2_
  30.8 0.0 collective-permute-start.4
  30.8 1.6 %collective-permute-start.6 = (bf16[96,2048]{1,0:T(8,128)(2,1)}, bf16[96,2048]{1,0:T(8,128)(2,1)S(1)}, u32[]{:S(2)}, u32[]{:S(2)}) collective-permute-start(bf16[96,2048]{1,0:T(8,128)(2,1)} %bitcast.13), channel_id=1, source_target_pairs={{0,8},{4,12},{8,0},{12,4},{1,9},{5,13},{9,1},{13,5},{2,10},{6,14},... | collective-permute-start | bytes 1179656 | tf_op jit(solution)/shard_map/ppermute | solution.py:24
  32.4 8.5 %collective-permute-done.8.refs_0_.refs_7_.refs_6_ = bf16[128,2048]{1,0:T(8,128)(2,1)S(1)} collective-permute-done((bf16[128,2048]{1,0:T(8,128)(2,1)S(1)}, bf16[128,2048]{1,0:T(8,128)(2,1)S(1)}, u32[]{:S(2)}, u32[]{:S(2)}) %collective-permute-start.8) | collective-permute-done | bytes 524320 | tf_op jit(solution)/shard_map/ppermute | solution.py:20
  40.9 1.2 collective-permute-start.9
  42.0 0.5 collective-permute-done.6.refs_8_.refs_3_
  42.5 0.0 collective-permute-start.5
  42.5 0.0 collective-permute-done.2.refs_3_.refs_2_.refs_1_
  42.5 0.5 collective-permute-start.7
  43.0 9.8 %collective-permute-done.11.refs_1_.refs_11_.refs_10_ = bf16[136,2048]{1,0:T(8,128)(2,1)S(1)} collective-permute-done((bf16[136,2048]{1,0:T(8,128)(2,1)S(1)}, bf16[136,2048]{1,0:T(8,128)(2,1)S(1)}, u32[]{:S(2)}, u32[]{:S(2)}) %collective-permute-start.11) | collective-permute-done | bytes 557088 | tf_op jit(solution)/shard_map/ppermute | solution.py:20
  52.8 1.2 collective-permute-start.12
  54.0 10.1 %collective-permute-done.9.refs_0_.refs_8_.refs_7_ = bf16[128,2048]{1,0:T(8,128)(2,1)S(1)} collective-permute-done((bf16[128,2048]{1,0:T(8,128)(2,1)S(1)}, bf16[128,2048]{1,0:T(8,128)(2,1)S(1)}, u32[]{:S(2)}, u32[]{:S(2)}) %collective-permute-start.9) | collective-permute-done | bytes 524320 | tf_op jit(solution)/shard_map/ppermute | solution.py:20
  64.0 0.0 collective-permute-done.4.refs_5_.refs_4_.refs_3_
  64.0 1.0 shard_map.86.refs_0_
  65.0 0.0 copy-start.2
  65.0 0.0 collective-permute-done.5.refs_7_.refs_2_
  65.0 0.0 collective-permute-done.7.refs_9_.refs_4_
  65.1 2.2 %shard_map.85 = (bf16[768,128]{1,0:T(8,128)(2,1)S(1)}, bf16[384,128]{1,0:T(8,128)(2,1)S(1)}, bf16[128,2048]{1,0:T(8,128)(2,1)S(1)}) custom-call(bf16[128,2048]{1,0:T(8,128)(2,1)S(1)} %collective-permute-done.refs_0_.refs_6_.refs_5_, bf16[136,2048]{1,0:T(8,128)(2,1)S(1)} %collective-permute-done.1.refs_1_.refs_10_.refs_9_, bf16[192,2048]{1,0:T(8,128)(2,1)S(1)} %bitcast.9, ...), custom_call_target="tpu_custom_call" | custom-call | flops 1006632960 | bytes 6619136 | tf_op jit(solution)/shard_map/pallas_call | solution.py:52
  67.3 2.2 %shard_map.87 = (bf16[768,128]{1,0:T(8,128)(2,1)S(1)}, bf16[384,128]{1,0:T(8,128)(2,1)S(1)}, bf16[128,2048]{1,0:T(8,128)(2,1)S(1)}) custom-call(bf16[128,2048]{1,0:T(8,128)(2,1)S(1)} %copy-done.2, bf16[136,2048]{1,0:T(8,128)(2,1)S(1)} %constant_dynamic-update-slice_fusion.refs_1_.refs_9_.refs_8_, bf16[192,2048]{1,0:T(8,128)(2,1)S(1)} %bitcast.10, ...), custom_call_target="tpu_custom_call" | custom-call | flops 1006632960 | bytes 6619136 | tf_op jit(solution)/shard_map/pallas_call | solution.py:52
  69.5 2.2 %shard_map.88 = (bf16[768,128]{1,0:T(8,128)(2,1)S(1)}, bf16[384,128]{1,0:T(8,128)(2,1)S(1)}, bf16[128,2048]{1,0:T(8,128)(2,1)S(1)}) custom-call(bf16[128,2048]{1,0:T(8,128)(2,1)S(1)} %collective-permute-done.8.refs_0_.refs_7_.refs_6_, bf16[136,2048]{1,0:T(8,128)(2,1)S(1)} %collective-permute-done.11.refs_1_.refs_11_.refs_10_, ...), custom_call_target="tpu_custom_call" | custom-call | flops 1006632960 | bytes 6619136 | tf_op jit(solution)/shard_map/pallas_call | solution.py:52
  71.7 3.4 %collective-permute-done.12.refs_12_.refs_11_ = bf16[136,2048]{1,0:T(8,128)(2,1)S(1)} collective-permute-done((bf16[136,2048]{1,0:T(8,128)(2,1)S(1)}, bf16[136,2048]{1,0:T(8,128)(2,1)S(1)}, u32[]{:S(2)}, u32[]{:S(2)}) %collective-permute-start.12) | collective-permute-done | bytes 557088 | tf_op jit(solution)/shard_map/ppermute | solution.py:20
  75.2 2.3 %shard_map.89 = (bf16[768,128]{1,0:T(8,128)(2,1)S(1)}, bf16[384,128]{1,0:T(8,128)(2,1)S(1)}, bf16[192,2048]{1,0:T(8,128)(2,1)S(1)}, bf16[192,2048]{1,0:T(8,128)(...) custom-call(f32[768,128]{1,0:T(8,128)S(1)} %shard_map.86.refs_0_, bf16[96,2048]{1,0:T(8,128)(2,1)S(1)} %bitcast.18, ...), custom_call_target="tpu_custom_call" | custom-call | flops 1409286144 | bytes 9830400 | tf_op jit(solution)/shard_map/pallas_call | solution.py:52
  77.5 0.1 collective-permute-start.14
  77.5 0.5 collective-permute-start.13
  78.1 0.9 collective-permute-start.10
  79.0 3.4 %collective-permute-start.17 = (bf16[128,1024]{1,0:T(8,128)(2,1)S(1)}, bf16[128,1024]{1,0:T(8,128)(2,1)S(1)}, u32[]{:S(2)}, u32[]{:S(2)}) collective-permute-start(bf16[128,1024]{1,0:T(8,128)(2,1)S(1)} %get-tuple-element.57), channel_id=1, source_target_pairs={{0,1},{1,3},{3,2},{2,0},{4,5},{5,7},{7,6},{6,4},{8,9},{9,11},{11,1... | collective-permute-start | bytes 786440 | tf_op jit(solution)/shard_map/ppermute | solution.py:20
  82.4 0.1 add_convert_fusion.3
  82.5 0.0 collective-permute-done.13
  82.5 0.3 add_convert_fusion.1
  82.7 5.5 %collective-permute-done.10 = bf16[128,1024]{1,0:T(8,128)(2,1)S(1)} collective-permute-done((bf16[128,1024]{1,0:T(8,128)(2,1)S(1)}, bf16[128,1024]{1,0:T(8,128)(2,1)S(1)}, u32[]{:S(2)}, u32[]{:S(2)}) %collective-permute-start.10) | collective-permute-done | bytes 262176 | tf_op jit(solution)/shard_map/ppermute | solution.py:20
  88.2 4.7 %collective-permute-done.17 = bf16[128,1024]{1,0:T(8,128)(2,1)S(1)} collective-permute-done((bf16[128,1024]{1,0:T(8,128)(2,1)S(1)}, bf16[128,1024]{1,0:T(8,128)(2,1)S(1)}, u32[]{:S(2)}, u32[]{:S(2)}) %collective-permute-start.17) | collective-permute-done | bytes 262176 | tf_op jit(solution)/shard_map/ppermute | solution.py:20
  92.9 0.2 add_convert_fusion.9
  93.1 0.9 collective-permute-start.15
  94.0 3.4 %collective-permute-start.18 = (bf16[128,1024]{1,0:T(8,128)(2,1)S(1)}, bf16[128,1024]{1,0:T(8,128)(2,1)S(1)}, u32[]{:S(2)}, u32[]{:S(2)}) collective-permute-start(bf16[128,1024]{1,0:T(8,128)(2,1)S(1)} %get-tuple-element.68), channel_id=1, source_target_pairs={{0,1},{1,3},{3,2},{2,0},{4,5},{5,7},{7,6},{6,4},{8,9},{9,11},{11,1... | collective-permute-start | bytes 786440 | tf_op jit(solution)/shard_map/ppermute | solution.py:20
  97.4 2.2 %shard_map.90 = (bf16[128,2048]{1,0:T(8,128)(2,1)S(1)}, bf16[192,2048]{1,0:T(8,128)(2,1)S(1)}, bf16[192,2048]{1,0:T(8,128)(2,1)S(1)}, bf16[96,2048]{1,0:T(8,128)(2,1)S(1)}, bf16[96,2048]{1,0:T(8,128)(2,1)S(1)}) custom-call(bf16[192,2048]{1,0:T(8,128)(2,1)S(1)} %bitcast.12, bf16[192,2048]{1,0:T(8,128)(2,1)S(1)} %collective-permute-done.2.refs_3_.refs_2_.refs_1_, ...), custom_call_target="tpu_custom_call" | custom-call | flops 1610612736 | bytes 11534336 | tf_op jit(solution)/shard_map/pallas_call | solution.py:52
  99.6 0.1 collective-permute-start.22
  99.7 1.6 %collective-permute-start.23 = (bf16[96,2048]{1,0:T(8,128)(2,1)S(1)}, bf16[96,2048]{1,0:T(8,128)(2,1)S(1)}, u32[]{:S(2)}, u32[]{:S(2)}) collective-permute-start(bf16[96,2048]{1,0:T(8,128)(2,1)S(1)} %add_convert_fusion.3), channel_id=1, source_target_pairs={{0,8},{4,12},{8,0},{12,4},{1,9},{5,13},{9,1},{13,5},{2,10},{6,14},... | collective-permute-start | bytes 1179656 | tf_op jit(solution)/shard_map/ppermute | solution.py:24
  101.3 0.2 collective-permute-start.20
  101.5 1.9 %collective-permute-done.15 = bf16[128,1024]{1,0:T(8,128)(2,1)S(1)} collective-permute-done((bf16[128,1024]{1,0:T(8,128)(2,1)S(1)}, bf16[128,1024]{1,0:T(8,128)(2,1)S(1)}, u32[]{:S(2)}, u32[]{:S(2)}) %collective-permute-start.15) | collective-permute-done | bytes 262176 | tf_op jit(solution)/shard_map/ppermute | solution.py:20
  103.3 1.6 %collective-permute-start.21 = (bf16[192,2048]{1,0:T(8,128)(2,1)S(1)}, bf16[192,2048]{1,0:T(8,128)(2,1)S(1)}, u32[]{:S(2)}, u32[]{:S(2)}) collective-permute-start(bf16[192,2048]{1,0:T(8,128)(2,1)S(1)} %add_convert_fusion.1), channel_id=1, source_target_pairs={{0,8},{4,12},{8,0},{12,4},{1,9},{5,13},{9,1},{13,5},{2,10},{6,14},... | collective-permute-start | bytes 2359304 | tf_op jit(solution)/shard_map/ppermute | solution.py:24
  104.9 2.3 %collective-permute-done.18 = bf16[128,1024]{1,0:T(8,128)(2,1)S(1)} collective-permute-done((bf16[128,1024]{1,0:T(8,128)(2,1)S(1)}, bf16[128,1024]{1,0:T(8,128)(2,1)S(1)}, u32[]{:S(2)}, u32[]{:S(2)}) %collective-permute-start.18) | collective-permute-done | bytes 262176 | tf_op jit(solution)/shard_map/ppermute | solution.py:20
  107.2 0.2 add_convert_fusion.8
  107.4 0.9 collective-permute-start.16
  108.2 0.0 collective-permute-done.22
  108.3 3.4 %collective-permute-start.19 = (bf16[128,1024]{1,0:T(8,128)(2,1)S(1)}, bf16[128,1024]{1,0:T(8,128)(2,1)S(1)}, u32[]{:S(2)}, u32[]{:S(2)}) collective-permute-start(bf16[128,1024]{1,0:T(8,128)(2,1)S(1)} %get-tuple-element.66), channel_id=1, source_target_pairs={{0,1},{1,3},{3,2},{2,0},{4,5},{5,7},{7,6},{6,4},{8,9},{9,11},{11,1... | collective-permute-start | bytes 786440 | tf_op jit(solution)/shard_map/ppermute | solution.py:20
  111.6 0.0 collective-permute-done.23
  111.7 1.0 add_bitcast_fusion
  112.7 4.9 %collective-permute-done.16 = bf16[128,1024]{1,0:T(8,128)(2,1)S(1)} collective-permute-done((bf16[128,1024]{1,0:T(8,128)(2,1)S(1)}, bf16[128,1024]{1,0:T(8,128)(2,1)S(1)}, u32[]{:S(2)}, u32[]{:S(2)}) %collective-permute-start.16) | collective-permute-done | bytes 262176 | tf_op jit(solution)/shard_map/ppermute | solution.py:20
  117.6 2.9 %collective-permute-done.19 = bf16[128,1024]{1,0:T(8,128)(2,1)S(1)} collective-permute-done((bf16[128,1024]{1,0:T(8,128)(2,1)S(1)}, bf16[128,1024]{1,0:T(8,128)(2,1)S(1)}, u32[]{:S(2)}, u32[]{:S(2)}) %collective-permute-start.19) | collective-permute-done | bytes 262176 | tf_op jit(solution)/shard_map/ppermute | solution.py:20
  120.5 0.2 add_convert_fusion.7
  120.7 0.8 pad_maximum_fusion
  121.5 6.6 %collective-permute-done.21 = bf16[192,2048]{1,0:T(8,128)(2,1)S(1)} collective-permute-done((bf16[192,2048]{1,0:T(8,128)(2,1)S(1)}, bf16[192,2048]{1,0:T(8,128)(2,1)S(1)}, u32[]{:S(2)}, u32[]{:S(2)}) %collective-permute-start.21) | collective-permute-done | bytes 786464 | tf_op jit(solution)/shard_map/ppermute | solution.py:24
  128.1 1.5 %convert_add_fusion = f32[192,2048]{1,0:T(8,128)} fusion(bf16[192,2048]{1,0:T(8,128)(2,1)S(1)} %collective-permute-done.21, bf16[192,2048]{1,0:T(8,128)(2,1)S(1)} %collective-permute-done.20, bf16[192,2048]{1,0:T(8,128)(2,1)S(1)} %get-tuple-element.59), kind=kLoop, calls=%fused_computation | loop fusion | flops 2752512 | bytes 3932160 | tf_op jit(solution)/shard_map/add | solution.py:43
  (11 shorter events, 0.1 us)
Async XLA Ops:
  0.6 63.4 %copy-start = (bf16[1,2,96,2048]{3,2,1,0:T(8,128)(2,1)S(1)}, bf16[1,2,96,2048]{3,2,1,0:T(8,128)(2,1)}, u32[]{:S(2)}) copy-start(bf16[1,2,96,2048]{3,2,1,0:T(8,128)(2,1)} %param.12) | copy-start | bytes 2359300
  0.6 17.1 %collective-permute-start = (bf16[128,2048]{1,0:T(8,128)(2,1)}, bf16[128,2048]{1,0:T(8,128)(2,1)S(1)}, u32[]{:S(2)}, u32[]{:S(2)}) collective-permute-start(bf16[128,2048]{1,0:T(8,128)(2,1)} %refs_4_.1), channel_id=1, source_target_pairs={{0,1},{1,3},{3,2},{2,0},{4,5},{5,7},{7,6},{6,4},{8,9},{9,11},{11,1... | collective-permute-start | bytes 1572872 | tf_op jit(solution)/shard_map/ppermute | solution.py:20
  3.7 27.1 %collective-permute-start.3 = (bf16[192,2048]{1,0:T(8,128)(2,1)}, bf16[192,2048]{1,0:T(8,128)(2,1)S(1)}, u32[]{:S(2)}, u32[]{:S(2)}) collective-permute-start(bf16[192,2048]{1,0:T(8,128)(2,1)} %bitcast.6), channel_id=1, source_target_pairs={{0,8},{4,12},{8,0},{12,4},{1,9},{5,13},{9,1},{13,5},{2,10},{6,14},... | collective-permute-start | bytes 2359304 | tf_op jit(solution)/shard_map/ppermute | solution.py:24
  7.1 22.5 %collective-permute-start.1 = (bf16[136,2048]{1,0:T(8,128)(2,1)S(1)}, bf16[136,2048]{1,0:T(8,128)(2,1)S(1)}, u32[]{:S(2)}, u32[]{:S(2)}) collective-permute-start(bf16[136,2048]{1,0:T(8,128)(2,1)S(1)} %constant_dynamic-update-slice_fusion.refs_1_.refs_9_.refs_8_), channel_id=1, source_target_pairs={{0,1},{1,3},{3,2},{2,0},{4,5},{5,7},{7,6},{6,4},{8,9},{9,11},{11,1... | collective-permute-start | bytes 1671176 | tf_op jit(solution)/shard_map/ppermute | solution.py:20
  9.8 32.8 %collective-permute-start.2 = (bf16[192,2048]{1,0:T(8,128)(2,1)}, bf16[192,2048]{1,0:T(8,128)(2,1)S(1)}, u32[]{:S(2)}, u32[]{:S(2)}) collective-permute-start(bf16[192,2048]{1,0:T(8,128)(2,1)} %bitcast.7), channel_id=1, source_target_pairs={{0,4},{4,0},{8,12},{12,8},{1,5},{5,1},{9,13},{13,9},{2,6},{6,2},{1... | collective-permute-start | bytes 2359304 | tf_op jit(solution)/shard_map/ppermute | solution.py:24
  17.7 23.2 %collective-permute-start.8 = (bf16[128,2048]{1,0:T(8,128)(2,1)S(1)}, bf16[128,2048]{1,0:T(8,128)(2,1)S(1)}, u32[]{:S(2)}, u32[]{:S(2)}) collective-permute-start(bf16[128,2048]{1,0:T(8,128)(2,1)S(1)} %collective-permute-done.refs_0_.refs_6_.refs_5_), channel_id=1, source_target_pairs={{0,1},{1,3},{3,2},{2,0},{4,5},{5,7},{7,6},{6,4},{8,9},{9,11},{11,1... | collective-permute-start | bytes 1572872 | tf_op jit(solution)/shard_map/ppermute | solution.py:20
  29.6 23.2 %collective-permute-start.11 = (bf16[136,2048]{1,0:T(8,128)(2,1)S(1)}, bf16[136,2048]{1,0:T(8,128)(2,1)S(1)}, u32[]{:S(2)}, u32[]{:S(2)}) collective-permute-start(bf16[136,2048]{1,0:T(8,128)(2,1)S(1)} %collective-permute-done.1.refs_1_.refs_10_.refs_9_), channel_id=1, source_target_pairs={{0,1},{1,3},{3,2},{2,0},{4,5},{5,7},{7,6},{6,4},{8,9},{9,11},{11,1... | collective-permute-start | bytes 1671176 | tf_op jit(solution)/shard_map/ppermute | solution.py:20
  30.8 33.3 %collective-permute-start.4 = (bf16[192,2048]{1,0:T(8,128)(2,1)S(1)}, bf16[192,2048]{1,0:T(8,128)(2,1)S(1)}, u32[]{:S(2)}, u32[]{:S(2)}) collective-permute-start(bf16[192,2048]{1,0:T(8,128)(2,1)S(1)} %collective-permute-done.3.refs_4_.refs_3_.refs_2_), channel_id=1, source_target_pairs={{0,4},{4,0},{8,12},{12,8},{1,5},{5,1},{9,13},{13,9},{2,6},{6,2},{1... | collective-permute-start | bytes 2359304 | tf_op jit(solution)/shard_map/ppermute | solution.py:24
  30.8 34.3 %copy-start.1 = (bf16[1,96,2048]{2,1,0:T(8,128)(2,1)S(1)}, bf16[1,96,2048]{2,1,0:T(8,128)(2,1)}, u32[]{:S(2)}) copy-start(bf16[1,96,2048]{2,1,0:T(8,128)(2,1)} %param.13) | copy-start | bytes 1179652
  30.8 11.7 %collective-permute-start.6 = (bf16[96,2048]{1,0:T(8,128)(2,1)}, bf16[96,2048]{1,0:T(8,128)(2,1)S(1)}, u32[]{:S(2)}, u32[]{:S(2)}) collective-permute-start(bf16[96,2048]{1,0:T(8,128)(2,1)} %bitcast.13), channel_id=1, source_target_pairs={{0,8},{4,12},{8,0},{12,4},{1,9},{5,13},{9,1},{13,5},{2,10},{6,14},... | collective-permute-start | bytes 1179656 | tf_op jit(solution)/shard_map/ppermute | solution.py:24
  40.9 23.2 %collective-permute-start.9 = (bf16[128,2048]{1,0:T(8,128)(2,1)S(1)}, bf16[128,2048]{1,0:T(8,128)(2,1)S(1)}, u32[]{:S(2)}, u32[]{:S(2)}) collective-permute-start(bf16[128,2048]{1,0:T(8,128)(2,1)S(1)} %collective-permute-done.8.refs_0_.refs_7_.refs_6_), channel_id=1, source_target_pairs={{0,1},{1,3},{3,2},{2,0},{4,5},{5,7},{7,6},{6,4},{8,9},{9,11},{11,1... | collective-permute-start | bytes 1572872 | tf_op jit(solution)/shard_map/ppermute | solution.py:20
  42.5 22.5 %collective-permute-start.5 = (bf16[96,2048]{1,0:T(8,128)(2,1)}, bf16[96,2048]{1,0:T(8,128)(2,1)S(1)}, u32[]{:S(2)}, u32[]{:S(2)}) collective-permute-start(bf16[96,2048]{1,0:T(8,128)(2,1)} %bitcast.14), channel_id=1, source_target_pairs={{0,4},{4,0},{8,12},{12,8},{1,5},{5,1},{9,13},{13,9},{2,6},{6,2},{1... | collective-permute-start | bytes 1179656 | tf_op jit(solution)/shard_map/ppermute | solution.py:24
  42.5 22.5 %collective-permute-start.7 = (bf16[96,2048]{1,0:T(8,128)(2,1)S(1)}, bf16[96,2048]{1,0:T(8,128)(2,1)S(1)}, u32[]{:S(2)}, u32[]{:S(2)}) collective-permute-start(bf16[96,2048]{1,0:T(8,128)(2,1)S(1)} %collective-permute-done.6.refs_8_.refs_3_), channel_id=1, source_target_pairs={{0,4},{4,0},{8,12},{12,8},{1,5},{5,1},{9,13},{13,9},{2,6},{6,2},{1... | collective-permute-start | bytes 1179656 | tf_op jit(solution)/shard_map/ppermute | solution.py:24
  52.8 22.3 %collective-permute-start.12 = (bf16[136,2048]{1,0:T(8,128)(2,1)S(1)}, bf16[136,2048]{1,0:T(8,128)(2,1)S(1)}, u32[]{:S(2)}, u32[]{:S(2)}) collective-permute-start(bf16[136,2048]{1,0:T(8,128)(2,1)S(1)} %collective-permute-done.11.refs_1_.refs_11_.refs_10_), channel_id=1, source_target_pairs={{0,1},{1,3},{3,2},{2,0},{4,5},{5,7},{7,6},{6,4},{8,9},{9,11},{11,1... | collective-permute-start | bytes 1671176 | tf_op jit(solution)/shard_map/ppermute | solution.py:20
  65.0 2.3 %copy-start.2 = (bf16[128,2048]{1,0:T(8,128)(2,1)S(1)}, bf16[128,2048]{1,0:T(8,128)(2,1)}, u32[]{:S(2)}) copy-start(bf16[128,2048]{1,0:T(8,128)(2,1)} %refs_4_.1) | copy-start | bytes 1572868
  77.5 4.9 %collective-permute-start.14 = (bf16[96,2048]{1,0:T(8,128)(2,1)S(1)}, bf16[96,2048]{1,0:T(8,128)(2,1)S(1)}, u32[]{:S(2)}, u32[]{:S(2)}) collective-permute-start(bf16[96,2048]{1,0:T(8,128)(2,1)S(1)} %get-tuple-element.50), channel_id=1, source_target_pairs={{0,4},{4,0},{8,12},{12,8},{1,5},{5,1},{9,13},{13,9},{2,6},{6,2},{1... | collective-permute-start | bytes 1179656 | tf_op jit(solution)/shard_map/ppermute | solution.py:24
  77.5 4.9 %collective-permute-start.13 = (bf16[192,2048]{1,0:T(8,128)(2,1)S(1)}, bf16[192,2048]{1,0:T(8,128)(2,1)S(1)}, u32[]{:S(2)}, u32[]{:S(2)}) collective-permute-start(bf16[192,2048]{1,0:T(8,128)(2,1)S(1)} %get-tuple-element.48), channel_id=1, source_target_pairs={{0,4},{4,0},{8,12},{12,8},{1,5},{5,1},{9,13},{13,9},{2,6},{6,2},{1... | collective-permute-start | bytes 2359304 | tf_op jit(solution)/shard_map/ppermute | solution.py:24
  78.1 10.1 %collective-permute-start.10 = (bf16[128,1024]{1,0:T(8,128)(2,1)S(1)}, bf16[128,1024]{1,0:T(8,128)(2,1)S(1)}, u32[]{:S(2)}, u32[]{:S(2)}) collective-permute-start(bf16[128,1024]{1,0:T(8,128)(2,1)S(1)} %get-tuple-element.40), channel_id=1, source_target_pairs={{0,1},{1,3},{3,2},{2,0},{4,5},{5,7},{7,6},{6,4},{8,9},{9,11},{11,1... | collective-permute-start | bytes 786440 | tf_op jit(solution)/shard_map/ppermute | solution.py:20
  79.0 14.0 %collective-permute-start.17 = (bf16[128,1024]{1,0:T(8,128)(2,1)S(1)}, bf16[128,1024]{1,0:T(8,128)(2,1)S(1)}, u32[]{:S(2)}, u32[]{:S(2)}) collective-permute-start(bf16[128,1024]{1,0:T(8,128)(2,1)S(1)} %get-tuple-element.57), channel_id=1, source_target_pairs={{0,1},{1,3},{3,2},{2,0},{4,5},{5,7},{7,6},{6,4},{8,9},{9,11},{11,1... | collective-permute-start | bytes 786440 | tf_op jit(solution)/shard_map/ppermute | solution.py:20
  93.1 10.2 %collective-permute-start.15 = (bf16[128,1024]{1,0:T(8,128)(2,1)S(1)}, bf16[128,1024]{1,0:T(8,128)(2,1)S(1)}, u32[]{:S(2)}, u32[]{:S(2)}) collective-permute-start(bf16[128,1024]{1,0:T(8,128)(2,1)S(1)} %get-tuple-element.67), channel_id=1, source_target_pairs={{0,1},{1,3},{3,2},{2,0},{4,5},{5,7},{7,6},{6,4},{8,9},{9,11},{11,1... | collective-permute-start | bytes 786440 | tf_op jit(solution)/shard_map/ppermute | solution.py:20
  94.0 13.1 %collective-permute-start.18 = (bf16[128,1024]{1,0:T(8,128)(2,1)S(1)}, bf16[128,1024]{1,0:T(8,128)(2,1)S(1)}, u32[]{:S(2)}, u32[]{:S(2)}) collective-permute-start(bf16[128,1024]{1,0:T(8,128)(2,1)S(1)} %get-tuple-element.68), channel_id=1, source_target_pairs={{0,1},{1,3},{3,2},{2,0},{4,5},{5,7},{7,6},{6,4},{8,9},{9,11},{11,1... | collective-permute-start | bytes 786440 | tf_op jit(solution)/shard_map/ppermute | solution.py:20
  99.6 8.6 %collective-permute-start.22 = (bf16[96,2048]{1,0:T(8,128)(2,1)S(1)}, bf16[96,2048]{1,0:T(8,128)(2,1)S(1)}, u32[]{:S(2)}, u32[]{:S(2)}) collective-permute-start(bf16[96,2048]{1,0:T(8,128)(2,1)S(1)} %get-tuple-element.62), channel_id=1, source_target_pairs={{0,4},{4,0},{8,12},{12,8},{1,5},{5,1},{9,13},{13,9},{2,6},{6,2},{1... | collective-permute-start | bytes 1179656 | tf_op jit(solution)/shard_map/ppermute | solution.py:24
  99.7 12.0 %collective-permute-start.23 = (bf16[96,2048]{1,0:T(8,128)(2,1)S(1)}, bf16[96,2048]{1,0:T(8,128)(2,1)S(1)}, u32[]{:S(2)}, u32[]{:S(2)}) collective-permute-start(bf16[96,2048]{1,0:T(8,128)(2,1)S(1)} %add_convert_fusion.3), channel_id=1, source_target_pairs={{0,8},{4,12},{8,0},{12,4},{1,9},{5,13},{9,1},{13,5},{2,10},{6,14},... | collective-permute-start | bytes 1179656 | tf_op jit(solution)/shard_map/ppermute | solution.py:24
  101.3 20.2 %collective-permute-start.20 = (bf16[192,2048]{1,0:T(8,128)(2,1)S(1)}, bf16[192,2048]{1,0:T(8,128)(2,1)S(1)}, u32[]{:S(2)}, u32[]{:S(2)}) collective-permute-start(bf16[192,2048]{1,0:T(8,128)(2,1)S(1)} %get-tuple-element.60), channel_id=1, source_target_pairs={{0,4},{4,0},{8,12},{12,8},{1,5},{5,1},{9,13},{13,9},{2,6},{6,2},{1... | collective-permute-start | bytes 2359304 | tf_op jit(solution)/shard_map/ppermute | solution.py:24
  103.3 24.7 %collective-permute-start.21 = (bf16[192,2048]{1,0:T(8,128)(2,1)S(1)}, bf16[192,2048]{1,0:T(8,128)(2,1)S(1)}, u32[]{:S(2)}, u32[]{:S(2)}) collective-permute-start(bf16[192,2048]{1,0:T(8,128)(2,1)S(1)} %add_convert_fusion.1), channel_id=1, source_target_pairs={{0,8},{4,12},{8,0},{12,4},{1,9},{5,13},{9,1},{13,5},{2,10},{6,14},... | collective-permute-start | bytes 2359304 | tf_op jit(solution)/shard_map/ppermute | solution.py:24
  107.4 10.2 %collective-permute-start.16 = (bf16[128,1024]{1,0:T(8,128)(2,1)S(1)}, bf16[128,1024]{1,0:T(8,128)(2,1)S(1)}, u32[]{:S(2)}, u32[]{:S(2)}) collective-permute-start(bf16[128,1024]{1,0:T(8,128)(2,1)S(1)} %get-tuple-element.65), channel_id=1, source_target_pairs={{0,1},{1,3},{3,2},{2,0},{4,5},{5,7},{7,6},{6,4},{8,9},{9,11},{11,1... | collective-permute-start | bytes 786440 | tf_op jit(solution)/shard_map/ppermute | solution.py:20
  108.3 12.2 %collective-permute-start.19 = (bf16[128,1024]{1,0:T(8,128)(2,1)S(1)}, bf16[128,1024]{1,0:T(8,128)(2,1)S(1)}, u32[]{:S(2)}, u32[]{:S(2)}) collective-permute-start(bf16[128,1024]{1,0:T(8,128)(2,1)S(1)} %get-tuple-element.66), channel_id=1, source_target_pairs={{0,1},{1,3},{3,2},{2,0},{4,5},{5,7},{7,6},{6,4},{8,9},{9,11},{11,1... | collective-permute-start | bytes 786440 | tf_op jit(solution)/shard_map/ppermute | solution.py:20

commit v3 on v2

--- a/solution.py
+++ b/solution.py
@@ -1,4 +1,5 @@
 import functools
+import math
 
 import jax
 import jax.numpy as jnp
@@ -33,18 +34,6 @@
     for bit in bits_of(lax.axis_size("expert"))[::-1]:
         held.update({k | bit: swapped(v, bit) for k, v in list(held.items())})
     return [held[k] for k in range(len(held))]
-
-
-def summed_to_owner(terms):
-    left, sent = dict(enumerate(terms)), None
-    for bit in bits_of(len(terms)):
-        stay = [k for k in left if not k & bit]
-        got = {k: swapped(left[k | bit], bit) for k in stay[::-1]}
-        left = {k: left[k].astype(F32) + got[k].astype(F32) for k in stay}
-        if len(left) > 1:
-            left = {k: v.astype(BF16) for k, v in left.items()}
-            sent = left[max(left)]
-    return left[0], sent
 
 
 def call(kernel, outs, *args, flops=0, scratch=()):
@@ -101,35 +90,91 @@
         contrib[:, cols] = total.astype(BF16)
 
 
-def put_weight_grads(ks, xs, dys, both, hid, gate_up, down):
-    wide, width = down[0].shape
-    count = xs[0].shape[0]
-    step = min(512, width)
-    for n, k in enumerate(ks):
-        for acts, rows, out, size in ((hid, dys, down[n], wide), (both, xs, gate_up[n], 2 * wide)):
-            left = jnp.concatenate([a[k * size : (k + 1) * size, :] for a in acts], axis=1)
-            for at in range(0, width, step):
-                cols = slice(at, at + step)
-                right = jnp.concatenate([r[:count, cols] for r in rows], axis=0)
-                out[:, cols] = dot_nn(left, right).astype(BF16)
-
-
-def weights_of(dyp, experts, rows):
-    width = dyp.shape[1]
-    per = width // rows
-    packed = dyp[rows:, :].astype(F32)
+def put_weight_grads(ks, split, xs, dys, both, hid, outs):
+    rows, width = xs[0].shape
+    block = dys[0].shape[1]
+    for k in ks:
+        mine, outs = (outs[:3], outs[3:]) if k in split else (outs[:1], outs[1:])
+        wide = sum(o.shape[0] for o in mine) // 3
+        left_x = jnp.concatenate([a[2 * k * wide : 2 * (k + 1) * wide, :] for a in both], axis=1)
+        left_dy = jnp.concatenate([a[k * wide : (k + 1) * wide, :] for a in hid], axis=1)
+        for n in range(width // block):
+            cols = slice(n * block, (n + 1) * block)
+            right_x = jnp.concatenate([x[:, cols] for x in xs], axis=0)
+            right_dy = jnp.concatenate([dy[n * rows : (n + 1) * rows, :] for dy in dys], axis=0)
+            got_x = dot_nn(left_x, right_x).astype(BF16)
+            got_dy = dot_nn(left_dy, right_dy).astype(BF16)
+            if len(mine) == 1:
+                mine[0][: 2 * wide, cols] = got_x
+                mine[0][2 * wide :, cols] = got_dy
+            else:
+                mine[0][:, cols] = got_x[:wide]
+                mine[1][:, cols] = got_x[wide:]
+                mine[2][:, cols] = got_dy
+
+
+def sum_kernel(counts, *refs):
+    parts, outs = [], refs[sum(counts) :]
+    for count in counts:
+        parts.append(refs[:count])
+        refs = refs[count:]
+    size = math.gcd(*(r.shape[0] for part in (*parts, outs) for r in part))
+
+    def rows_at(part, at):
+        for ref in part:
+            if at < ref.shape[0]:
+                return ref, slice(at, at + size)
+            at -= ref.shape[0]
+
+    for at in range(0, sum(r.shape[0] for r in outs), size):
+        total = None
+        for part in parts:
+            ref, rows = rows_at(part, at)
+            term = ref[rows, :].astype(F32)
+            total = term if total is None else total + term
+        ref, rows = rows_at(outs, at)
+        ref[rows, :] = total.astype(ref.dtype)
+
+
+def summed(addends, outs):
+    counts = tuple(len(a) for a in addends)
+    return call(functools.partial(sum_kernel, counts), outs, *(r for a in addends for r in a))
+
+
+def travelling(dy, prob):
+    rows, width = dy.shape
+    block = 2 * rows if width % (2 * rows) == 0 else width
+    stacked = dy.reshape(rows, width // block, block).transpose(1, 0, 2).reshape(-1, block)
+    below = -(-prob.size // (16 * block)) * 16
+    packed = jnp.zeros((below * block,), BF16).at[: prob.size].set(prob.reshape(-1))
+    return jnp.concatenate([stacked, packed.reshape(below, block)])
+
+
+def weights_of(dyp, experts, rows, width):
+    block = dyp.shape[1]
+    per = block // rows
+    packed = dyp[width // block * rows :, :].astype(F32)
     return [
         packed[k // per : k // per + 1, k % per * rows : (k % per + 1) * rows] for k in range(experts)
     ]
 
 
+def back_of(down, dyp, rows):
+    block = dyp.shape[1]
+    total = None
+    for n in range(down.shape[1] // block):
+        term = dot_nt(down[:, n * block : (n + 1) * block], dyp[n * rows : (n + 1) * rows, :])
+        total = term if total is None else total + term
+    return total
+
+
 def slab_kernel(experts, *refs):
     (x, dyp), gate_up, down, (both, hid, contrib) = spread(refs, 2, experts, experts)
     rows, wide = x.shape[0], down[0].shape[0]
-    weights = weights_of(dyp, experts, rows)
+    weights = weights_of(dyp, experts, rows, x.shape[1])
     for k in range(experts):
         acts = dot_nt(gate_up[k][...], x[...])
-        back = dot_nt(down[k][...], dyp[:rows, :])
+        back = back_of(down[k], dyp, rows)
         gate_grad, up_grad, weighted = grads_of(acts[:wide], acts[wide:], back, weights[k])
         both[2 * k * wide : (2 * k + 1) * wide, :] = gate_grad
         both[(2 * k + 1) * wide : (2 * k + 2) * wide, :] = up_grad
@@ -144,28 +189,28 @@
         acts[2 * k * wide : 2 * (k + 1) * wide, :] = dot_nt(gate_up[k][...], x[...])
 
 
-def far_kernel(experts, slabs, ks, *refs):
+def far_kernel(experts, slabs, ks, split, *refs):
     (acts,), down, xs, dys, both, hid, outs = spread(
         refs, 1, experts, slabs, slabs, slabs - 1, slabs - 1
     )
-    (last, last_hid), out_gate_up, out_down, _ = spread(outs, 2, len(ks), len(ks))
+    (last, last_hid), grads = spread(outs, 2)
     rows, wide = xs[0].shape[0], down[0].shape[0]
-    weights = weights_of(dys[-1], experts, rows)
+    weights = weights_of(dys[-1], experts, rows, down[0].shape[1])
     for k in range(experts):
-        back = dot_nt(down[k][...], dys[-1][:rows, :])
+        back = back_of(down[k], dys[-1], rows)
         gate_act = acts[2 * k * wide : (2 * k + 1) * wide, :]
         up_act = acts[(2 * k + 1) * wide : (2 * k + 2) * wide, :]
         gate_grad, up_grad, weighted = grads_of(gate_act, up_act, back, weights[k])
         last[2 * k * wide : (2 * k + 1) * wide, :] = gate_grad
         last[(2 * k + 1) * wide : (2 * k + 2) * wide, :] = up_grad
         last_hid[k * wide : (k + 1) * wide, :] = weighted
-    put_weight_grads(ks, xs, dys, (*both, last), (*hid, last_hid), out_gate_up, out_down)
+    put_weight_grads(ks, split, xs, dys, (*both, last), (*hid, last_hid), grads)
 
 
 def near_kernel(experts, slabs, ks, *refs):
     gate_up, xs, dys, both, hid, outs = spread(refs, experts, slabs, slabs, slabs, slabs)
-    (contrib,), out_gate_up, out_down, _ = spread(outs, 1, len(ks), len(ks))
-    put_weight_grads(ks, xs, dys, both, hid, out_gate_up, out_down)
+    (contrib,), grads = spread(outs, 1)
+    put_weight_grads(ks, (), xs, dys, both, hid, grads)
     put_contrib(both[-1], gate_up, contrib)
 
 
@@ -188,12 +233,11 @@
     prob = jnp.sum(
         jnp.where(route_ids[None] == names[:, None, None], route_probs[None], 0), axis=2
     ).astype(BF16)
-    packed = jnp.zeros((-(-prob.size // (8 * width)) * 8 * width,), BF16).at[: prob.size].set(prob.reshape(-1))
-    xs, dys = [tokens], [jnp.concatenate([cotangent, packed.reshape(-1, width)])]
+    xs, dys = [tokens], [travelling(cotangent, prob)]
     for _ in range(turns - 1):
         xs.append(onward(xs[-1]))
         dys.append(onward(dys[-1]))
-    gate_up = all_experts(w_gate_up.reshape(2 * wide, width))
+    gate_up = all_experts(after(w_gate_up, prob).reshape(2 * wide, width))
     down = all_experts(w_down.reshape(wide, width))
 
     slabs, units = len(xs), experts * wide
@@ -218,9 +262,11 @@
 
     far = tuple(range(experts // 2, experts))[::-1]
     near = tuple(range(experts // 2))[::-1]
-    grads = [shape(2 * wide, width)] * len(far) + [shape(wide, width)] * len(far)
+    split = tuple(k for k in far if k % 2)
+    whole, third = shape(3 * wide, width), shape(wide, width)
+    grads = [piece for k in far for piece in ([third] * 3 if k in split else [whole])]
     b, h, *got_far = call(
-        functools.partial(far_kernel, experts, slabs, far),
+        functools.partial(far_kernel, experts, slabs, far, split),
         (shape(2 * units, rows), shape(units, rows), *grads),
         acts, *down, *xs, *dys, *both, *hid,
         flops=3 * slabs * unit_flops // 2 + unit_flops,
@@ -229,27 +275,37 @@
     hid.append(h)
     c, *got_near = call(
         functools.partial(near_kernel, experts, slabs, near),
-        (shape(rows, width), *grads),
+        (shape(rows, width), *[whole] * len(near)),
         *gate_up, *xs, *dys, *both, *hid,
         flops=3 * slabs * unit_flops // 2 + 2 * unit_flops,
     )
     contrib.append(c)
-    terms_gate_up = dict(zip(far + near, got_far[: len(far)] + got_near[: len(near)]))
-    terms_down = dict(zip(far + near, got_far[len(far) :] + got_near[len(near) :]))
-    grad_down, sent_down = summed_to_owner([terms_down[k] for k in range(experts)])
-    grad_gate_up, sent_gate_up = summed_to_owner([terms_gate_up[k] for k in range(experts)])
-
-    half = width // 2
-    done = []
-    for cols in (slice(0, half), slice(half, width)):
-        part = onward(after(contrib[1 % slabs][:, cols], xs[-1]))
-        part = after(part, sent_gate_up, sent_down)
-        for i in range(2, slabs + 1):
-            if i > 2:
-                part = onward(part)
-            part = (part.astype(F32) + contrib[i % slabs][:, cols].astype(F32)).astype(BF16)
-        done.append(part)
-    acc = jnp.concatenate(done, axis=1)
+    terms = {k: [(got,)] for k, got in zip(near, got_near)}
+    for k in far:
+        count = 3 if k in split else 1
+        terms[k], got_far = [tuple(got_far[:count])], got_far[count:]
+
+    total = contrib[0].astype(F32)
+    if slabs > 1:
+        total = total + onward(after(contrib[1], both[-1]), -1).astype(F32)
+    acc = None
+    if slabs > 2:
+        acc = onward(after(contrib[2], acts, *both[:-1]))
+    for bit in bits_of(experts):
+        for k in sorted((k for k in terms if k & bit), reverse=True):
+            out = terms.pop(k)
+            if len(out) > 1:
+                out = [summed(out, [whole])]
+                if bit == 2 and acc is not None:
+                    acc = after(acc, *out[0])
+            terms[k ^ bit].append(tuple(swapped(v, bit) for v in out[0]))
+    grad_gate_up, grad_down = summed(terms[0], [shape(2 * wide, width, F32), shape(wide, width, F32)])
+
+    for i in range(3, slabs):
+        acc = onward((acc.astype(F32) + contrib[i].astype(F32)).astype(BF16))
+    if slabs > 2:
+        total = total + acc.astype(F32)
+    acc = total.astype(BF16)
     return acc, grad_gate_up.reshape(1, 2, wide, width), grad_down.reshape(1, wide, width)
 
 

time: 130 us -> 112 us (0.86)
  waiting for transfers between devices: 79.6 us -> 61.9 us
  other arithmetic: 5.08 us -> 1.96 us
  Pallas kernels: 12.1 us -> 14.3 us
  starting transfers between devices: 30.8 us -> 32.3 us
    ppermute x12 -> x9, waiting for transfers between devices: 72.4 us -> 56 us  [onward(): return lax.ppermute(block, 'dp', ring_pairs(lax.axis_size('dp'), turns))]
    ppermute x12 -> x9, starting transfers between devices: 23.2 us -> 26.3 us  [onward(): return lax.ppermute(block, 'dp', ring_pairs(lax.axis_size('dp'), turns))]
    pallas_call x6 -> x8, Pallas kernels: 12.1 us -> 14.3 us  [call(): pl.pallas_call(kernel, out_shape=list(outs), in_specs=[pl.BlockSpec(memor...]
    ppermute x12 -> x11, starting transfers between devices: 7.6 us -> 6.01 us  [swapped(): lax.ppermute(block, 'expert', [(i, i ^ bit) for i in range(lax.axis_size(...]
    add x1 -> x0, other arithmetic: 1.54 us -> none  [summed_to_owner(): left = {k: left[k].astype(F32) + got[k].astype(F32) for k in stay}]
    ppermute x12 -> x11, waiting for transfers between devices: 7.16 us -> 5.89 us  [swapped(): lax.ppermute(block, 'expert', [(i, i ^ bit) for i in range(lax.axis_size(...]
  transfers between devices with their start and end apart: 24 -> 20, of which waited for: 14 -> 10; matrix products, arithmetic and copies ran while one was open for 3% -> 3% of each run, Pallas kernels for 8% -> 11%
where the time goes in v3:
time: 112 us
  waiting for transfers between devices  61.9 us (55%)
  starting transfers between devices  32.3 us (29%)
  Pallas kernels  14.3 us (13%)
  other arithmetic  1.96 us (2%)
    ppermute x9, waiting for transfers between devices, onward(): return lax.ppermute(block, 'dp', ring_pairs(lax.axis_size('dp'), turns))  56 us
    ppermute x9, starting transfers between devices, onward(): return lax.ppermute(block, 'dp', ring_pairs(lax.axis_size('dp'), turns))  26.3 us
    pallas_call x8, Pallas kernels, call(): pl.pallas_call(kernel, out_shape=list(outs), in_specs=[pl.BlockSpec(memor...  14.3 us
    ppermute x11, starting transfers between devices, swapped(): lax.ppermute(block, 'expert', [(i, i ^ bit) for i in range(lax.axis_size(...  6.01 us
    ppermute x11, waiting for transfers between devices, swapped(): lax.ppermute(block, 'expert', [(i, i ^ bit) for i in range(lax.axis_size(...  5.89 us
  transfers between devices with their start and end apart: 20, of which 10 were waited for; matrix products, arithmetic and copies ran while one was open for 3% of the time, Pallas kernels for 11%

profile of v3, /device:TPU:0, one launch (start us, length us, event | category | flops | bytes accessed | tf_op | source)
XLA Modules:
  0.0 112.3 jit_solution(3275497111813287443)
XLA Ops:
  0.6 0.0 copy-start
  0.6 0.0 copy-start.1
  0.7 3.1 %collective-permute-start.6 = (bf16[128,2048]{1,0:T(8,128)(2,1)}, bf16[128,2048]{1,0:T(8,128)(2,1)S(1)}, u32[]{:S(2)}, u32[]{:S(2)}) collective-permute-start(bf16[128,2048]{1,0:T(8,128)(2,1)} %refs_4_.1), channel_id=1, source_target_pairs={{0,1},{1,3},{3,2},{2,0},{4,5},{5,7},{7,6},{6,4},{8,9},{9,11},{11,1... | collective-permute-start | bytes 1572872 | tf_op jit(solution)/shard_map/ppermute | solution.py:21
  3.7 0.8 fusion
  4.5 1.5 %collective-permute-start.1 = (bf16[192,2048]{1,0:T(8,128)(2,1)}, bf16[192,2048]{1,0:T(8,128)(2,1)S(1)}, u32[]{:S(2)}, u32[]{:S(2)}) collective-permute-start(bf16[192,2048]{1,0:T(8,128)(2,1)} %bitcast.12), channel_id=1, source_target_pairs={{0,8},{4,12},{8,0},{12,4},{1,9},{5,13},{9,1},{13,5},{2,10},{6,14},... | collective-permute-start | bytes 2359304 | tf_op jit(solution)/shard_map/ppermute | solution.py:25
  6.0 1.1 copy.15
  7.2 2.6 %collective-permute-start.7 = (bf16[1040,256]{1,0:T(8,128)(2,1)S(1)}, bf16[1040,256]{1,0:T(8,128)(2,1)S(1)}, u32[]{:S(2)}, u32[]{:S(2)}) collective-permute-start(bf16[1040,256]{1,0:T(8,128)(2,1)S(1)} %pad_maximum_fusion.refs_1_.refs_9_.refs_8_), channel_id=1, source_target_pairs={{0,1},{1,3},{3,2},{2,0},{4,5},{5,7},{7,6},{6,4},{8,9},{9,11},{11,1... | collective-permute-start | bytes 1597448 | tf_op jit(solution)/shard_map/ppermute | solution.py:21
  9.8 0.0 copy-done
  9.8 0.0 collective-permute-start
  9.8 7.9 %collective-permute-done.6.refs_0_.refs_6_.refs_5_ = bf16[128,2048]{1,0:T(8,128)(2,1)S(1)} collective-permute-done((bf16[128,2048]{1,0:T(8,128)(2,1)}, bf16[128,2048]{1,0:T(8,128)(2,1)S(1)}, u32[]{:S(2)}, u32[]{:S(2)}) %collective-permute-start.6) | collective-permute-done | bytes 524320 | tf_op jit(solution)/shard_map/ppermute | solution.py:21
  17.7 1.3 %collective-permute-start.8 = (bf16[128,2048]{1,0:T(8,128)(2,1)S(1)}, bf16[128,2048]{1,0:T(8,128)(2,1)S(1)}, u32[]{:S(2)}, u32[]{:S(2)}) collective-permute-start(bf16[128,2048]{1,0:T(8,128)(2,1)S(1)} %collective-permute-done.6.refs_0_.refs_6_.refs_5_), channel_id=1, source_target_pairs={{0,1},{1,3},{3,2},{2,0},{4,5},{5,7},{7,6},{6,4},{8,9},{9,11},{11,1... | collective-permute-start | bytes 1572872 | tf_op jit(solution)/shard_map/ppermute | solution.py:21
  19.0 4.7 %collective-permute-done.1.refs_4_.refs_3_.refs_2_ = bf16[192,2048]{1,0:T(8,128)(2,1)S(1)} collective-permute-done((bf16[192,2048]{1,0:T(8,128)(2,1)}, bf16[192,2048]{1,0:T(8,128)(2,1)S(1)}, u32[]{:S(2)}, u32[]{:S(2)}) %collective-permute-start.1) | collective-permute-done | bytes 786464 | tf_op jit(solution)/shard_map/ppermute | solution.py:25
  23.7 0.0 collective-permute-start.2
  23.7 0.0 copy-done.1
  23.7 1.5 %collective-permute-start.4 = (bf16[96,2048]{1,0:T(8,128)(2,1)S(1)}, bf16[96,2048]{1,0:T(8,128)(2,1)S(1)}, u32[]{:S(2)}, u32[]{:S(2)}) collective-permute-start(bf16[96,2048]{1,0:T(8,128)(2,1)S(1)} %bitcast.19), channel_id=1, source_target_pairs={{0,8},{4,12},{8,0},{12,4},{1,9},{5,13},{9,1},{13,5},{2,10},{6,14},... | collective-permute-start | bytes 1179656 | tf_op jit(solution)/shard_map/ppermute | solution.py:25
  25.2 3.9 %collective-permute-done.7.refs_1_.refs_10_.refs_9_ = bf16[1040,256]{1,0:T(8,128)(2,1)S(1)} collective-permute-done((bf16[1040,256]{1,0:T(8,128)(2,1)S(1)}, bf16[1040,256]{1,0:T(8,128)(2,1)S(1)}, u32[]{:S(2)}, u32[]{:S(2)}) %collective-permute-start.7) | collective-permute-done | bytes 532512 | tf_op jit(solution)/shard_map/ppermute | solution.py:21
  29.1 1.2 %collective-permute-start.10 = (bf16[1040,256]{1,0:T(8,128)(2,1)S(1)}, bf16[1040,256]{1,0:T(8,128)(2,1)S(1)}, u32[]{:S(2)}, u32[]{:S(2)}) collective-permute-start(bf16[1040,256]{1,0:T(8,128)(2,1)S(1)} %collective-permute-done.7.refs_1_.refs_10_.refs_9_), channel_id=1, source_target_pairs={{0,1},{1,3},{3,2},{2,0},{4,5},{5,7},{7,6},{6,4},{8,9},{9,11},{11,1... | collective-permute-start | bytes 1597448 | tf_op jit(solution)/shard_map/ppermute | solution.py:21
  30.3 10.1 %collective-permute-done.8.refs_0_.refs_7_.refs_6_ = bf16[128,2048]{1,0:T(8,128)(2,1)S(1)} collective-permute-done((bf16[128,2048]{1,0:T(8,128)(2,1)S(1)}, bf16[128,2048]{1,0:T(8,128)(2,1)S(1)}, u32[]{:S(2)}, u32[]{:S(2)}) %collective-permute-start.8) | collective-permute-done | bytes 524320 | tf_op jit(solution)/shard_map/ppermute | solution.py:21
  40.4 1.2 %collective-permute-start.9 = (bf16[128,2048]{1,0:T(8,128)(2,1)S(1)}, bf16[128,2048]{1,0:T(8,128)(2,1)S(1)}, u32[]{:S(2)}, u32[]{:S(2)}) collective-permute-start(bf16[128,2048]{1,0:T(8,128)(2,1)S(1)} %collective-permute-done.8.refs_0_.refs_7_.refs_6_), channel_id=1, source_target_pairs={{0,1},{1,3},{3,2},{2,0},{4,5},{5,7},{7,6},{6,4},{8,9},{9,11},{11,1... | collective-permute-start | bytes 1572872 | tf_op jit(solution)/shard_map/ppermute | solution.py:21
  41.5 0.0 collective-permute-done.4.refs_8_.refs_3_
  41.5 0.0 collective-permute-start.3
  41.5 0.0 collective-permute-done.refs_3_.refs_2_.refs_1_
  41.5 0.5 collective-permute-start.5
  42.0 9.7 %collective-permute-done.10.refs_1_.refs_11_.refs_10_ = bf16[1040,256]{1,0:T(8,128)(2,1)S(1)} collective-permute-done((bf16[1040,256]{1,0:T(8,128)(2,1)S(1)}, bf16[1040,256]{1,0:T(8,128)(2,1)S(1)}, u32[]{:S(2)}, u32[]{:S(2)}) %collective-permute-start.10) | collective-permute-done | bytes 532512 | tf_op jit(solution)/shard_map/ppermute | solution.py:21
  51.8 1.2 %collective-permute-start.11 = (bf16[1040,256]{1,0:T(8,128)(2,1)S(1)}, bf16[1040,256]{1,0:T(8,128)(2,1)S(1)}, u32[]{:S(2)}, u32[]{:S(2)}) collective-permute-start(bf16[1040,256]{1,0:T(8,128)(2,1)S(1)} %collective-permute-done.10.refs_1_.refs_11_.refs_10_), channel_id=1, source_target_pairs={{0,1},{1,3},{3,2},{2,0},{4,5},{5,7},{7,6},{6,4},{8,9},{9,11},{11,1... | collective-permute-start | bytes 1597448 | tf_op jit(solution)/shard_map/ppermute | solution.py:21
  52.9 10.1 %collective-permute-done.9.refs_0_.refs_8_.refs_7_ = bf16[128,2048]{1,0:T(8,128)(2,1)S(1)} collective-permute-done((bf16[128,2048]{1,0:T(8,128)(2,1)S(1)}, bf16[128,2048]{1,0:T(8,128)(2,1)S(1)}, u32[]{:S(2)}, u32[]{:S(2)}) %collective-permute-start.9) | collective-permute-done | bytes 524320 | tf_op jit(solution)/shard_map/ppermute | solution.py:21
  63.0 0.0 collective-permute-done.2.refs_5_.refs_4_.refs_3_
  63.0 1.0 shard_map.87.refs_0_
  64.0 0.0 collective-permute-done.3.refs_7_.refs_2_
  64.0 0.0 collective-permute-done.5.refs_9_.refs_4_
  64.0 2.2 %shard_map.88 = (bf16[768,128]{1,0:T(8,128)(2,1)S(1)}, bf16[384,128]{1,0:T(8,128)(2,1)S(1)}, bf16[128,2048]{1,0:T(8,128)(2,1)S(1)}) custom-call(bf16[128,2048]{1,0:T(8,128)(2,1)S(1)} %collective-permute-done.8.refs_0_.refs_7_.refs_6_, bf16[1040,256]{1,0:T(8,128)(2,1)S(1)} %collective-permute-done.10.refs_1_.refs_11_.refs_10_, ...), custom_call_target="tpu_custom_call" | custom-call | flops 1006632960 | bytes 6594560 | tf_op jit(solution)/shard_map/pallas_call | solution.py:41
  66.2 0.0 copy-start.2
  66.3 2.2 %shard_map.86 = (bf16[768,128]{1,0:T(8,128)(2,1)S(1)}, bf16[384,128]{1,0:T(8,128)(2,1)S(1)}, bf16[128,2048]{1,0:T(8,128)(2,1)S(1)}) custom-call(bf16[128,2048]{1,0:T(8,128)(2,1)S(1)} %collective-permute-done.6.refs_0_.refs_6_.refs_5_, bf16[1040,256]{1,0:T(8,128)(2,1)S(1)} %collective-permute-done.7.refs_1_.refs_10_.refs_9_, bf16[192,2048]{1,0:T(8,128)(2,1)S(1)} %bitcast.16, ...), custom_call_target="tpu_custom_call" | custom-call | flops 1006632960 | bytes 6594560 | tf_op jit(solution)/shard_map/pallas_call | solution.py:41
  68.5 0.0 copy-done.2
  68.5 2.2 %shard_map.85 = (bf16[768,128]{1,0:T(8,128)(2,1)S(1)}, bf16[384,128]{1,0:T(8,128)(2,1)S(1)}, bf16[128,2048]{1,0:T(8,128)(2,1)S(1)}) custom-call(bf16[128,2048]{1,0:T(8,128)(2,1)S(1)} %copy-done.2, bf16[1040,256]{1,0:T(8,128)(2,1)S(1)} %pad_maximum_fusion.refs_1_.refs_9_.refs_8_, bf16[192,2048]{1,0:T(8,128)(2,1)S(1)} %bitcast.17, ...), custom_call_target="tpu_custom_call" | custom-call | flops 1006632960 | bytes 6594560 | tf_op jit(solution)/shard_map/pallas_call | solution.py:41
  70.7 1.2 %collective-permute-start.13 = (bf16[128,2048]{1,0:T(8,128)(2,1)S(1)}, bf16[128,2048]{1,0:T(8,128)(2,1)S(1)}, u32[]{:S(2)}, u32[]{:S(2)}) collective-permute-start(bf16[128,2048]{1,0:T(8,128)(2,1)S(1)} %get-tuple-element.51), channel_id=1, source_target_pairs={{0,1},{1,3},{3,2},{2,0},{4,5},{5,7},{7,6},{6,4},{8,9},{9,11},{11,1... | collective-permute-start | bytes 1572872 | tf_op jit(solution)/shard_map/ppermute | solution.py:21
  71.9 2.5 %collective-permute-done.11.refs_12_.refs_11_ = bf16[1040,256]{1,0:T(8,128)(2,1)S(1)} collective-permute-done((bf16[1040,256]{1,0:T(8,128)(2,1)S(1)}, bf16[1040,256]{1,0:T(8,128)(2,1)S(1)}, u32[]{:S(2)}, u32[]{:S(2)}) %collective-permute-start.11) | collective-permute-done | bytes 532512 | tf_op jit(solution)/shard_map/ppermute | solution.py:21
  74.4 2.4 %shard_map.89 = (bf16[768,128]{1,0:T(8,128)(2,1)S(1)}, bf16[384,128]{1,0:T(8,128)(2,1)S(1)}, bf16[96,2048]{1,0:T(8,128)(2,1)S(1)}, bf16[96,2048]{1,0:T(8,128)(2,...) custom-call(f32[768,128]{1,0:T(8,128)S(1)} %shard_map.87.refs_0_, bf16[96,2048]{1,0:T(8,128)(2,1)S(1)} %bitcast.24, ...), custom_call_target="tpu_custom_call" | custom-call | flops 1409286144 | bytes 9732096 | tf_op jit(solution)/shard_map/pallas_call | solution.py:41
  76.8 0.1 collective-permute-start.14
  76.9 0.5 collective-permute-start.15
  77.4 0.1 collective-permute-start.16
  77.5 2.1 %collective-permute-start.12 = (bf16[128,2048]{1,0:T(8,128)(2,1)S(1)}, bf16[128,2048]{1,0:T(8,128)(2,1)S(1)}, u32[]{:S(2)}, u32[]{:S(2)}) collective-permute-start(bf16[128,2048]{1,0:T(8,128)(2,1)S(1)} %get-tuple-element.49), channel_id=1, source_target_pairs={{0,2},{1,0},{3,1},{2,3},{4,6},{5,4},{7,5},{6,7},{8,10},{9,8},{11,9... | collective-permute-start | bytes 1572872 | tf_op jit(solution)/shard_map/ppermute | solution.py:21
  79.5 2.3 %shard_map.91 = (bf16[128,2048]{1,0:T(8,128)(2,1)S(1)}, bf16[288,2048]{1,0:T(8,128)(2,1)S(1)}, bf16[288,2048]{1,0:T(8,128)(2,1)S(1)}) custom-call(bf16[192,2048]{1,0:T(8,128)(2,1)S(1)} %bitcast.18, bf16[192,2048]{1,0:T(8,128)(2,1)S(1)} %collective-permute-done.refs_3_.refs_2_.refs_1_, bf16[192,2048]{1,0:T(8,128)(2,1)S(1)} %collective-permute-done.1.refs_4_.refs_3_.refs_2_, ...), custom_call_target="tpu_custom_call" | custom-call | flops 1610612736 | bytes 11436032 | tf_op jit(solution)/shard_map/pallas_call | solution.py:41
  81.8 0.0 collective-permute-done.14.refs_1_
  81.8 0.2 collective-permute-start.18
  82.1 0.0 collective-permute-done.15.refs_2_
  82.1 0.0 collective-permute-done.16.refs_3_
  82.1 0.3 shard_map.90
  82.3 1.6 %collective-permute-start.19 = (bf16[288,2048]{1,0:T(8,128)(2,1)S(1)}, bf16[288,2048]{1,0:T(8,128)(2,1)S(1)}, u32[]{:S(2)}, u32[]{:S(2)}) collective-permute-start(bf16[288,2048]{1,0:T(8,128)(2,1)S(1)} %shard_map.90), channel_id=1, source_target_pairs={{0,8},{4,12},{8,0},{12,4},{1,9},{5,13},{9,1},{13,5},{2,10},{6,14},... | collective-permute-start | bytes 3538952 | tf_op jit(solution)/shard_map/ppermute | solution.py:25
  83.9 1.4 %collective-permute-done.13 = bf16[128,2048]{1,0:T(8,128)(2,1)S(1)} collective-permute-done((bf16[128,2048]{1,0:T(8,128)(2,1)S(1)}, bf16[128,2048]{1,0:T(8,128)(2,1)S(1)}, u32[]{:S(2)}, u32[]{:S(2)}) %collective-permute-start.13) | collective-permute-done | bytes 524320 | tf_op jit(solution)/shard_map/ppermute | solution.py:21
  85.3 0.1 add_convert_fusion.1
  85.5 12.6 %collective-permute-start.17 = (bf16[128,2048]{1,0:T(8,128)(2,1)S(1)}, bf16[128,2048]{1,0:T(8,128)(2,1)S(1)}, u32[]{:S(2)}, u32[]{:S(2)}) collective-permute-start(bf16[128,2048]{1,0:T(8,128)(2,1)S(1)} %add_convert_fusion.1), channel_id=1, source_target_pairs={{0,1},{1,3},{3,2},{2,0},{4,5},{5,7},{7,6},{6,4},{8,9},{9,11},{11,1... | collective-permute-start | bytes 1572872 | tf_op jit(solution)/shard_map/ppermute | solution.py:21
  98.1 0.0 collective-permute-done.12
  98.1 10.4 %collective-permute-done.17 = bf16[128,2048]{1,0:T(8,128)(2,1)S(1)} collective-permute-done((bf16[128,2048]{1,0:T(8,128)(2,1)S(1)}, bf16[128,2048]{1,0:T(8,128)(2,1)S(1)}, u32[]{:S(2)}, u32[]{:S(2)}) %collective-permute-start.17) | collective-permute-done | bytes 524320 | tf_op jit(solution)/shard_map/ppermute | solution.py:21
  108.5 1.0 add_convert_fusion
  109.5 0.0 collective-permute-done.18.refs_1_
  109.5 1.1 %collective-permute-done.19.refs_2_ = bf16[288,2048]{1,0:T(8,128)(2,1)S(1)} collective-permute-done((bf16[288,2048]{1,0:T(8,128)(2,1)S(1)}, bf16[288,2048]{1,0:T(8,128)(2,1)S(1)}, u32[]{:S(2)}, u32[]{:S(2)}) %collective-permute-start.19) | collective-permute-done | bytes 1179680 | tf_op jit(solution)/shard_map/ppermute | solution.py:25
  110.6 1.7 %shard_map.92 = (f32[192,2048]{1,0:T(8,128)}, f32[96,2048]{1,0:T(8,128)}) custom-call(bf16[288,2048]{1,0:T(8,128)(2,1)S(1)} %get-tuple-element.59.refs_0_, bf16[288,2048]{1,0:T(8,128)(2,1)S(1)} %collective-permute-done.18.refs_1_, bf16[288,2048]{1,0:T(8,128)(2,1)S(1)} %collective-permute-done.19.refs_2_), custom_call_target="tpu_custom_call" | custom-call | bytes 5898240 | tf_op jit(solution)/shard_map/pallas_call | solution.py:41
  (4 shorter events, 0.1 us)
Async XLA Ops:
  0.6 9.2 %copy-start = (bf16[1,2,96,2048]{3,2,1,0:T(8,128)(2,1)S(1)}, bf16[1,2,96,2048]{3,2,1,0:T(8,128)(2,1)}, u32[]{:S(2)}) copy-start(bf16[1,2,96,2048]{3,2,1,0:T(8,128)(2,1)} %param.12) | copy-start | bytes 2359300
  0.6 23.1 %copy-start.1 = (bf16[1,96,2048]{2,1,0:T(8,128)(2,1)S(1)}, bf16[1,96,2048]{2,1,0:T(8,128)(2,1)}, u32[]{:S(2)}) copy-start(bf16[1,96,2048]{2,1,0:T(8,128)(2,1)} %param.13) | copy-start | bytes 1179652
  0.7 17.1 %collective-permute-start.6 = (bf16[128,2048]{1,0:T(8,128)(2,1)}, bf16[128,2048]{1,0:T(8,128)(2,1)S(1)}, u32[]{:S(2)}, u32[]{:S(2)}) collective-permute-start(bf16[128,2048]{1,0:T(8,128)(2,1)} %refs_4_.1), channel_id=1, source_target_pairs={{0,1},{1,3},{3,2},{2,0},{4,5},{5,7},{7,6},{6,4},{8,9},{9,11},{11,1... | collective-permute-start | bytes 1572872 | tf_op jit(solution)/shard_map/ppermute | solution.py:21
  4.5 19.2 %collective-permute-start.1 = (bf16[192,2048]{1,0:T(8,128)(2,1)}, bf16[192,2048]{1,0:T(8,128)(2,1)S(1)}, u32[]{:S(2)}, u32[]{:S(2)}) collective-permute-start(bf16[192,2048]{1,0:T(8,128)(2,1)} %bitcast.12), channel_id=1, source_target_pairs={{0,8},{4,12},{8,0},{12,4},{1,9},{5,13},{9,1},{13,5},{2,10},{6,14},... | collective-permute-start | bytes 2359304 | tf_op jit(solution)/shard_map/ppermute | solution.py:25
  7.2 22.0 %collective-permute-start.7 = (bf16[1040,256]{1,0:T(8,128)(2,1)S(1)}, bf16[1040,256]{1,0:T(8,128)(2,1)S(1)}, u32[]{:S(2)}, u32[]{:S(2)}) collective-permute-start(bf16[1040,256]{1,0:T(8,128)(2,1)S(1)} %pad_maximum_fusion.refs_1_.refs_9_.refs_8_), channel_id=1, source_target_pairs={{0,1},{1,3},{3,2},{2,0},{4,5},{5,7},{7,6},{6,4},{8,9},{9,11},{11,1... | collective-permute-start | bytes 1597448 | tf_op jit(solution)/shard_map/ppermute | solution.py:21
  9.8 31.7 %collective-permute-start = (bf16[192,2048]{1,0:T(8,128)(2,1)S(1)}, bf16[192,2048]{1,0:T(8,128)(2,1)S(1)}, u32[]{:S(2)}, u32[]{:S(2)}) collective-permute-start(bf16[192,2048]{1,0:T(8,128)(2,1)S(1)} %bitcast.13), channel_id=1, source_target_pairs={{0,4},{4,0},{8,12},{12,8},{1,5},{5,1},{9,13},{13,9},{2,6},{6,2},{1... | collective-permute-start | bytes 2359304 | tf_op jit(solution)/shard_map/ppermute | solution.py:25
  17.7 22.6 %collective-permute-start.8 = (bf16[128,2048]{1,0:T(8,128)(2,1)S(1)}, bf16[128,2048]{1,0:T(8,128)(2,1)S(1)}, u32[]{:S(2)}, u32[]{:S(2)}) collective-permute-start(bf16[128,2048]{1,0:T(8,128)(2,1)S(1)} %collective-permute-done.6.refs_0_.refs_6_.refs_5_), channel_id=1, source_target_pairs={{0,1},{1,3},{3,2},{2,0},{4,5},{5,7},{7,6},{6,4},{8,9},{9,11},{11,1... | collective-permute-start | bytes 1572872 | tf_op jit(solution)/shard_map/ppermute | solution.py:21
  23.7 39.3 %collective-permute-start.2 = (bf16[192,2048]{1,0:T(8,128)(2,1)S(1)}, bf16[192,2048]{1,0:T(8,128)(2,1)S(1)}, u32[]{:S(2)}, u32[]{:S(2)}) collective-permute-start(bf16[192,2048]{1,0:T(8,128)(2,1)S(1)} %collective-permute-done.1.refs_4_.refs_3_.refs_2_), channel_id=1, source_target_pairs={{0,4},{4,0},{8,12},{12,8},{1,5},{5,1},{9,13},{13,9},{2,6},{6,2},{1... | collective-permute-start | bytes 2359304 | tf_op jit(solution)/shard_map/ppermute | solution.py:25
  23.7 17.8 %collective-permute-start.4 = (bf16[96,2048]{1,0:T(8,128)(2,1)S(1)}, bf16[96,2048]{1,0:T(8,128)(2,1)S(1)}, u32[]{:S(2)}, u32[]{:S(2)}) collective-permute-start(bf16[96,2048]{1,0:T(8,128)(2,1)S(1)} %bitcast.19), channel_id=1, source_target_pairs={{0,8},{4,12},{8,0},{12,4},{1,9},{5,13},{9,1},{13,5},{2,10},{6,14},... | collective-permute-start | bytes 1179656 | tf_op jit(solution)/shard_map/ppermute | solution.py:25
  29.1 22.6 %collective-permute-start.10 = (bf16[1040,256]{1,0:T(8,128)(2,1)S(1)}, bf16[1040,256]{1,0:T(8,128)(2,1)S(1)}, u32[]{:S(2)}, u32[]{:S(2)}) collective-permute-start(bf16[1040,256]{1,0:T(8,128)(2,1)S(1)} %collective-permute-done.7.refs_1_.refs_10_.refs_9_), channel_id=1, source_target_pairs={{0,1},{1,3},{3,2},{2,0},{4,5},{5,7},{7,6},{6,4},{8,9},{9,11},{11,1... | collective-permute-start | bytes 1597448 | tf_op jit(solution)/shard_map/ppermute | solution.py:21
  40.4 22.6 %collective-permute-start.9 = (bf16[128,2048]{1,0:T(8,128)(2,1)S(1)}, bf16[128,2048]{1,0:T(8,128)(2,1)S(1)}, u32[]{:S(2)}, u32[]{:S(2)}) collective-permute-start(bf16[128,2048]{1,0:T(8,128)(2,1)S(1)} %collective-permute-done.8.refs_0_.refs_7_.refs_6_), channel_id=1, source_target_pairs={{0,1},{1,3},{3,2},{2,0},{4,5},{5,7},{7,6},{6,4},{8,9},{9,11},{11,1... | collective-permute-start | bytes 1572872 | tf_op jit(solution)/shard_map/ppermute | solution.py:21
  41.5 22.5 %collective-permute-start.3 = (bf16[96,2048]{1,0:T(8,128)(2,1)S(1)}, bf16[96,2048]{1,0:T(8,128)(2,1)S(1)}, u32[]{:S(2)}, u32[]{:S(2)}) collective-permute-start(bf16[96,2048]{1,0:T(8,128)(2,1)S(1)} %bitcast.20), channel_id=1, source_target_pairs={{0,4},{4,0},{8,12},{12,8},{1,5},{5,1},{9,13},{13,9},{2,6},{6,2},{1... | collective-permute-start | bytes 1179656 | tf_op jit(solution)/shard_map/ppermute | solution.py:25
  41.5 22.5 %collective-permute-start.5 = (bf16[96,2048]{1,0:T(8,128)(2,1)S(1)}, bf16[96,2048]{1,0:T(8,128)(2,1)S(1)}, u32[]{:S(2)}, u32[]{:S(2)}) collective-permute-start(bf16[96,2048]{1,0:T(8,128)(2,1)S(1)} %collective-permute-done.4.refs_8_.refs_3_), channel_id=1, source_target_pairs={{0,4},{4,0},{8,12},{12,8},{1,5},{5,1},{9,13},{13,9},{2,6},{6,2},{1... | collective-permute-start | bytes 1179656 | tf_op jit(solution)/shard_map/ppermute | solution.py:25
  51.8 22.6 %collective-permute-start.11 = (bf16[1040,256]{1,0:T(8,128)(2,1)S(1)}, bf16[1040,256]{1,0:T(8,128)(2,1)S(1)}, u32[]{:S(2)}, u32[]{:S(2)}) collective-permute-start(bf16[1040,256]{1,0:T(8,128)(2,1)S(1)} %collective-permute-done.10.refs_1_.refs_11_.refs_10_), channel_id=1, source_target_pairs={{0,1},{1,3},{3,2},{2,0},{4,5},{5,7},{7,6},{6,4},{8,9},{9,11},{11,1... | collective-permute-start | bytes 1597448 | tf_op jit(solution)/shard_map/ppermute | solution.py:21
  66.2 2.2 %copy-start.2 = (bf16[128,2048]{1,0:T(8,128)(2,1)S(1)}, bf16[128,2048]{1,0:T(8,128)(2,1)}, u32[]{:S(2)}) copy-start(bf16[128,2048]{1,0:T(8,128)(2,1)} %refs_4_.1) | copy-start | bytes 1572868
  70.7 14.6 %collective-permute-start.13 = (bf16[128,2048]{1,0:T(8,128)(2,1)S(1)}, bf16[128,2048]{1,0:T(8,128)(2,1)S(1)}, u32[]{:S(2)}, u32[]{:S(2)}) collective-permute-start(bf16[128,2048]{1,0:T(8,128)(2,1)S(1)} %get-tuple-element.51), channel_id=1, source_target_pairs={{0,1},{1,3},{3,2},{2,0},{4,5},{5,7},{7,6},{6,4},{8,9},{9,11},{11,1... | collective-permute-start | bytes 1572872 | tf_op jit(solution)/shard_map/ppermute | solution.py:21
  76.8 5.0 %collective-permute-start.14 = (bf16[96,2048]{1,0:T(8,128)(2,1)S(1)}, bf16[96,2048]{1,0:T(8,128)(2,1)S(1)}, u32[]{:S(2)}, u32[]{:S(2)}) collective-permute-start(bf16[96,2048]{1,0:T(8,128)(2,1)S(1)} %get-tuple-element.53), channel_id=1, source_target_pairs={{0,4},{4,0},{8,12},{12,8},{1,5},{5,1},{9,13},{13,9},{2,6},{6,2},{1... | collective-permute-start | bytes 1179656 | tf_op jit(solution)/shard_map/ppermute | solution.py:25
  76.9 5.2 %collective-permute-start.15 = (bf16[96,2048]{1,0:T(8,128)(2,1)S(1)}, bf16[96,2048]{1,0:T(8,128)(2,1)S(1)}, u32[]{:S(2)}, u32[]{:S(2)}) collective-permute-start(bf16[96,2048]{1,0:T(8,128)(2,1)S(1)} %get-tuple-element.54), channel_id=1, source_target_pairs={{0,4},{4,0},{8,12},{12,8},{1,5},{5,1},{9,13},{13,9},{2,6},{6,2},{1... | collective-permute-start | bytes 1179656 | tf_op jit(solution)/shard_map/ppermute | solution.py:25
  77.4 4.7 %collective-permute-start.16 = (bf16[96,2048]{1,0:T(8,128)(2,1)S(1)}, bf16[96,2048]{1,0:T(8,128)(2,1)S(1)}, u32[]{:S(2)}, u32[]{:S(2)}) collective-permute-start(bf16[96,2048]{1,0:T(8,128)(2,1)S(1)} %get-tuple-element.55), channel_id=1, source_target_pairs={{0,4},{4,0},{8,12},{12,8},{1,5},{5,1},{9,13},{13,9},{2,6},{6,2},{1... | collective-permute-start | bytes 1179656 | tf_op jit(solution)/shard_map/ppermute | solution.py:25
  77.5 20.6 %collective-permute-start.12 = (bf16[128,2048]{1,0:T(8,128)(2,1)S(1)}, bf16[128,2048]{1,0:T(8,128)(2,1)S(1)}, u32[]{:S(2)}, u32[]{:S(2)}) collective-permute-start(bf16[128,2048]{1,0:T(8,128)(2,1)S(1)} %get-tuple-element.49), channel_id=1, source_target_pairs={{0,2},{1,0},{3,1},{2,3},{4,6},{5,4},{7,5},{6,7},{8,10},{9,8},{11,9... | collective-permute-start | bytes 1572872 | tf_op jit(solution)/shard_map/ppermute | solution.py:21
  81.8 27.7 %collective-permute-start.18 = (bf16[288,2048]{1,0:T(8,128)(2,1)S(1)}, bf16[288,2048]{1,0:T(8,128)(2,1)S(1)}, u32[]{:S(2)}, u32[]{:S(2)}) collective-permute-start(bf16[288,2048]{1,0:T(8,128)(2,1)S(1)} %get-tuple-element.60), channel_id=1, source_target_pairs={{0,4},{4,0},{8,12},{12,8},{1,5},{5,1},{9,13},{13,9},{2,6},{6,2},{1... | collective-permute-start | bytes 3538952 | tf_op jit(solution)/shard_map/ppermute | solution.py:25
  82.3 28.3 %collective-permute-start.19 = (bf16[288,2048]{1,0:T(8,128)(2,1)S(1)}, bf16[288,2048]{1,0:T(8,128)(2,1)S(1)}, u32[]{:S(2)}, u32[]{:S(2)}) collective-permute-start(bf16[288,2048]{1,0:T(8,128)(2,1)S(1)} %shard_map.90), channel_id=1, source_target_pairs={{0,8},{4,12},{8,0},{12,4},{1,9},{5,13},{9,1},{13,5},{2,10},{6,14},... | collective-permute-start | bytes 3538952 | tf_op jit(solution)/shard_map/ppermute | solution.py:25
  85.5 23.0 %collective-permute-start.17 = (bf16[128,2048]{1,0:T(8,128)(2,1)S(1)}, bf16[128,2048]{1,0:T(8,128)(2,1)S(1)}, u32[]{:S(2)}, u32[]{:S(2)}) collective-permute-start(bf16[128,2048]{1,0:T(8,128)(2,1)S(1)} %add_convert_fusion.1), channel_id=1, source_target_pairs={{0,1},{1,3},{3,2},{2,0},{4,5},{5,7},{7,6},{6,4},{8,9},{9,11},{11,1... | collective-permute-start | bytes 1572872 | tf_op jit(solution)/shard_map/ppermute | solution.py:21

commit v4 on v3

--- a/solution.py
+++ b/solution.py
@@ -9,6 +9,7 @@
 from jax.sharding import PartitionSpec as P
 
 BF16 = jnp.bfloat16
+COSTS = {"slab": 2, "acts": 4, "far": 1, "even": 5, "near": 2, "join": 1, "tokens": 4, "last": 2}
 F32 = jnp.float32
 
 
@@ -36,8 +37,7 @@
     return [held[k] for k in range(len(held))]
 
 
-def call(kernel, outs, *args, flops=0, scratch=()):
-    total = sum(a.size * a.dtype.itemsize for a in (*args, *outs))
+def call(kernel, outs, *args, cost=0.0, scratch=()):
     return pl.pallas_call(
         kernel,
         out_shape=list(outs),
@@ -45,7 +45,7 @@
         out_specs=[pl.BlockSpec(memory_space=pltpu.VMEM)] * len(outs),
         scratch_shapes=list(scratch),
         compiler_params=pltpu.CompilerParams(vmem_limit_bytes=40 * 1024 * 1024),
-        cost_estimate=pl.CostEstimate(flops=flops, bytes_accessed=total, transcendentals=0),
+        cost_estimate=pl.CostEstimate(flops=int(cost * 1e9), bytes_accessed=0, transcendentals=0),
     )(*args)
 
 
@@ -136,9 +136,46 @@
         ref[rows, :] = total.astype(ref.dtype)
 
 
-def summed(addends, outs):
+def finish_kernel(count, *refs):
+    terms, refs = refs[:count], refs[count:]
+    outs, held, sems = refs[: len(refs) // 2], refs[len(refs) // 2 : -1], refs[-1]
+    copies, first = [], 0
+    for out, buffer in zip(outs, held):
+        rows = out.shape[0] // 2
+        for at in (0, rows):
+            total = None
+            for ref in terms:
+                term = ref[first : first + rows, :].astype(F32)
+                total = term if total is None else total + term
+            buffer[at : at + rows, :] = total.astype(buffer.dtype)
+            copy = pltpu.make_async_copy(
+                buffer.at[at : at + rows, :], out.at[at : at + rows, :], sems.at[len(copies)]
+            )
+            copy.start()
+            copies.append(copy)
+            first += rows
+    for copy in copies:
+        copy.wait()
+
+
+def finished(args, outs, cost):
+    return pl.pallas_call(
+        functools.partial(finish_kernel, len(args)),
+        out_shape=list(outs),
+        in_specs=[pl.BlockSpec(memory_space=pltpu.VMEM)] * len(args),
+        out_specs=[pl.BlockSpec(memory_space=pl.ANY)] * len(outs),
+        scratch_shapes=[
+            *[pltpu.VMEM(o.shape, o.dtype) for o in outs],
+            pltpu.SemaphoreType.DMA((2 * len(outs),)),
+        ],
+        compiler_params=pltpu.CompilerParams(vmem_limit_bytes=40 * 1024 * 1024),
+        cost_estimate=pl.CostEstimate(flops=int(cost * 1e9), bytes_accessed=0, transcendentals=0),
+    )(*args)
+
+
+def summed(addends, outs, cost=0.0):
     counts = tuple(len(a) for a in addends)
-    return call(functools.partial(sum_kernel, counts), outs, *(r for a in addends for r in a))
+    return call(functools.partial(sum_kernel, counts), outs, *(r for a in addends for r in a), cost=cost)
 
 
 def travelling(dy, prob):
@@ -207,6 +244,11 @@
     put_weight_grads(ks, split, xs, dys, (*both, last), (*hid, last_hid), grads)
 
 
+def grads_kernel(slabs, ks, *refs):
+    xs, dys, both, hid, grads = spread(refs, slabs, slabs, slabs, slabs)
+    put_weight_grads(ks, (), xs, dys, both, hid, grads)
+
+
 def near_kernel(experts, slabs, ks, *refs):
     gate_up, xs, dys, both, hid, outs = spread(refs, experts, slabs, slabs, slabs, slabs)
     (contrib,), grads = spread(outs, 1)
@@ -219,7 +261,7 @@
 
 
 def after(value, *others):
-    return lax.optimization_barrier((value, *others))[0]
+    return lax.optimization_barrier((value, *others))[0] if others else value
 
 
 def body(tokens, route_ids, route_probs, cotangent, w_gate_up, w_down):
@@ -241,14 +283,13 @@
     down = all_experts(w_down.reshape(wide, width))
 
     slabs, units = len(xs), experts * wide
-    unit_flops = 2 * rows * width * units
     both, hid, contrib = [], [], []
     for x, dyp in zip(xs[:-1], dys):
         b, h, c = call(
             functools.partial(slab_kernel, experts),
             (shape(2 * units, rows), shape(units, rows), shape(rows, width)),
             x, dyp, *gate_up, *down,
-            flops=5 * unit_flops,
+            cost=COSTS["slab"],
         )
         both.append(b)
         hid.append(h)
@@ -257,55 +298,81 @@
         functools.partial(acts_kernel, experts),
         (shape(2 * units, rows, F32),),
         xs[-1], *gate_up,
-        flops=2 * unit_flops,
+        cost=COSTS["acts"],
     )
 
     far = tuple(range(experts // 2, experts))[::-1]
     near = tuple(range(experts // 2))[::-1]
     split = tuple(k for k in far if k % 2)
+    even = tuple(k for k in far if not k % 2)
     whole, third = shape(3 * wide, width), shape(wide, width)
-    grads = [piece for k in far for piece in ([third] * 3 if k in split else [whole])]
-    b, h, *got_far = call(
-        functools.partial(far_kernel, experts, slabs, far, split),
-        (shape(2 * units, rows), shape(units, rows), *grads),
+    b, h, *got_split = call(
+        functools.partial(far_kernel, experts, slabs, split, split),
+        (shape(2 * units, rows), shape(units, rows), *[third] * (3 * len(split))),
         acts, *down, *xs, *dys, *both, *hid,
-        flops=3 * slabs * unit_flops // 2 + unit_flops,
+        cost=COSTS["far"],
     )
     both.append(b)
     hid.append(h)
+    got_even = call(
+        functools.partial(grads_kernel, slabs, even),
+        [whole] * len(even),
+        *xs, *dys, *both, *hid,
+        cost=COSTS["even"],
+    )
+    got_far = []
+    for k in far:
+        if k in split:
+            got_far, got_split = [*got_far, *got_split[:3]], got_split[3:]
+        else:
+            got_far, got_even = [*got_far, got_even[0]], got_even[1:]
+    terms = {}
+    for k in far:
+        count = 3 if k in split else 1
+        terms[k], got_far = [tuple(got_far[:count])], got_far[count:]
+    first_bit, *other_bits = bits_of(experts)
+
+    def swap_out(ks, bit):
+        for k in ks:
+            out = terms.pop(k)
+            if len(out) > 1:
+                out = [summed(out, [whole])]
+                joined.extend(out[0])
+            terms.setdefault(k ^ bit, []).append(tuple(swapped(v, bit) for v in out[0]))
+
+    joined = []
+    swap_out(split, first_bit)
+    if len(other_bits) == 1:
+        out = summed(terms.pop(even[0]), [whole], COSTS["join"])
+        joined.extend(out)
+        terms[0] = [(swapped(out[0], other_bits[0]),)]
     c, *got_near = call(
         functools.partial(near_kernel, experts, slabs, near),
         (shape(rows, width), *[whole] * len(near)),
-        *gate_up, *xs, *dys, *both, *hid,
-        flops=3 * slabs * unit_flops // 2 + 2 * unit_flops,
+        *gate_up, *xs, *dys, *both[:-1], after(both[-1], *joined), *hid,
+        cost=COSTS["near"],
     )
     contrib.append(c)
-    terms = {k: [(got,)] for k, got in zip(near, got_near)}
-    for k in far:
-        count = 3 if k in split else 1
-        terms[k], got_far = [tuple(got_far[:count])], got_far[count:]
-
-    total = contrib[0].astype(F32)
-    if slabs > 1:
-        total = total + onward(after(contrib[1], both[-1]), -1).astype(F32)
+    for k, got in zip(near, got_near):
+        terms.setdefault(k, []).insert(0, (got,))
+    back = [onward(after(contrib[1], *joined), -1)] if slabs > 1 else []
     acc = None
     if slabs > 2:
-        acc = onward(after(contrib[2], acts, *both[:-1]))
-    for bit in bits_of(experts):
-        for k in sorted((k for k in terms if k & bit), reverse=True):
-            out = terms.pop(k)
-            if len(out) > 1:
-                out = [summed(out, [whole])]
-                if bit == 2 and acc is not None:
-                    acc = after(acc, *out[0])
-            terms[k ^ bit].append(tuple(swapped(v, bit) for v in out[0]))
-    grad_gate_up, grad_down = summed(terms[0], [shape(2 * wide, width, F32), shape(wide, width, F32)])
-
+        acc = onward(after(contrib[2], acts))
+    if acc is not None and joined:
+        acc = after(acc, *joined)
+    swap_out([k for k in near if k % 2], first_bit)
+    if len(other_bits) != 1:
+        for bit in other_bits:
+            swap_out(sorted((k for k in terms if k & bit), reverse=True), bit)
     for i in range(3, slabs):
         acc = onward((acc.astype(F32) + contrib[i].astype(F32)).astype(BF16))
-    if slabs > 2:
-        total = total + acc.astype(F32)
-    acc = total.astype(BF16)
+    tokens_terms = [contrib[0], *back, *([acc] if slabs > 2 else [])]
+    (acc,) = finished(tokens_terms, [shape(rows, width)], COSTS["tokens"])
+    own, *others = [t for (t,) in terms[0]]
+    grad_gate_up, grad_down = finished(
+        [after(own, acc), *others], [shape(2 * wide, width, F32), shape(wide, width, F32)], COSTS["last"]
+    )
     return acc, grad_gate_up.reshape(1, 2, wide, width), grad_down.reshape(1, wide, width)
 
 

time: 112 us -> 111 us (level)
  waiting for transfers between devices: 61.9 us -> 59.7 us
    ppermute x9, waiting for transfers between devices: 56 us -> 46.5 us  [onward(): return lax.ppermute(block, 'dp', ring_pairs(lax.axis_size('dp'), turns))]
    ppermute x11, waiting for transfers between devices: 5.89 us -> 13.1 us  [swapped(): lax.ppermute(block, 'expert', [(i, i ^ bit) for i in range(lax.axis_size(...]
    pallas_call x0 -> x2, Pallas kernels: none -> 2.47 us  [finished(): pl.pallas_call(functools.partial(finish_kernel, len(args)), out_shape=lis...]
    pallas_call x8, Pallas kernels: 14.3 us -> 12.7 us  [call(): pl.pallas_call(kernel, out_shape=list(outs), in_specs=[pl.BlockSpec(memor...]
  transfers between devices with their start and end apart: 20 -> 20, of which waited for: 10 -> 12; matrix products, arithmetic and copies ran while one was open for 3% -> 2% of each run, Pallas kernels for 11% -> 12%
where the time goes in v4:
time: 111 us
  waiting for transfers between devices  59.7 us (54%)
  starting transfers between devices  33.3 us (30%)
  Pallas kernels  15.1 us (14%)
  local copies, waits for them, and re-layouts  1.11 us (1%)
    ppermute x9, waiting for transfers between devices, onward(): return lax.ppermute(block, 'dp', ring_pairs(lax.axis_size('dp'), turns))  46.5 us
    ppermute x9, starting transfers between devices, onward(): return lax.ppermute(block, 'dp', ring_pairs(lax.axis_size('dp'), turns))  27.1 us
    ppermute x11, waiting for transfers between devices, swapped(): lax.ppermute(block, 'expert', [(i, i ^ bit) for i in range(lax.axis_size(...  13.1 us
    pallas_call x8, Pallas kernels, call(): pl.pallas_call(kernel, out_shape=list(outs), in_specs=[pl.BlockSpec(memor...  12.7 us
    ppermute x11, starting transfers between devices, swapped(): lax.ppermute(block, 'expert', [(i, i ^ bit) for i in range(lax.axis_size(...  6.22 us
    pallas_call x2, Pallas kernels, finished(): pl.pallas_call(functools.partial(finish_kernel, len(args)), out_shape=lis...  2.47 us
  transfers between devices with their start and end apart: 20, of which 12 were waited for; matrix products, arithmetic and copies ran while one was open for 2% of the time, Pallas kernels for 12%

profile of v4, /device:TPU:0, one launch (start us, length us, event | category | flops | bytes accessed | tf_op | source)
XLA Modules:
  0.0 111.1 jit_solution(224667838944791795)
XLA Ops:
  0.6 0.0 copy-start.1
  0.6 0.0 copy-start.2
  0.7 3.1 %collective-permute-start.6 = (bf16[128,2048]{1,0:T(8,128)(2,1)}, bf16[128,2048]{1,0:T(8,128)(2,1)S(1)}, u32[]{:S(2)}, u32[]{:S(2)}) collective-permute-start(bf16[128,2048]{1,0:T(8,128)(2,1)} %refs_4_.1), channel_id=1, source_target_pairs={{0,1},{1,3},{3,2},{2,0},{4,5},{5,7},{7,6},{6,4},{8,9},{9,11},{11,1... | collective-permute-start | bytes 1572872 | tf_op jit(solution)/shard_map/ppermute | solution.py:22
  3.7 0.8 fusion
  4.5 1.5 %collective-permute-start.1 = (bf16[192,2048]{1,0:T(8,128)(2,1)}, bf16[192,2048]{1,0:T(8,128)(2,1)S(1)}, u32[]{:S(2)}, u32[]{:S(2)}) collective-permute-start(bf16[192,2048]{1,0:T(8,128)(2,1)} %bitcast.12), channel_id=1, source_target_pairs={{0,8},{4,12},{8,0},{12,4},{1,9},{5,13},{9,1},{13,5},{2,10},{6,14},... | collective-permute-start | bytes 2359304 | tf_op jit(solution)/shard_map/ppermute | solution.py:26
  6.0 1.1 copy.15
  7.2 2.6 %collective-permute-start.7 = (bf16[1040,256]{1,0:T(8,128)(2,1)S(1)}, bf16[1040,256]{1,0:T(8,128)(2,1)S(1)}, u32[]{:S(2)}, u32[]{:S(2)}) collective-permute-start(bf16[1040,256]{1,0:T(8,128)(2,1)S(1)} %pad_maximum_fusion.refs_1_.refs_9_.refs_4_.refs_8_), channel_id=1, source_target_pairs={{0,1},{1,3},{3,2},{2,0},{4,5},{5,7},{7,6},{6,4},{8,9},{9,11},{11,1... | collective-permute-start | bytes 1597448 | tf_op jit(solution)/shard_map/ppermute | solution.py:22
  9.8 7.9 %collective-permute-done.6.refs_0_.refs_6_.refs_1_.refs_5_ = bf16[128,2048]{1,0:T(8,128)(2,1)S(1)} collective-permute-done((bf16[128,2048]{1,0:T(8,128)(2,1)}, bf16[128,2048]{1,0:T(8,128)(2,1)S(1)}, u32[]{:S(2)}, u32[]{:S(2)}) %collective-permute-start.6) | collective-permute-done | bytes 524320 | tf_op jit(solution)/shard_map/ppermute | solution.py:22
  17.7 1.3 %collective-permute-start.8 = (bf16[128,2048]{1,0:T(8,128)(2,1)S(1)}, bf16[128,2048]{1,0:T(8,128)(2,1)S(1)}, u32[]{:S(2)}, u32[]{:S(2)}) collective-permute-start(bf16[128,2048]{1,0:T(8,128)(2,1)S(1)} %collective-permute-done.6.refs_0_.refs_6_.refs_1_.refs_5_), channel_id=1, source_target_pairs={{0,1},{1,3},{3,2},{2,0},{4,5},{5,7},{7,6},{6,4},{8,9},{9,11},{11,1... | collective-permute-start | bytes 1572872 | tf_op jit(solution)/shard_map/ppermute | solution.py:22
  19.0 0.0 copy-done.1
  19.0 0.0 collective-permute-start
  19.0 4.7 %collective-permute-done.1.refs_4_.refs_3_.refs_2_ = bf16[192,2048]{1,0:T(8,128)(2,1)S(1)} collective-permute-done((bf16[192,2048]{1,0:T(8,128)(2,1)}, bf16[192,2048]{1,0:T(8,128)(2,1)S(1)}, u32[]{:S(2)}, u32[]{:S(2)}) %collective-permute-start.1) | collective-permute-done | bytes 786464 | tf_op jit(solution)/shard_map/ppermute | solution.py:26
  23.7 0.0 collective-permute-start.2
  23.7 5.4 %collective-permute-done.7.refs_1_.refs_10_.refs_5_.refs_9_ = bf16[1040,256]{1,0:T(8,128)(2,1)S(1)} collective-permute-done((bf16[1040,256]{1,0:T(8,128)(2,1)S(1)}, bf16[1040,256]{1,0:T(8,128)(2,1)S(1)}, u32[]{:S(2)}, u32[]{:S(2)}) %collective-permute-start.7) | collective-permute-done | bytes 532512 | tf_op jit(solution)/shard_map/ppermute | solution.py:22
  29.1 1.2 %collective-permute-start.10 = (bf16[1040,256]{1,0:T(8,128)(2,1)S(1)}, bf16[1040,256]{1,0:T(8,128)(2,1)S(1)}, u32[]{:S(2)}, u32[]{:S(2)}) collective-permute-start(bf16[1040,256]{1,0:T(8,128)(2,1)S(1)} %collective-permute-done.7.refs_1_.refs_10_.refs_5_.refs_9_), channel_id=1, source_target_pairs={{0,1},{1,3},{3,2},{2,0},{4,5},{5,7},{7,6},{6,4},{8,9},{9,11},{11,1... | collective-permute-start | bytes 1597448 | tf_op jit(solution)/shard_map/ppermute | solution.py:22
  30.3 10.1 %collective-permute-done.8.refs_0_.refs_7_.refs_2_.refs_6_ = bf16[128,2048]{1,0:T(8,128)(2,1)S(1)} collective-permute-done((bf16[128,2048]{1,0:T(8,128)(2,1)S(1)}, bf16[128,2048]{1,0:T(8,128)(2,1)S(1)}, u32[]{:S(2)}, u32[]{:S(2)}) %collective-permute-start.8) | collective-permute-done | bytes 524320 | tf_op jit(solution)/shard_map/ppermute | solution.py:22
  40.4 1.2 %collective-permute-start.9 = (bf16[128,2048]{1,0:T(8,128)(2,1)S(1)}, bf16[128,2048]{1,0:T(8,128)(2,1)S(1)}, u32[]{:S(2)}, u32[]{:S(2)}) collective-permute-start(bf16[128,2048]{1,0:T(8,128)(2,1)S(1)} %collective-permute-done.8.refs_0_.refs_7_.refs_2_.refs_6_), channel_id=1, source_target_pairs={{0,1},{1,3},{3,2},{2,0},{4,5},{5,7},{7,6},{6,4},{8,9},{9,11},{11,1... | collective-permute-start | bytes 1572872 | tf_op jit(solution)/shard_map/ppermute | solution.py:22
  41.5 0.0 copy-done.2
  41.5 1.5 %collective-permute-start.4 = (bf16[96,2048]{1,0:T(8,128)(2,1)S(1)}, bf16[96,2048]{1,0:T(8,128)(2,1)S(1)}, u32[]{:S(2)}, u32[]{:S(2)}) collective-permute-start(bf16[96,2048]{1,0:T(8,128)(2,1)S(1)} %bitcast.19), channel_id=1, source_target_pairs={{0,8},{4,12},{8,0},{12,4},{1,9},{5,13},{9,1},{13,5},{2,10},{6,14},... | collective-permute-start | bytes 1179656 | tf_op jit(solution)/shard_map/ppermute | solution.py:26
  43.0 7.0 %collective-permute-done.4.refs_8_.refs_3_ = bf16[96,2048]{1,0:T(8,128)(2,1)S(1)} collective-permute-done((bf16[96,2048]{1,0:T(8,128)(2,1)S(1)}, bf16[96,2048]{1,0:T(8,128)(2,1)S(1)}, u32[]{:S(2)}, u32[]{:S(2)}) %collective-permute-start.4) | collective-permute-done | bytes 393248 | tf_op jit(solution)/shard_map/ppermute | solution.py:26
  50.1 0.0 collective-permute-start.3
  50.1 0.0 collective-permute-done.refs_3_.refs_2_.refs_1_
  50.1 0.5 collective-permute-start.5
  50.6 1.2 %collective-permute-done.10.refs_1_.refs_11_.refs_6_.refs_10_ = bf16[1040,256]{1,0:T(8,128)(2,1)S(1)} collective-permute-done((bf16[1040,256]{1,0:T(8,128)(2,1)S(1)}, bf16[1040,256]{1,0:T(8,128)(2,1)S(1)}, u32[]{:S(2)}, u32[]{:S(2)}) %collective-permute-start.10) | collective-permute-done | bytes 532512 | tf_op jit(solution)/shard_map/ppermute | solution.py:22
  51.8 2.2 %collective-permute-start.11 = (bf16[1040,256]{1,0:T(8,128)(2,1)S(1)}, bf16[1040,256]{1,0:T(8,128)(2,1)S(1)}, u32[]{:S(2)}, u32[]{:S(2)}) collective-permute-start(bf16[1040,256]{1,0:T(8,128)(2,1)S(1)} %collective-permute-done.10.refs_1_.refs_11_.refs_6_.refs_10_), channel_id=1, source_target_pairs={{0,1},{1,3},{3,2},{2,0},{4,5},{5,7},{7,6},{6,4},{8,9},{9,11},{11,1... | collective-permute-start | bytes 1597448 | tf_op jit(solution)/shard_map/ppermute | solution.py:22
  54.0 9.0 %collective-permute-done.9.refs_0_.refs_8_.refs_3_.refs_7_ = bf16[128,2048]{1,0:T(8,128)(2,1)S(1)} collective-permute-done((bf16[128,2048]{1,0:T(8,128)(2,1)S(1)}, bf16[128,2048]{1,0:T(8,128)(2,1)S(1)}, u32[]{:S(2)}, u32[]{:S(2)}) %collective-permute-start.9) | collective-permute-done | bytes 524320 | tf_op jit(solution)/shard_map/ppermute | solution.py:22
  63.0 0.0 collective-permute-done.2.refs_5_.refs_4_.refs_3_
  63.0 1.0 shard_map.88.refs_0_
  64.0 0.0 collective-permute-done.3.refs_7_.refs_2_
  64.0 0.0 collective-permute-done.5.refs_9_.refs_4_
  64.0 2.2 %shard_map.87 = (bf16[768,128]{1,0:T(8,128)(2,1)S(1)}, bf16[384,128]{1,0:T(8,128)(2,1)S(1)}, bf16[128,2048]{1,0:T(8,128)(2,1)S(1)}) custom-call(bf16[128,2048]{1,0:T(8,128)(2,1)S(1)} %collective-permute-done.8.refs_0_.refs_7_.refs_2_.refs_6_, bf16[1040,256]{1,0:T(8,128)(2,1)S(1)} %collective-permute-done.10.refs_1_.refs_11_.refs_6_.refs_10_, ...), custom_call_target="tpu_custom_call" | custom-call | flops 2000000000 | tf_op jit(solution)/shard_map/pallas_call | solution.py:41
  66.2 0.0 copy-start
  66.2 1.2 %collective-permute-start.16 = (bf16[128,2048]{1,0:T(8,128)(2,1)S(1)}, bf16[128,2048]{1,0:T(8,128)(2,1)S(1)}, u32[]{:S(2)}, u32[]{:S(2)}) collective-permute-start(bf16[128,2048]{1,0:T(8,128)(2,1)S(1)} %get-tuple-element.56), channel_id=1, source_target_pairs={{0,1},{1,3},{3,2},{2,0},{4,5},{5,7},{7,6},{6,4},{8,9},{9,11},{11,1... | collective-permute-start | bytes 1572872 | tf_op jit(solution)/shard_map/ppermute | solution.py:22
  67.4 2.2 %shard_map.86 = (bf16[768,128]{1,0:T(8,128)(2,1)S(1)}, bf16[384,128]{1,0:T(8,128)(2,1)S(1)}, bf16[128,2048]{1,0:T(8,128)(2,1)S(1)}) custom-call(bf16[128,2048]{1,0:T(8,128)(2,1)S(1)} %collective-permute-done.6.refs_0_.refs_6_.refs_1_.refs_5_, bf16[1040,256]{1,0:T(8,128)(2,1)S(1)} %collective-permute-done.7.refs_1_.refs_10_.refs_5_.refs_9_, ...), custom_call_target="tpu_custom_call" | custom-call | flops 2000000000 | tf_op jit(solution)/shard_map/pallas_call | solution.py:41
  69.7 0.0 copy-done
  69.7 2.2 %shard_map.85 = (bf16[768,128]{1,0:T(8,128)(2,1)S(1)}, bf16[384,128]{1,0:T(8,128)(2,1)S(1)}, bf16[128,2048]{1,0:T(8,128)(2,1)S(1)}) custom-call(bf16[128,2048]{1,0:T(8,128)(2,1)S(1)} %copy-done, bf16[1040,256]{1,0:T(8,128)(2,1)S(1)} %pad_maximum_fusion.refs_1_.refs_9_.refs_4_.refs_8_, bf16[192,2048]{1,0:T(8,128)(2,1)S(1)} %bitcast.17, ...), custom_call_target="tpu_custom_call" | custom-call | flops 2000000000 | tf_op jit(solution)/shard_map/pallas_call | solution.py:41
  71.9 2.5 %collective-permute-done.11.refs_12_.refs_7_.refs_11_ = bf16[1040,256]{1,0:T(8,128)(2,1)S(1)} collective-permute-done((bf16[1040,256]{1,0:T(8,128)(2,1)S(1)}, bf16[1040,256]{1,0:T(8,128)(2,1)S(1)}, u32[]{:S(2)}, u32[]{:S(2)}) %collective-permute-start.11) | collective-permute-done | bytes 532512 | tf_op jit(solution)/shard_map/ppermute | solution.py:22
  74.4 1.6 %shard_map.89 = (bf16[768,128]{1,0:T(8,128)(2,1)S(1)}, bf16[384,128]{1,0:T(8,128)(2,1)S(1)}, bf16[96,2048]{1,0:T(8,128)(2,1)S(1)}, bf16[96,2048]{1,0:T(8,128)(2,1)S(1)}, bf16[96,2048]{1,0:T(8,128)(2,1)S(1)}) custom-call(f32[768,128]{1,0:T(8,128)S(1)} %shard_map.88.refs_0_, bf16[96,2048]{1,0:T(8,128)(2,1)S(1)} %bitcast.24, ...), custom_call_target="tpu_custom_call" | custom-call | flops 1000000000 | tf_op jit(solution)/shard_map/pallas_call | solution.py:41
  76.0 0.1 collective-permute-start.12
  76.1 0.5 collective-permute-start.13
  76.6 0.1 collective-permute-start.14
  76.7 0.9 shard_map.90.refs_0_
  77.6 0.2 collective-permute-done.12.refs_1_
  77.8 0.6 collective-permute-done.13.refs_2_
  78.4 0.6 collective-permute-done.14.refs_3_
  78.9 0.3 shard_map.91
  79.2 1.9 %collective-permute-start.18 = (bf16[288,2048]{1,0:T(8,128)(2,1)S(1)}, bf16[288,2048]{1,0:T(8,128)(2,1)S(1)}, u32[]{:S(2)}, u32[]{:S(2)}) collective-permute-start(bf16[288,2048]{1,0:T(8,128)(2,1)S(1)} %shard_map.91), channel_id=1, source_target_pairs={{0,8},{4,12},{8,0},{12,4},{1,9},{5,13},{9,1},{13,5},{2,10},{6,14},... | collective-permute-start | bytes 3538952 | tf_op jit(solution)/shard_map/ppermute | solution.py:26
  81.2 1.7 %collective-permute-start.15 = (bf16[128,2048]{1,0:T(8,128)(2,1)S(1)}, bf16[128,2048]{1,0:T(8,128)(2,1)S(1)}, u32[]{:S(2)}, u32[]{:S(2)}) collective-permute-start(bf16[128,2048]{1,0:T(8,128)(2,1)S(1)} %get-tuple-element.54), channel_id=1, source_target_pairs={{0,2},{1,0},{3,1},{2,3},{4,6},{5,4},{7,5},{6,7},{8,10},{9,8},{11,9... | collective-permute-start | bytes 1572872 | tf_op jit(solution)/shard_map/ppermute | solution.py:22
  82.8 2.3 %shard_map.92 = (bf16[128,2048]{1,0:T(8,128)(2,1)S(1)}, bf16[288,2048]{1,0:T(8,128)(2,1)S(1)}, bf16[288,2048]{1,0:T(8,128)(2,1)S(1)}) custom-call(bf16[192,2048]{1,0:T(8,128)(2,1)S(1)} %bitcast.18, bf16[192,2048]{1,0:T(8,128)(2,1)S(1)} %collective-permute-done.refs_3_.refs_2_.refs_1_, bf16[192,2048]{1,0:T(8,128)(2,1)S(1)} %collective-permute-done.1.refs_4_.refs_3_.refs_2_, ...), custom_call_target="tpu_custom_call" | custom-call | flops 2000000000 | tf_op jit(solution)/shard_map/pallas_call | solution.py:41
  85.1 0.1 collective-permute-start.19
  85.2 0.0 collective-permute-done.16
  85.2 0.1 add_convert_fusion
  85.3 12.7 %collective-permute-start.17 = (bf16[128,2048]{1,0:T(8,128)(2,1)S(1)}, bf16[128,2048]{1,0:T(8,128)(2,1)S(1)}, u32[]{:S(2)}, u32[]{:S(2)}) collective-permute-start(bf16[128,2048]{1,0:T(8,128)(2,1)S(1)} %add_convert_fusion), channel_id=1, source_target_pairs={{0,1},{1,3},{3,2},{2,0},{4,5},{5,7},{7,6},{6,4},{8,9},{9,11},{11,1... | collective-permute-start | bytes 1572872 | tf_op jit(solution)/shard_map/ppermute | solution.py:22
  98.0 0.0 collective-permute-done.15.refs_1_
  98.0 10.4 %collective-permute-done.17.refs_2_ = bf16[128,2048]{1,0:T(8,128)(2,1)S(1)} collective-permute-done((bf16[128,2048]{1,0:T(8,128)(2,1)S(1)}, bf16[128,2048]{1,0:T(8,128)(2,1)S(1)}, u32[]{:S(2)}, u32[]{:S(2)}) %collective-permute-start.17) | collective-permute-done | bytes 524320 | tf_op jit(solution)/shard_map/ppermute | solution.py:22
  108.5 0.9 shard_map.93
  109.4 0.0 collective-permute-done.19.refs_2_
  109.4 0.0 collective-permute-done.18.refs_1_
  109.4 1.6 %shard_map.94 = (f32[192,2048]{1,0:T(8,128)}, f32[96,2048]{1,0:T(8,128)}) custom-call(bf16[288,2048]{1,0:T(8,128)(2,1)S(1)} %get-tuple-element.61.refs_0_, bf16[288,2048]{1,0:T(8,128)(2,1)S(1)} %collective-permute-done.18.refs_1_, bf16[288,2048]{1,0:T(8,128)(2,1)S(1)} %collective-permute-done.19.refs_2_), custom_call_target="tpu_custom_call" | custom-call | flops 2000000000 | tf_op jit(solution)/shard_map/pallas_call | solution.py:162
  (4 shorter events, 0.1 us)
Async XLA Ops:
  0.6 18.3 %copy-start.1 = (bf16[1,2,96,2048]{3,2,1,0:T(8,128)(2,1)S(1)}, bf16[1,2,96,2048]{3,2,1,0:T(8,128)(2,1)}, u32[]{:S(2)}) copy-start(bf16[1,2,96,2048]{3,2,1,0:T(8,128)(2,1)} %param.12) | copy-start | bytes 2359300
  0.6 40.9 %copy-start.2 = (bf16[1,96,2048]{2,1,0:T(8,128)(2,1)S(1)}, bf16[1,96,2048]{2,1,0:T(8,128)(2,1)}, u32[]{:S(2)}) copy-start(bf16[1,96,2048]{2,1,0:T(8,128)(2,1)} %param.13) | copy-start | bytes 1179652
  0.7 17.1 %collective-permute-start.6 = (bf16[128,2048]{1,0:T(8,128)(2,1)}, bf16[128,2048]{1,0:T(8,128)(2,1)S(1)}, u32[]{:S(2)}, u32[]{:S(2)}) collective-permute-start(bf16[128,2048]{1,0:T(8,128)(2,1)} %refs_4_.1), channel_id=1, source_target_pairs={{0,1},{1,3},{3,2},{2,0},{4,5},{5,7},{7,6},{6,4},{8,9},{9,11},{11,1... | collective-permute-start | bytes 1572872 | tf_op jit(solution)/shard_map/ppermute | solution.py:22
  4.5 19.2 %collective-permute-start.1 = (bf16[192,2048]{1,0:T(8,128)(2,1)}, bf16[192,2048]{1,0:T(8,128)(2,1)S(1)}, u32[]{:S(2)}, u32[]{:S(2)}) collective-permute-start(bf16[192,2048]{1,0:T(8,128)(2,1)} %bitcast.12), channel_id=1, source_target_pairs={{0,8},{4,12},{8,0},{12,4},{1,9},{5,13},{9,1},{13,5},{2,10},{6,14},... | collective-permute-start | bytes 2359304 | tf_op jit(solution)/shard_map/ppermute | solution.py:26
  7.2 22.0 %collective-permute-start.7 = (bf16[1040,256]{1,0:T(8,128)(2,1)S(1)}, bf16[1040,256]{1,0:T(8,128)(2,1)S(1)}, u32[]{:S(2)}, u32[]{:S(2)}) collective-permute-start(bf16[1040,256]{1,0:T(8,128)(2,1)S(1)} %pad_maximum_fusion.refs_1_.refs_9_.refs_4_.refs_8_), channel_id=1, source_target_pairs={{0,1},{1,3},{3,2},{2,0},{4,5},{5,7},{7,6},{6,4},{8,9},{9,11},{11,1... | collective-permute-start | bytes 1597448 | tf_op jit(solution)/shard_map/ppermute | solution.py:22
  17.7 22.6 %collective-permute-start.8 = (bf16[128,2048]{1,0:T(8,128)(2,1)S(1)}, bf16[128,2048]{1,0:T(8,128)(2,1)S(1)}, u32[]{:S(2)}, u32[]{:S(2)}) collective-permute-start(bf16[128,2048]{1,0:T(8,128)(2,1)S(1)} %collective-permute-done.6.refs_0_.refs_6_.refs_1_.refs_5_), channel_id=1, source_target_pairs={{0,1},{1,3},{3,2},{2,0},{4,5},{5,7},{7,6},{6,4},{8,9},{9,11},{11,1... | collective-permute-start | bytes 1572872 | tf_op jit(solution)/shard_map/ppermute | solution.py:22
  19.0 31.1 %collective-permute-start = (bf16[192,2048]{1,0:T(8,128)(2,1)S(1)}, bf16[192,2048]{1,0:T(8,128)(2,1)S(1)}, u32[]{:S(2)}, u32[]{:S(2)}) collective-permute-start(bf16[192,2048]{1,0:T(8,128)(2,1)S(1)} %bitcast.13), channel_id=1, source_target_pairs={{0,4},{4,0},{8,12},{12,8},{1,5},{5,1},{9,13},{13,9},{2,6},{6,2},{1... | collective-permute-start | bytes 2359304 | tf_op jit(solution)/shard_map/ppermute | solution.py:26
  23.7 39.3 %collective-permute-start.2 = (bf16[192,2048]{1,0:T(8,128)(2,1)S(1)}, bf16[192,2048]{1,0:T(8,128)(2,1)S(1)}, u32[]{:S(2)}, u32[]{:S(2)}) collective-permute-start(bf16[192,2048]{1,0:T(8,128)(2,1)S(1)} %collective-permute-done.1.refs_4_.refs_3_.refs_2_), channel_id=1, source_target_pairs={{0,4},{4,0},{8,12},{12,8},{1,5},{5,1},{9,13},{13,9},{2,6},{6,2},{1... | collective-permute-start | bytes 2359304 | tf_op jit(solution)/shard_map/ppermute | solution.py:26
  29.1 22.6 %collective-permute-start.10 = (bf16[1040,256]{1,0:T(8,128)(2,1)S(1)}, bf16[1040,256]{1,0:T(8,128)(2,1)S(1)}, u32[]{:S(2)}, u32[]{:S(2)}) collective-permute-start(bf16[1040,256]{1,0:T(8,128)(2,1)S(1)} %collective-permute-done.7.refs_1_.refs_10_.refs_5_.refs_9_), channel_id=1, source_target_pairs={{0,1},{1,3},{3,2},{2,0},{4,5},{5,7},{7,6},{6,4},{8,9},{9,11},{11,1... | collective-permute-start | bytes 1597448 | tf_op jit(solution)/shard_map/ppermute | solution.py:22
  40.4 22.6 %collective-permute-start.9 = (bf16[128,2048]{1,0:T(8,128)(2,1)S(1)}, bf16[128,2048]{1,0:T(8,128)(2,1)S(1)}, u32[]{:S(2)}, u32[]{:S(2)}) collective-permute-start(bf16[128,2048]{1,0:T(8,128)(2,1)S(1)} %collective-permute-done.8.refs_0_.refs_7_.refs_2_.refs_6_), channel_id=1, source_target_pairs={{0,1},{1,3},{3,2},{2,0},{4,5},{5,7},{7,6},{6,4},{8,9},{9,11},{11,1... | collective-permute-start | bytes 1572872 | tf_op jit(solution)/shard_map/ppermute | solution.py:22
  41.5 8.6 %collective-permute-start.4 = (bf16[96,2048]{1,0:T(8,128)(2,1)S(1)}, bf16[96,2048]{1,0:T(8,128)(2,1)S(1)}, u32[]{:S(2)}, u32[]{:S(2)}) collective-permute-start(bf16[96,2048]{1,0:T(8,128)(2,1)S(1)} %bitcast.19), channel_id=1, source_target_pairs={{0,8},{4,12},{8,0},{12,4},{1,9},{5,13},{9,1},{13,5},{2,10},{6,14},... | collective-permute-start | bytes 1179656 | tf_op jit(solution)/shard_map/ppermute | solution.py:26
  50.1 13.9 %collective-permute-start.3 = (bf16[96,2048]{1,0:T(8,128)(2,1)S(1)}, bf16[96,2048]{1,0:T(8,128)(2,1)S(1)}, u32[]{:S(2)}, u32[]{:S(2)}) collective-permute-start(bf16[96,2048]{1,0:T(8,128)(2,1)S(1)} %bitcast.20), channel_id=1, source_target_pairs={{0,4},{4,0},{8,12},{12,8},{1,5},{5,1},{9,13},{13,9},{2,6},{6,2},{1... | collective-permute-start | bytes 1179656 | tf_op jit(solution)/shard_map/ppermute | solution.py:26
  50.1 13.9 %collective-permute-start.5 = (bf16[96,2048]{1,0:T(8,128)(2,1)S(1)}, bf16[96,2048]{1,0:T(8,128)(2,1)S(1)}, u32[]{:S(2)}, u32[]{:S(2)}) collective-permute-start(bf16[96,2048]{1,0:T(8,128)(2,1)S(1)} %collective-permute-done.4.refs_8_.refs_3_), channel_id=1, source_target_pairs={{0,4},{4,0},{8,12},{12,8},{1,5},{5,1},{9,13},{13,9},{2,6},{6,2},{1... | collective-permute-start | bytes 1179656 | tf_op jit(solution)/shard_map/ppermute | solution.py:26
  51.8 22.6 %collective-permute-start.11 = (bf16[1040,256]{1,0:T(8,128)(2,1)S(1)}, bf16[1040,256]{1,0:T(8,128)(2,1)S(1)}, u32[]{:S(2)}, u32[]{:S(2)}) collective-permute-start(bf16[1040,256]{1,0:T(8,128)(2,1)S(1)} %collective-permute-done.10.refs_1_.refs_11_.refs_6_.refs_10_), channel_id=1, source_target_pairs={{0,1},{1,3},{3,2},{2,0},{4,5},{5,7},{7,6},{6,4},{8,9},{9,11},{11,1... | collective-permute-start | bytes 1597448 | tf_op jit(solution)/shard_map/ppermute | solution.py:22
  66.2 3.5 %copy-start = (bf16[128,2048]{1,0:T(8,128)(2,1)S(1)}, bf16[128,2048]{1,0:T(8,128)(2,1)}, u32[]{:S(2)}) copy-start(bf16[128,2048]{1,0:T(8,128)(2,1)} %refs_4_.1) | copy-start | bytes 1572868
  66.2 18.9 %collective-permute-start.16 = (bf16[128,2048]{1,0:T(8,128)(2,1)S(1)}, bf16[128,2048]{1,0:T(8,128)(2,1)S(1)}, u32[]{:S(2)}, u32[]{:S(2)}) collective-permute-start(bf16[128,2048]{1,0:T(8,128)(2,1)S(1)} %get-tuple-element.56), channel_id=1, source_target_pairs={{0,1},{1,3},{3,2},{2,0},{4,5},{5,7},{7,6},{6,4},{8,9},{9,11},{11,1... | collective-permute-start | bytes 1572872 | tf_op jit(solution)/shard_map/ppermute | solution.py:22
  76.0 1.8 %collective-permute-start.12 = (bf16[96,2048]{1,0:T(8,128)(2,1)S(1)}, bf16[96,2048]{1,0:T(8,128)(2,1)S(1)}, u32[]{:S(2)}, u32[]{:S(2)}) collective-permute-start(bf16[96,2048]{1,0:T(8,128)(2,1)S(1)} %get-tuple-element.51), channel_id=1, source_target_pairs={{0,4},{4,0},{8,12},{12,8},{1,5},{5,1},{9,13},{13,9},{2,6},{6,2},{1... | collective-permute-start | bytes 1179656 | tf_op jit(solution)/shard_map/ppermute | solution.py:26
  76.1 2.3 %collective-permute-start.13 = (bf16[96,2048]{1,0:T(8,128)(2,1)S(1)}, bf16[96,2048]{1,0:T(8,128)(2,1)S(1)}, u32[]{:S(2)}, u32[]{:S(2)}) collective-permute-start(bf16[96,2048]{1,0:T(8,128)(2,1)S(1)} %get-tuple-element.52), channel_id=1, source_target_pairs={{0,4},{4,0},{8,12},{12,8},{1,5},{5,1},{9,13},{13,9},{2,6},{6,2},{1... | collective-permute-start | bytes 1179656 | tf_op jit(solution)/shard_map/ppermute | solution.py:26
  76.6 2.3 %collective-permute-start.14 = (bf16[96,2048]{1,0:T(8,128)(2,1)S(1)}, bf16[96,2048]{1,0:T(8,128)(2,1)S(1)}, u32[]{:S(2)}, u32[]{:S(2)}) collective-permute-start(bf16[96,2048]{1,0:T(8,128)(2,1)S(1)} %get-tuple-element.53), channel_id=1, source_target_pairs={{0,4},{4,0},{8,12},{12,8},{1,5},{5,1},{9,13},{13,9},{2,6},{6,2},{1... | collective-permute-start | bytes 1179656 | tf_op jit(solution)/shard_map/ppermute | solution.py:26
  79.2 30.2 %collective-permute-start.18 = (bf16[288,2048]{1,0:T(8,128)(2,1)S(1)}, bf16[288,2048]{1,0:T(8,128)(2,1)S(1)}, u32[]{:S(2)}, u32[]{:S(2)}) collective-permute-start(bf16[288,2048]{1,0:T(8,128)(2,1)S(1)} %shard_map.91), channel_id=1, source_target_pairs={{0,8},{4,12},{8,0},{12,4},{1,9},{5,13},{9,1},{13,5},{2,10},{6,14},... | collective-permute-start | bytes 3538952 | tf_op jit(solution)/shard_map/ppermute | solution.py:26
  81.2 16.9 %collective-permute-start.15 = (bf16[128,2048]{1,0:T(8,128)(2,1)S(1)}, bf16[128,2048]{1,0:T(8,128)(2,1)S(1)}, u32[]{:S(2)}, u32[]{:S(2)}) collective-permute-start(bf16[128,2048]{1,0:T(8,128)(2,1)S(1)} %get-tuple-element.54), channel_id=1, source_target_pairs={{0,2},{1,0},{3,1},{2,3},{4,6},{5,4},{7,5},{6,7},{8,10},{9,8},{11,9... | collective-permute-start | bytes 1572872 | tf_op jit(solution)/shard_map/ppermute | solution.py:22
  85.1 24.3 %collective-permute-start.19 = (bf16[288,2048]{1,0:T(8,128)(2,1)S(1)}, bf16[288,2048]{1,0:T(8,128)(2,1)S(1)}, u32[]{:S(2)}, u32[]{:S(2)}) collective-permute-start(bf16[288,2048]{1,0:T(8,128)(2,1)S(1)} %get-tuple-element.62), channel_id=1, source_target_pairs={{0,4},{4,0},{8,12},{12,8},{1,5},{5,1},{9,13},{13,9},{2,6},{6,2},{1... | collective-permute-start | bytes 3538952 | tf_op jit(solution)/shard_map/ppermute | solution.py:26
  85.3 23.1 %collective-permute-start.17 = (bf16[128,2048]{1,0:T(8,128)(2,1)S(1)}, bf16[128,2048]{1,0:T(8,128)(2,1)S(1)}, u32[]{:S(2)}, u32[]{:S(2)}) collective-permute-start(bf16[128,2048]{1,0:T(8,128)(2,1)S(1)} %add_convert_fusion), channel_id=1, source_target_pairs={{0,1},{1,3},{3,2},{2,0},{4,5},{5,7},{7,6},{6,4},{8,9},{9,11},{11,1... | collective-permute-start | bytes 1572872 | tf_op jit(solution)/shard_map/ppermute | solution.py:22

commit v5 on v4

--- a/solution.py
+++ b/solution.py
@@ -9,7 +9,7 @@
 from jax.sharding import PartitionSpec as P
 
 BF16 = jnp.bfloat16
-COSTS = {"slab": 2, "acts": 4, "far": 1, "even": 5, "near": 2, "join": 1, "tokens": 4, "last": 2}
+COSTS = {"slab": 2, "acts": 4, "far": 1, "even": 5, "near": 2, "join": 1, "add": 8, "last": 2}
 F32 = jnp.float32
 
 
@@ -136,16 +136,17 @@
         ref[rows, :] = total.astype(ref.dtype)
 
 
-def finish_kernel(count, *refs):
-    terms, refs = refs[:count], refs[count:]
+def finish_kernel(counts, *refs):
+    groups, refs = [refs[: counts[0]], refs[counts[0] : sum(counts)]], refs[sum(counts) :]
     outs, held, sems = refs[: len(refs) // 2], refs[len(refs) // 2 : -1], refs[-1]
-    copies, first = [], 0
-    for out, buffer in zip(outs, held):
+    copies, first = [], [0, 0]
+    for n, (out, buffer) in enumerate(zip(outs, held)):
+        group = min(n, 1)
         rows = out.shape[0] // 2
         for at in (0, rows):
             total = None
-            for ref in terms:
-                term = ref[first : first + rows, :].astype(F32)
+            for ref in groups[group]:
+                term = ref[first[group] : first[group] + rows, :].astype(F32)
                 total = term if total is None else total + term
             buffer[at : at + rows, :] = total.astype(buffer.dtype)
             copy = pltpu.make_async_copy(
@@ -153,14 +154,15 @@
             )
             copy.start()
             copies.append(copy)
-            first += rows
+            first[group] += rows
     for copy in copies:
         copy.wait()
 
 
-def finished(args, outs, cost):
+def finished(groups, outs, cost):
+    args = [r for group in groups for r in group]
     return pl.pallas_call(
-        functools.partial(finish_kernel, len(args)),
+        functools.partial(finish_kernel, tuple(len(g) for g in groups)),
         out_shape=list(outs),
         in_specs=[pl.BlockSpec(memory_space=pltpu.VMEM)] * len(args),
         out_specs=[pl.BlockSpec(memory_space=pl.ANY)] * len(outs),
@@ -366,12 +368,13 @@
         for bit in other_bits:
             swap_out(sorted((k for k in terms if k & bit), reverse=True), bit)
     for i in range(3, slabs):
-        acc = onward((acc.astype(F32) + contrib[i].astype(F32)).astype(BF16))
+        (acc,) = summed([(acc,), (contrib[i],)], [shape(rows, width)], COSTS["add"])
+        acc = onward(acc)
     tokens_terms = [contrib[0], *back, *([acc] if slabs > 2 else [])]
-    (acc,) = finished(tokens_terms, [shape(rows, width)], COSTS["tokens"])
-    own, *others = [t for (t,) in terms[0]]
-    grad_gate_up, grad_down = finished(
-        [after(own, acc), *others], [shape(2 * wide, width, F32), shape(wide, width, F32)], COSTS["last"]
+    acc, grad_gate_up, grad_down = finished(
+        [tokens_terms, [t for (t,) in terms[0]]],
+        [shape(rows, width), shape(2 * wide, width, F32), shape(wide, width, F32)],
+        COSTS["last"],
     )
     return acc, grad_gate_up.reshape(1, 2, wide, width), grad_down.reshape(1, wide, width)
 

time: 111 us -> 111 us (level)
    pallas_call x2 -> x1, Pallas kernels: 2.47 us -> 1.76 us  [finished(): pl.pallas_call(functools.partial(finish_kernel, tuple((len(g) for g in gr...]
    pallas_call x8 -> x9, Pallas kernels: 12.7 us -> 12.8 us  [call(): pl.pallas_call(kernel, out_shape=list(outs), in_specs=[pl.BlockSpec(memor...]
where the time goes in v5:
time: 111 us; the launch traced here: 110 us
  waiting for transfers between devices  59.7 us (54%)
  starting transfers between devices  33.3 us (30%)
  Pallas kernels  14.5 us (13%)
  local copies, waits for them, and re-layouts  1.11 us (1%)
    ppermute x9, waiting for transfers between devices, onward(): return lax.ppermute(block, 'dp', ring_pairs(lax.axis_size('dp'), turns))  46.6 us
    ppermute x9, starting transfers between devices, onward(): return lax.ppermute(block, 'dp', ring_pairs(lax.axis_size('dp'), turns))  27.1 us
    ppermute x11, waiting for transfers between devices, swapped(): lax.ppermute(block, 'expert', [(i, i ^ bit) for i in range(lax.axis_size(...  13.1 us
    pallas_call x9, Pallas kernels, call(): pl.pallas_call(kernel, out_shape=list(outs), in_specs=[pl.BlockSpec(memor...  12.8 us
    ppermute x11, starting transfers between devices, swapped(): lax.ppermute(block, 'expert', [(i, i ^ bit) for i in range(lax.axis_size(...  6.22 us
  transfers between devices with their start and end apart: 20, of which 12 were waited for; matrix products, arithmetic and copies ran while one was open for 2% of the time, Pallas kernels for 12%

profile of v5, /device:TPU:0, one launch (start us, length us, event | category | flops | bytes accessed | tf_op | source)
XLA Modules:
  0.0 110.4 jit_solution(7995737711253703703)
XLA Ops:
  0.6 0.0 copy-start.1
  0.6 0.0 copy-start.2
  0.7 3.1 %collective-permute-start.6 = (bf16[128,2048]{1,0:T(8,128)(2,1)}, bf16[128,2048]{1,0:T(8,128)(2,1)S(1)}, u32[]{:S(2)}, u32[]{:S(2)}) collective-permute-start(bf16[128,2048]{1,0:T(8,128)(2,1)} %refs_4_.1), channel_id=1, source_target_pairs={{0,1},{1,3},{3,2},{2,0},{4,5},{5,7},{7,6},{6,4},{8,9},{9,11},{11,1... | collective-permute-start | bytes 1572872 | tf_op jit(solution)/shard_map/ppermute | solution.py:22
  3.7 0.8 fusion
  4.5 1.5 %collective-permute-start.1 = (bf16[192,2048]{1,0:T(8,128)(2,1)}, bf16[192,2048]{1,0:T(8,128)(2,1)S(1)}, u32[]{:S(2)}, u32[]{:S(2)}) collective-permute-start(bf16[192,2048]{1,0:T(8,128)(2,1)} %bitcast.12), channel_id=1, source_target_pairs={{0,8},{4,12},{8,0},{12,4},{1,9},{5,13},{9,1},{13,5},{2,10},{6,14},... | collective-permute-start | bytes 2359304 | tf_op jit(solution)/shard_map/ppermute | solution.py:26
  6.0 1.1 copy.15
  7.2 2.6 %collective-permute-start.7 = (bf16[1040,256]{1,0:T(8,128)(2,1)S(1)}, bf16[1040,256]{1,0:T(8,128)(2,1)S(1)}, u32[]{:S(2)}, u32[]{:S(2)}) collective-permute-start(bf16[1040,256]{1,0:T(8,128)(2,1)S(1)} %pad_maximum_fusion.refs_1_.refs_9_.refs_4_.refs_8_), channel_id=1, source_target_pairs={{0,1},{1,3},{3,2},{2,0},{4,5},{5,7},{7,6},{6,4},{8,9},{9,11},{11,1... | collective-permute-start | bytes 1597448 | tf_op jit(solution)/shard_map/ppermute | solution.py:22
  9.8 7.9 %collective-permute-done.6.refs_0_.refs_6_.refs_1_.refs_5_ = bf16[128,2048]{1,0:T(8,128)(2,1)S(1)} collective-permute-done((bf16[128,2048]{1,0:T(8,128)(2,1)}, bf16[128,2048]{1,0:T(8,128)(2,1)S(1)}, u32[]{:S(2)}, u32[]{:S(2)}) %collective-permute-start.6) | collective-permute-done | bytes 524320 | tf_op jit(solution)/shard_map/ppermute | solution.py:22
  17.7 1.3 %collective-permute-start.8 = (bf16[128,2048]{1,0:T(8,128)(2,1)S(1)}, bf16[128,2048]{1,0:T(8,128)(2,1)S(1)}, u32[]{:S(2)}, u32[]{:S(2)}) collective-permute-start(bf16[128,2048]{1,0:T(8,128)(2,1)S(1)} %collective-permute-done.6.refs_0_.refs_6_.refs_1_.refs_5_), channel_id=1, source_target_pairs={{0,1},{1,3},{3,2},{2,0},{4,5},{5,7},{7,6},{6,4},{8,9},{9,11},{11,1... | collective-permute-start | bytes 1572872 | tf_op jit(solution)/shard_map/ppermute | solution.py:22
  19.0 0.0 copy-done.1
  19.0 0.0 collective-permute-start
  19.0 4.7 %collective-permute-done.1.refs_4_.refs_3_.refs_2_ = bf16[192,2048]{1,0:T(8,128)(2,1)S(1)} collective-permute-done((bf16[192,2048]{1,0:T(8,128)(2,1)}, bf16[192,2048]{1,0:T(8,128)(2,1)S(1)}, u32[]{:S(2)}, u32[]{:S(2)}) %collective-permute-start.1) | collective-permute-done | bytes 786464 | tf_op jit(solution)/shard_map/ppermute | solution.py:26
  23.7 0.0 collective-permute-start.2
  23.7 5.4 %collective-permute-done.7.refs_1_.refs_10_.refs_5_.refs_9_ = bf16[1040,256]{1,0:T(8,128)(2,1)S(1)} collective-permute-done((bf16[1040,256]{1,0:T(8,128)(2,1)S(1)}, bf16[1040,256]{1,0:T(8,128)(2,1)S(1)}, u32[]{:S(2)}, u32[]{:S(2)}) %collective-permute-start.7) | collective-permute-done | bytes 532512 | tf_op jit(solution)/shard_map/ppermute | solution.py:22
  29.1 1.2 %collective-permute-start.10 = (bf16[1040,256]{1,0:T(8,128)(2,1)S(1)}, bf16[1040,256]{1,0:T(8,128)(2,1)S(1)}, u32[]{:S(2)}, u32[]{:S(2)}) collective-permute-start(bf16[1040,256]{1,0:T(8,128)(2,1)S(1)} %collective-permute-done.7.refs_1_.refs_10_.refs_5_.refs_9_), channel_id=1, source_target_pairs={{0,1},{1,3},{3,2},{2,0},{4,5},{5,7},{7,6},{6,4},{8,9},{9,11},{11,1... | collective-permute-start | bytes 1597448 | tf_op jit(solution)/shard_map/ppermute | solution.py:22
  30.3 10.1 %collective-permute-done.8.refs_0_.refs_7_.refs_2_.refs_6_ = bf16[128,2048]{1,0:T(8,128)(2,1)S(1)} collective-permute-done((bf16[128,2048]{1,0:T(8,128)(2,1)S(1)}, bf16[128,2048]{1,0:T(8,128)(2,1)S(1)}, u32[]{:S(2)}, u32[]{:S(2)}) %collective-permute-start.8) | collective-permute-done | bytes 524320 | tf_op jit(solution)/shard_map/ppermute | solution.py:22
  40.4 1.2 %collective-permute-start.9 = (bf16[128,2048]{1,0:T(8,128)(2,1)S(1)}, bf16[128,2048]{1,0:T(8,128)(2,1)S(1)}, u32[]{:S(2)}, u32[]{:S(2)}) collective-permute-start(bf16[128,2048]{1,0:T(8,128)(2,1)S(1)} %collective-permute-done.8.refs_0_.refs_7_.refs_2_.refs_6_), channel_id=1, source_target_pairs={{0,1},{1,3},{3,2},{2,0},{4,5},{5,7},{7,6},{6,4},{8,9},{9,11},{11,1... | collective-permute-start | bytes 1572872 | tf_op jit(solution)/shard_map/ppermute | solution.py:22
  41.5 0.0 copy-done.2
  41.5 1.5 %collective-permute-start.4 = (bf16[96,2048]{1,0:T(8,128)(2,1)S(1)}, bf16[96,2048]{1,0:T(8,128)(2,1)S(1)}, u32[]{:S(2)}, u32[]{:S(2)}) collective-permute-start(bf16[96,2048]{1,0:T(8,128)(2,1)S(1)} %bitcast.19), channel_id=1, source_target_pairs={{0,8},{4,12},{8,0},{12,4},{1,9},{5,13},{9,1},{13,5},{2,10},{6,14},... | collective-permute-start | bytes 1179656 | tf_op jit(solution)/shard_map/ppermute | solution.py:26
  43.0 7.0 %collective-permute-done.4.refs_8_.refs_3_ = bf16[96,2048]{1,0:T(8,128)(2,1)S(1)} collective-permute-done((bf16[96,2048]{1,0:T(8,128)(2,1)S(1)}, bf16[96,2048]{1,0:T(8,128)(2,1)S(1)}, u32[]{:S(2)}, u32[]{:S(2)}) %collective-permute-start.4) | collective-permute-done | bytes 393248 | tf_op jit(solution)/shard_map/ppermute | solution.py:26
  50.1 0.0 collective-permute-start.3
  50.1 0.0 collective-permute-done.refs_3_.refs_2_.refs_1_
  50.1 0.5 collective-permute-start.5
  50.6 1.2 %collective-permute-done.10.refs_1_.refs_11_.refs_6_.refs_10_ = bf16[1040,256]{1,0:T(8,128)(2,1)S(1)} collective-permute-done((bf16[1040,256]{1,0:T(8,128)(2,1)S(1)}, bf16[1040,256]{1,0:T(8,128)(2,1)S(1)}, u32[]{:S(2)}, u32[]{:S(2)}) %collective-permute-start.10) | collective-permute-done | bytes 532512 | tf_op jit(solution)/shard_map/ppermute | solution.py:22
  51.8 2.2 %collective-permute-start.11 = (bf16[1040,256]{1,0:T(8,128)(2,1)S(1)}, bf16[1040,256]{1,0:T(8,128)(2,1)S(1)}, u32[]{:S(2)}, u32[]{:S(2)}) collective-permute-start(bf16[1040,256]{1,0:T(8,128)(2,1)S(1)} %collective-permute-done.10.refs_1_.refs_11_.refs_6_.refs_10_), channel_id=1, source_target_pairs={{0,1},{1,3},{3,2},{2,0},{4,5},{5,7},{7,6},{6,4},{8,9},{9,11},{11,1... | collective-permute-start | bytes 1597448 | tf_op jit(solution)/shard_map/ppermute | solution.py:22
  54.0 9.0 %collective-permute-done.9.refs_0_.refs_8_.refs_3_.refs_7_ = bf16[128,2048]{1,0:T(8,128)(2,1)S(1)} collective-permute-done((bf16[128,2048]{1,0:T(8,128)(2,1)S(1)}, bf16[128,2048]{1,0:T(8,128)(2,1)S(1)}, u32[]{:S(2)}, u32[]{:S(2)}) %collective-permute-start.9) | collective-permute-done | bytes 524320 | tf_op jit(solution)/shard_map/ppermute | solution.py:22
  63.0 0.0 collective-permute-done.2.refs_5_.refs_4_.refs_3_
  63.0 1.0 shard_map.88.refs_0_
  64.0 0.0 collective-permute-done.3.refs_7_.refs_2_
  64.0 0.0 collective-permute-done.5.refs_9_.refs_4_
  64.0 2.2 %shard_map.87 = (bf16[768,128]{1,0:T(8,128)(2,1)S(1)}, bf16[384,128]{1,0:T(8,128)(2,1)S(1)}, bf16[128,2048]{1,0:T(8,128)(2,1)S(1)}) custom-call(bf16[128,2048]{1,0:T(8,128)(2,1)S(1)} %collective-permute-done.8.refs_0_.refs_7_.refs_2_.refs_6_, bf16[1040,256]{1,0:T(8,128)(2,1)S(1)} %collective-permute-done.10.refs_1_.refs_11_.refs_6_.refs_10_, ...), custom_call_target="tpu_custom_call" | custom-call | flops 2000000000 | tf_op jit(solution)/shard_map/pallas_call | solution.py:41
  66.2 0.0 copy-start
  66.2 1.2 %collective-permute-start.16 = (bf16[128,2048]{1,0:T(8,128)(2,1)S(1)}, bf16[128,2048]{1,0:T(8,128)(2,1)S(1)}, u32[]{:S(2)}, u32[]{:S(2)}) collective-permute-start(bf16[128,2048]{1,0:T(8,128)(2,1)S(1)} %get-tuple-element.56), channel_id=1, source_target_pairs={{0,1},{1,3},{3,2},{2,0},{4,5},{5,7},{7,6},{6,4},{8,9},{9,11},{11,1... | collective-permute-start | bytes 1572872 | tf_op jit(solution)/shard_map/ppermute | solution.py:22
  67.4 2.2 %shard_map.86 = (bf16[768,128]{1,0:T(8,128)(2,1)S(1)}, bf16[384,128]{1,0:T(8,128)(2,1)S(1)}, bf16[128,2048]{1,0:T(8,128)(2,1)S(1)}) custom-call(bf16[128,2048]{1,0:T(8,128)(2,1)S(1)} %collective-permute-done.6.refs_0_.refs_6_.refs_1_.refs_5_, bf16[1040,256]{1,0:T(8,128)(2,1)S(1)} %collective-permute-done.7.refs_1_.refs_10_.refs_5_.refs_9_, ...), custom_call_target="tpu_custom_call" | custom-call | flops 2000000000 | tf_op jit(solution)/shard_map/pallas_call | solution.py:41
  69.7 0.0 copy-done
  69.7 2.2 %shard_map.85 = (bf16[768,128]{1,0:T(8,128)(2,1)S(1)}, bf16[384,128]{1,0:T(8,128)(2,1)S(1)}, bf16[128,2048]{1,0:T(8,128)(2,1)S(1)}) custom-call(bf16[128,2048]{1,0:T(8,128)(2,1)S(1)} %copy-done, bf16[1040,256]{1,0:T(8,128)(2,1)S(1)} %pad_maximum_fusion.refs_1_.refs_9_.refs_4_.refs_8_, bf16[192,2048]{1,0:T(8,128)(2,1)S(1)} %bitcast.17, ...), custom_call_target="tpu_custom_call" | custom-call | flops 2000000000 | tf_op jit(solution)/shard_map/pallas_call | solution.py:41
  71.9 2.5 %collective-permute-done.11.refs_12_.refs_7_.refs_11_ = bf16[1040,256]{1,0:T(8,128)(2,1)S(1)} collective-permute-done((bf16[1040,256]{1,0:T(8,128)(2,1)S(1)}, bf16[1040,256]{1,0:T(8,128)(2,1)S(1)}, u32[]{:S(2)}, u32[]{:S(2)}) %collective-permute-start.11) | collective-permute-done | bytes 532512 | tf_op jit(solution)/shard_map/ppermute | solution.py:22
  74.4 1.6 %shard_map.89 = (bf16[768,128]{1,0:T(8,128)(2,1)S(1)}, bf16[384,128]{1,0:T(8,128)(2,1)S(1)}, bf16[96,2048]{1,0:T(8,128)(2,1)S(1)}, bf16[96,2048]{1,0:T(8,128)(2,1)S(1)}, bf16[96,2048]{1,0:T(8,128)(2,1)S(1)}) custom-call(f32[768,128]{1,0:T(8,128)S(1)} %shard_map.88.refs_0_, bf16[96,2048]{1,0:T(8,128)(2,1)S(1)} %bitcast.24, ...), custom_call_target="tpu_custom_call" | custom-call | flops 1000000000 | tf_op jit(solution)/shard_map/pallas_call | solution.py:41
  76.0 0.1 collective-permute-start.12
  76.1 0.5 collective-permute-start.13
  76.6 0.1 collective-permute-start.14
  76.7 0.9 shard_map.90.refs_0_
  77.6 0.2 collective-permute-done.12.refs_1_
  77.8 0.6 collective-permute-done.13.refs_2_
  78.4 0.6 collective-permute-done.14.refs_3_
  78.9 0.3 shard_map.91
  79.2 1.9 %collective-permute-start.18 = (bf16[288,2048]{1,0:T(8,128)(2,1)S(1)}, bf16[288,2048]{1,0:T(8,128)(2,1)S(1)}, u32[]{:S(2)}, u32[]{:S(2)}) collective-permute-start(bf16[288,2048]{1,0:T(8,128)(2,1)S(1)} %shard_map.91), channel_id=1, source_target_pairs={{0,8},{4,12},{8,0},{12,4},{1,9},{5,13},{9,1},{13,5},{2,10},{6,14},... | collective-permute-start | bytes 3538952 | tf_op jit(solution)/shard_map/ppermute | solution.py:26
  81.2 1.7 %collective-permute-start.15 = (bf16[128,2048]{1,0:T(8,128)(2,1)S(1)}, bf16[128,2048]{1,0:T(8,128)(2,1)S(1)}, u32[]{:S(2)}, u32[]{:S(2)}) collective-permute-start(bf16[128,2048]{1,0:T(8,128)(2,1)S(1)} %get-tuple-element.54), channel_id=1, source_target_pairs={{0,2},{1,0},{3,1},{2,3},{4,6},{5,4},{7,5},{6,7},{8,10},{9,8},{11,9... | collective-permute-start | bytes 1572872 | tf_op jit(solution)/shard_map/ppermute | solution.py:22
  82.8 2.3 %shard_map.92 = (bf16[128,2048]{1,0:T(8,128)(2,1)S(1)}, bf16[288,2048]{1,0:T(8,128)(2,1)S(1)}, bf16[288,2048]{1,0:T(8,128)(2,1)S(1)}) custom-call(bf16[192,2048]{1,0:T(8,128)(2,1)S(1)} %bitcast.18, bf16[192,2048]{1,0:T(8,128)(2,1)S(1)} %collective-permute-done.refs_3_.refs_2_.refs_1_, bf16[192,2048]{1,0:T(8,128)(2,1)S(1)} %collective-permute-done.1.refs_4_.refs_3_.refs_2_, ...), custom_call_target="tpu_custom_call" | custom-call | flops 2000000000 | tf_op jit(solution)/shard_map/pallas_call | solution.py:41
  85.1 0.1 collective-permute-start.19
  85.2 0.0 collective-permute-done.16.refs_0_
  85.2 0.1 shard_map.93
  85.3 12.7 %collective-permute-start.17 = (bf16[128,2048]{1,0:T(8,128)(2,1)S(1)}, bf16[128,2048]{1,0:T(8,128)(2,1)S(1)}, u32[]{:S(2)}, u32[]{:S(2)}) collective-permute-start(bf16[128,2048]{1,0:T(8,128)(2,1)S(1)} %shard_map.93), channel_id=1, source_target_pairs={{0,1},{1,3},{3,2},{2,0},{4,5},{5,7},{7,6},{6,4},{8,9},{9,11},{11,1... | collective-permute-start | bytes 1572872 | tf_op jit(solution)/shard_map/ppermute | solution.py:22
  98.0 0.0 collective-permute-done.15.refs_1_
  98.0 10.4 %collective-permute-done.17.refs_2_ = bf16[128,2048]{1,0:T(8,128)(2,1)S(1)} collective-permute-done((bf16[128,2048]{1,0:T(8,128)(2,1)S(1)}, bf16[128,2048]{1,0:T(8,128)(2,1)S(1)}, u32[]{:S(2)}, u32[]{:S(2)}) %collective-permute-start.17) | collective-permute-done | bytes 524320 | tf_op jit(solution)/shard_map/ppermute | solution.py:22
  108.5 0.0 collective-permute-done.19.refs_5_
  108.5 0.0 collective-permute-done.18.refs_4_
  108.5 1.8 %shard_map.94 = (bf16[128,2048]{1,0:T(8,128)(2,1)}, f32[192,2048]{1,0:T(8,128)}, f32[96,2048]{1,0:T(8,128)}) custom-call(bf16[128,2048]{1,0:T(8,128)(2,1)S(1)} %get-tuple-element.41.refs_0_, bf16[128,2048]{1,0:T(8,128)(2,1)S(1)} %collective-permute-done.15.refs_1_, bf16[128,2048]{1,0:T(8,128)(2,1)S(1)} %collective-permute-done.17.refs_2_, ...), custom_call_target="tpu_custom_call" | custom-call | flops 2000000000 | tf_op jit(solution)/shard_map/pallas_call | solution.py:164
  (4 shorter events, 0.1 us)
Async XLA Ops:
  0.6 18.3 %copy-start.1 = (bf16[1,2,96,2048]{3,2,1,0:T(8,128)(2,1)S(1)}, bf16[1,2,96,2048]{3,2,1,0:T(8,128)(2,1)}, u32[]{:S(2)}) copy-start(bf16[1,2,96,2048]{3,2,1,0:T(8,128)(2,1)} %param.12) | copy-start | bytes 2359300
  0.6 40.9 %copy-start.2 = (bf16[1,96,2048]{2,1,0:T(8,128)(2,1)S(1)}, bf16[1,96,2048]{2,1,0:T(8,128)(2,1)}, u32[]{:S(2)}) copy-start(bf16[1,96,2048]{2,1,0:T(8,128)(2,1)} %param.13) | copy-start | bytes 1179652
  0.7 17.1 %collective-permute-start.6 = (bf16[128,2048]{1,0:T(8,128)(2,1)}, bf16[128,2048]{1,0:T(8,128)(2,1)S(1)}, u32[]{:S(2)}, u32[]{:S(2)}) collective-permute-start(bf16[128,2048]{1,0:T(8,128)(2,1)} %refs_4_.1), channel_id=1, source_target_pairs={{0,1},{1,3},{3,2},{2,0},{4,5},{5,7},{7,6},{6,4},{8,9},{9,11},{11,1... | collective-permute-start | bytes 1572872 | tf_op jit(solution)/shard_map/ppermute | solution.py:22
  4.5 19.2 %collective-permute-start.1 = (bf16[192,2048]{1,0:T(8,128)(2,1)}, bf16[192,2048]{1,0:T(8,128)(2,1)S(1)}, u32[]{:S(2)}, u32[]{:S(2)}) collective-permute-start(bf16[192,2048]{1,0:T(8,128)(2,1)} %bitcast.12), channel_id=1, source_target_pairs={{0,8},{4,12},{8,0},{12,4},{1,9},{5,13},{9,1},{13,5},{2,10},{6,14},... | collective-permute-start | bytes 2359304 | tf_op jit(solution)/shard_map/ppermute | solution.py:26
  7.2 22.0 %collective-permute-start.7 = (bf16[1040,256]{1,0:T(8,128)(2,1)S(1)}, bf16[1040,256]{1,0:T(8,128)(2,1)S(1)}, u32[]{:S(2)}, u32[]{:S(2)}) collective-permute-start(bf16[1040,256]{1,0:T(8,128)(2,1)S(1)} %pad_maximum_fusion.refs_1_.refs_9_.refs_4_.refs_8_), channel_id=1, source_target_pairs={{0,1},{1,3},{3,2},{2,0},{4,5},{5,7},{7,6},{6,4},{8,9},{9,11},{11,1... | collective-permute-start | bytes 1597448 | tf_op jit(solution)/shard_map/ppermute | solution.py:22
  17.7 22.6 %collective-permute-start.8 = (bf16[128,2048]{1,0:T(8,128)(2,1)S(1)}, bf16[128,2048]{1,0:T(8,128)(2,1)S(1)}, u32[]{:S(2)}, u32[]{:S(2)}) collective-permute-start(bf16[128,2048]{1,0:T(8,128)(2,1)S(1)} %collective-permute-done.6.refs_0_.refs_6_.refs_1_.refs_5_), channel_id=1, source_target_pairs={{0,1},{1,3},{3,2},{2,0},{4,5},{5,7},{7,6},{6,4},{8,9},{9,11},{11,1... | collective-permute-start | bytes 1572872 | tf_op jit(solution)/shard_map/ppermute | solution.py:22
  19.0 31.1 %collective-permute-start = (bf16[192,2048]{1,0:T(8,128)(2,1)S(1)}, bf16[192,2048]{1,0:T(8,128)(2,1)S(1)}, u32[]{:S(2)}, u32[]{:S(2)}) collective-permute-start(bf16[192,2048]{1,0:T(8,128)(2,1)S(1)} %bitcast.13), channel_id=1, source_target_pairs={{0,4},{4,0},{8,12},{12,8},{1,5},{5,1},{9,13},{13,9},{2,6},{6,2},{1... | collective-permute-start | bytes 2359304 | tf_op jit(solution)/shard_map/ppermute | solution.py:26
  23.7 39.3 %collective-permute-start.2 = (bf16[192,2048]{1,0:T(8,128)(2,1)S(1)}, bf16[192,2048]{1,0:T(8,128)(2,1)S(1)}, u32[]{:S(2)}, u32[]{:S(2)}) collective-permute-start(bf16[192,2048]{1,0:T(8,128)(2,1)S(1)} %collective-permute-done.1.refs_4_.refs_3_.refs_2_), channel_id=1, source_target_pairs={{0,4},{4,0},{8,12},{12,8},{1,5},{5,1},{9,13},{13,9},{2,6},{6,2},{1... | collective-permute-start | bytes 2359304 | tf_op jit(solution)/shard_map/ppermute | solution.py:26
  29.1 22.6 %collective-permute-start.10 = (bf16[1040,256]{1,0:T(8,128)(2,1)S(1)}, bf16[1040,256]{1,0:T(8,128)(2,1)S(1)}, u32[]{:S(2)}, u32[]{:S(2)}) collective-permute-start(bf16[1040,256]{1,0:T(8,128)(2,1)S(1)} %collective-permute-done.7.refs_1_.refs_10_.refs_5_.refs_9_), channel_id=1, source_target_pairs={{0,1},{1,3},{3,2},{2,0},{4,5},{5,7},{7,6},{6,4},{8,9},{9,11},{11,1... | collective-permute-start | bytes 1597448 | tf_op jit(solution)/shard_map/ppermute | solution.py:22
  40.4 22.6 %collective-permute-start.9 = (bf16[128,2048]{1,0:T(8,128)(2,1)S(1)}, bf16[128,2048]{1,0:T(8,128)(2,1)S(1)}, u32[]{:S(2)}, u32[]{:S(2)}) collective-permute-start(bf16[128,2048]{1,0:T(8,128)(2,1)S(1)} %collective-permute-done.8.refs_0_.refs_7_.refs_2_.refs_6_), channel_id=1, source_target_pairs={{0,1},{1,3},{3,2},{2,0},{4,5},{5,7},{7,6},{6,4},{8,9},{9,11},{11,1... | collective-permute-start | bytes 1572872 | tf_op jit(solution)/shard_map/ppermute | solution.py:22
  41.5 8.6 %collective-permute-start.4 = (bf16[96,2048]{1,0:T(8,128)(2,1)S(1)}, bf16[96,2048]{1,0:T(8,128)(2,1)S(1)}, u32[]{:S(2)}, u32[]{:S(2)}) collective-permute-start(bf16[96,2048]{1,0:T(8,128)(2,1)S(1)} %bitcast.19), channel_id=1, source_target_pairs={{0,8},{4,12},{8,0},{12,4},{1,9},{5,13},{9,1},{13,5},{2,10},{6,14},... | collective-permute-start | bytes 1179656 | tf_op jit(solution)/shard_map/ppermute | solution.py:26
  50.1 13.9 %collective-permute-start.3 = (bf16[96,2048]{1,0:T(8,128)(2,1)S(1)}, bf16[96,2048]{1,0:T(8,128)(2,1)S(1)}, u32[]{:S(2)}, u32[]{:S(2)}) collective-permute-start(bf16[96,2048]{1,0:T(8,128)(2,1)S(1)} %bitcast.20), channel_id=1, source_target_pairs={{0,4},{4,0},{8,12},{12,8},{1,5},{5,1},{9,13},{13,9},{2,6},{6,2},{1... | collective-permute-start | bytes 1179656 | tf_op jit(solution)/shard_map/ppermute | solution.py:26
  50.1 13.9 %collective-permute-start.5 = (bf16[96,2048]{1,0:T(8,128)(2,1)S(1)}, bf16[96,2048]{1,0:T(8,128)(2,1)S(1)}, u32[]{:S(2)}, u32[]{:S(2)}) collective-permute-start(bf16[96,2048]{1,0:T(8,128)(2,1)S(1)} %collective-permute-done.4.refs_8_.refs_3_), channel_id=1, source_target_pairs={{0,4},{4,0},{8,12},{12,8},{1,5},{5,1},{9,13},{13,9},{2,6},{6,2},{1... | collective-permute-start | bytes 1179656 | tf_op jit(solution)/shard_map/ppermute | solution.py:26
  51.8 22.6 %collective-permute-start.11 = (bf16[1040,256]{1,0:T(8,128)(2,1)S(1)}, bf16[1040,256]{1,0:T(8,128)(2,1)S(1)}, u32[]{:S(2)}, u32[]{:S(2)}) collective-permute-start(bf16[1040,256]{1,0:T(8,128)(2,1)S(1)} %collective-permute-done.10.refs_1_.refs_11_.refs_6_.refs_10_), channel_id=1, source_target_pairs={{0,1},{1,3},{3,2},{2,0},{4,5},{5,7},{7,6},{6,4},{8,9},{9,11},{11,1... | collective-permute-start | bytes 1597448 | tf_op jit(solution)/shard_map/ppermute | solution.py:22
  66.2 3.5 %copy-start = (bf16[128,2048]{1,0:T(8,128)(2,1)S(1)}, bf16[128,2048]{1,0:T(8,128)(2,1)}, u32[]{:S(2)}) copy-start(bf16[128,2048]{1,0:T(8,128)(2,1)} %refs_4_.1) | copy-start | bytes 1572868
  66.2 18.9 %collective-permute-start.16 = (bf16[128,2048]{1,0:T(8,128)(2,1)S(1)}, bf16[128,2048]{1,0:T(8,128)(2,1)S(1)}, u32[]{:S(2)}, u32[]{:S(2)}) collective-permute-start(bf16[128,2048]{1,0:T(8,128)(2,1)S(1)} %get-tuple-element.56), channel_id=1, source_target_pairs={{0,1},{1,3},{3,2},{2,0},{4,5},{5,7},{7,6},{6,4},{8,9},{9,11},{11,1... | collective-permute-start | bytes 1572872 | tf_op jit(solution)/shard_map/ppermute | solution.py:22
  76.0 1.8 %collective-permute-start.12 = (bf16[96,2048]{1,0:T(8,128)(2,1)S(1)}, bf16[96,2048]{1,0:T(8,128)(2,1)S(1)}, u32[]{:S(2)}, u32[]{:S(2)}) collective-permute-start(bf16[96,2048]{1,0:T(8,128)(2,1)S(1)} %get-tuple-element.51), channel_id=1, source_target_pairs={{0,4},{4,0},{8,12},{12,8},{1,5},{5,1},{9,13},{13,9},{2,6},{6,2},{1... | collective-permute-start | bytes 1179656 | tf_op jit(solution)/shard_map/ppermute | solution.py:26
  76.1 2.3 %collective-permute-start.13 = (bf16[96,2048]{1,0:T(8,128)(2,1)S(1)}, bf16[96,2048]{1,0:T(8,128)(2,1)S(1)}, u32[]{:S(2)}, u32[]{:S(2)}) collective-permute-start(bf16[96,2048]{1,0:T(8,128)(2,1)S(1)} %get-tuple-element.52), channel_id=1, source_target_pairs={{0,4},{4,0},{8,12},{12,8},{1,5},{5,1},{9,13},{13,9},{2,6},{6,2},{1... | collective-permute-start | bytes 1179656 | tf_op jit(solution)/shard_map/ppermute | solution.py:26
  76.6 2.3 %collective-permute-start.14 = (bf16[96,2048]{1,0:T(8,128)(2,1)S(1)}, bf16[96,2048]{1,0:T(8,128)(2,1)S(1)}, u32[]{:S(2)}, u32[]{:S(2)}) collective-permute-start(bf16[96,2048]{1,0:T(8,128)(2,1)S(1)} %get-tuple-element.53), channel_id=1, source_target_pairs={{0,4},{4,0},{8,12},{12,8},{1,5},{5,1},{9,13},{13,9},{2,6},{6,2},{1... | collective-permute-start | bytes 1179656 | tf_op jit(solution)/shard_map/ppermute | solution.py:26
  79.2 29.3 %collective-permute-start.18 = (bf16[288,2048]{1,0:T(8,128)(2,1)S(1)}, bf16[288,2048]{1,0:T(8,128)(2,1)S(1)}, u32[]{:S(2)}, u32[]{:S(2)}) collective-permute-start(bf16[288,2048]{1,0:T(8,128)(2,1)S(1)} %shard_map.91), channel_id=1, source_target_pairs={{0,8},{4,12},{8,0},{12,4},{1,9},{5,13},{9,1},{13,5},{2,10},{6,14},... | collective-permute-start | bytes 3538952 | tf_op jit(solution)/shard_map/ppermute | solution.py:26
  81.2 16.9 %collective-permute-start.15 = (bf16[128,2048]{1,0:T(8,128)(2,1)S(1)}, bf16[128,2048]{1,0:T(8,128)(2,1)S(1)}, u32[]{:S(2)}, u32[]{:S(2)}) collective-permute-start(bf16[128,2048]{1,0:T(8,128)(2,1)S(1)} %get-tuple-element.54), channel_id=1, source_target_pairs={{0,2},{1,0},{3,1},{2,3},{4,6},{5,4},{7,5},{6,7},{8,10},{9,8},{11,9... | collective-permute-start | bytes 1572872 | tf_op jit(solution)/shard_map/ppermute | solution.py:22
  85.1 23.4 %collective-permute-start.19 = (bf16[288,2048]{1,0:T(8,128)(2,1)S(1)}, bf16[288,2048]{1,0:T(8,128)(2,1)S(1)}, u32[]{:S(2)}, u32[]{:S(2)}) collective-permute-start(bf16[288,2048]{1,0:T(8,128)(2,1)S(1)} %get-tuple-element.61), channel_id=1, source_target_pairs={{0,4},{4,0},{8,12},{12,8},{1,5},{5,1},{9,13},{13,9},{2,6},{6,2},{1... | collective-permute-start | bytes 3538952 | tf_op jit(solution)/shard_map/ppermute | solution.py:26
  85.3 23.1 %collective-permute-start.17 = (bf16[128,2048]{1,0:T(8,128)(2,1)S(1)}, bf16[128,2048]{1,0:T(8,128)(2,1)S(1)}, u32[]{:S(2)}, u32[]{:S(2)}) collective-permute-start(bf16[128,2048]{1,0:T(8,128)(2,1)S(1)} %shard_map.93), channel_id=1, source_target_pairs={{0,1},{1,3},{3,2},{2,0},{4,5},{5,7},{7,6},{6,4},{8,9},{9,11},{11,1... | collective-permute-start | bytes 1572872 | tf_op jit(solution)/shard_map/ppermute | solution.py:22

commit v6 on v5

--- a/solution.py
+++ b/solution.py
@@ -85,7 +85,7 @@
         cols = slice(at, at + step)
         total = None
         for k, block in enumerate(gate_up):
-            term = dot_tn(both[k * wide2 : (k + 1) * wide2, :], block[:, cols])
+            term = dot_tn(rows_of(both, k, wide2), block[:, cols])
             total = term if total is None else total + term
         contrib[:, cols] = total.astype(BF16)
 
@@ -96,8 +96,8 @@
     for k in ks:
         mine, outs = (outs[:3], outs[3:]) if k in split else (outs[:1], outs[1:])
         wide = sum(o.shape[0] for o in mine) // 3
-        left_x = jnp.concatenate([a[2 * k * wide : 2 * (k + 1) * wide, :] for a in both], axis=1)
-        left_dy = jnp.concatenate([a[k * wide : (k + 1) * wide, :] for a in hid], axis=1)
+        left_x = jnp.concatenate([rows_of(a, k, 2 * wide) for a in both], axis=1)
+        left_dy = jnp.concatenate([rows_of(a, k, wide) for a in hid], axis=1)
         for n in range(width // block):
             cols = slice(n * block, (n + 1) * block)
             right_x = jnp.concatenate([x[:, cols] for x in xs], axis=0)
@@ -142,13 +142,16 @@
     copies, first = [], [0, 0]
     for n, (out, buffer) in enumerate(zip(outs, held)):
         group = min(n, 1)
-        rows = out.shape[0] // 2
-        for at in (0, rows):
-            total = None
-            for ref in groups[group]:
-                term = ref[first[group] : first[group] + rows, :].astype(F32)
-                total = term if total is None else total + term
-            buffer[at : at + rows, :] = total.astype(buffer.dtype)
+        height = out.shape[0]
+        rows = height // 4 if height % 64 == 0 else height // 2
+        for at in range(0, height, rows):
+            step = 16 if rows % 16 == 0 else rows
+            for low in range(0, rows, step):
+                total = None
+                for ref in groups[group]:
+                    term = ref[first[group] + low : first[group] + low + step, :].astype(F32)
+                    total = term if total is None else total + term
+                buffer[at + low : at + low + step, :] = total.astype(buffer.dtype)
             copy = pltpu.make_async_copy(
                 buffer.at[at : at + rows, :], out.at[at : at + rows, :], sems.at[len(copies)]
             )
@@ -168,7 +171,7 @@
         out_specs=[pl.BlockSpec(memory_space=pl.ANY)] * len(outs),
         scratch_shapes=[
             *[pltpu.VMEM(o.shape, o.dtype) for o in outs],
-            pltpu.SemaphoreType.DMA((2 * len(outs),)),
+            pltpu.SemaphoreType.DMA((4 * len(outs),)),
         ],
         compiler_params=pltpu.CompilerParams(vmem_limit_bytes=40 * 1024 * 1024),
         cost_estimate=pl.CostEstimate(flops=int(cost * 1e9), bytes_accessed=0, transcendentals=0),
@@ -196,6 +199,15 @@
     return [
         packed[k // per : k // per + 1, k % per * rows : (k % per + 1) * rows] for k in range(experts)
     ]
+
+
+def rows_of(terms, k, size):
+    if not isinstance(terms, tuple):
+        return terms[k * size : (k + 1) * size, :]
+    rest, some, names = terms
+    if k in names:
+        return rows_of(some, names.index(k), size)
+    return rows_of(rest, k - sum(n < k for n in names), size)
 
 
 def back_of(down, dyp, rows):
@@ -228,32 +240,48 @@
         acts[2 * k * wide : 2 * (k + 1) * wide, :] = dot_nt(gate_up[k][...], x[...])
 
 
-def far_kernel(experts, slabs, ks, split, *refs):
-    (acts,), down, xs, dys, both, hid, outs = spread(
-        refs, 1, experts, slabs, slabs, slabs - 1, slabs - 1
-    )
-    (last, last_hid), grads = spread(outs, 2)
-    rows, wide = xs[0].shape[0], down[0].shape[0]
-    weights = weights_of(dys[-1], experts, rows, down[0].shape[1])
-    for k in range(experts):
-        back = back_of(down[k], dys[-1], rows)
+def put_last(ks, experts, rows, acts, down, dy, both, hid):
+    wide = down[0].shape[0]
+    weights = weights_of(dy, experts, rows, down[0].shape[1])
+    for n, k in enumerate(ks):
+        back = back_of(down[n], dy, rows)
         gate_act = acts[2 * k * wide : (2 * k + 1) * wide, :]
         up_act = acts[(2 * k + 1) * wide : (2 * k + 2) * wide, :]
         gate_grad, up_grad, weighted = grads_of(gate_act, up_act, back, weights[k])
-        last[2 * k * wide : (2 * k + 1) * wide, :] = gate_grad
-        last[(2 * k + 1) * wide : (2 * k + 2) * wide, :] = up_grad
-        last_hid[k * wide : (k + 1) * wide, :] = weighted
-    put_weight_grads(ks, split, xs, dys, (*both, last), (*hid, last_hid), grads)
-
-
-def grads_kernel(slabs, ks, *refs):
-    xs, dys, both, hid, grads = spread(refs, slabs, slabs, slabs, slabs)
-    put_weight_grads(ks, (), xs, dys, both, hid, grads)
-
-
-def near_kernel(experts, slabs, ks, *refs):
-    gate_up, xs, dys, both, hid, outs = spread(refs, experts, slabs, slabs, slabs, slabs)
+        both[2 * n * wide : (2 * n + 1) * wide, :] = gate_grad
+        both[(2 * n + 1) * wide : (2 * n + 2) * wide, :] = up_grad
+        hid[n * wide : (n + 1) * wide, :] = weighted
+
+
+def far_kernel(experts, slabs, split, *refs):
+    (acts,), down, xs, dys, both, hid, outs = spread(
+        refs, 1, len(split), slabs, slabs, slabs - 1, slabs - 1
+    )
+    (last, last_hid), grads = spread(outs, 2)
+    put_last(split, experts, xs[0].shape[0], acts, down, dys[-1], last, last_hid)
+    put_weight_grads(
+        split, split, xs, dys,
+        (*both, (None, last, split)), (*hid, (None, last_hid, split)), grads,
+    )
+
+
+def rest_kernel(experts, slabs, ks, rest, *refs):
+    (acts,), down, xs, dys, both, hid, outs = spread(
+        refs, 1, len(rest), slabs, slabs, slabs - 1, slabs - 1
+    )
+    (last, last_hid), grads = spread(outs, 2)
+    put_last(rest, experts, xs[0].shape[0], acts, down, dys[-1], last, last_hid)
+    names = tuple(k for k in range(experts) if k not in rest)
+    put_weight_grads(
+        ks, (), xs, dys, (*both, (last, None, names)), (*hid, (last_hid, None, names)), grads
+    )
+
+
+def near_kernel(experts, slabs, ks, split, *refs):
+    gate_up, xs, dys, both, hid, outs = spread(refs, experts, slabs, slabs, slabs + 1, slabs + 1)
     (contrib,), grads = spread(outs, 1)
+    both = (*both[:-2], (both[-2], both[-1], split))
+    hid = (*hid[:-2], (hid[-2], hid[-1], split))
     put_weight_grads(ks, (), xs, dys, both, hid, grads)
     put_contrib(both[-1], gate_up, contrib)
 
@@ -305,33 +333,31 @@
 
     far = tuple(range(experts // 2, experts))[::-1]
     near = tuple(range(experts // 2))[::-1]
-    split = tuple(k for k in far if k % 2)
+    split = tuple(k for k in range(experts // 2, experts) if k % 2)
     even = tuple(k for k in far if not k % 2)
+    rest = tuple(k for k in range(experts) if k not in split)
     whole, third = shape(3 * wide, width), shape(wide, width)
+
+    def last_terms(ks):
+        return shape(2 * len(ks) * wide, rows), shape(len(ks) * wide, rows)
+
     b, h, *got_split = call(
-        functools.partial(far_kernel, experts, slabs, split, split),
-        (shape(2 * units, rows), shape(units, rows), *[third] * (3 * len(split))),
-        acts, *down, *xs, *dys, *both, *hid,
+        functools.partial(far_kernel, experts, slabs, split),
+        (*last_terms(split), *[third] * (3 * len(split))),
+        acts, *(down[k] for k in split), *xs, *dys, *both, *hid,
         cost=COSTS["far"],
     )
-    both.append(b)
-    hid.append(h)
-    got_even = call(
-        functools.partial(grads_kernel, slabs, even),
-        [whole] * len(even),
-        *xs, *dys, *both, *hid,
+    b_rest, h_rest, *got_even = call(
+        functools.partial(rest_kernel, experts, slabs, even, rest),
+        (*last_terms(rest), *[whole] * len(even)),
+        acts, *(down[k] for k in rest), *xs, *dys, *both, *hid,
         cost=COSTS["even"],
     )
-    got_far = []
-    for k in far:
-        if k in split:
-            got_far, got_split = [*got_far, *got_split[:3]], got_split[3:]
-        else:
-            got_far, got_even = [*got_far, got_even[0]], got_even[1:]
-    terms = {}
-    for k in far:
-        count = 3 if k in split else 1
-        terms[k], got_far = [tuple(got_far[:count])], got_far[count:]
+    both += [b_rest, b]
+    hid += [h_rest, h]
+    got_split = dict(zip(split, zip(got_split[::3], got_split[1::3], got_split[2::3])))
+    got_even = dict(zip(even, got_even))
+    terms = {k: [got_split[k]] if k in split else [(got_even[k],)] for k in far}
     first_bit, *other_bits = bits_of(experts)
 
     def swap_out(ks, bit):
@@ -349,7 +375,7 @@
         joined.extend(out)
         terms[0] = [(swapped(out[0], other_bits[0]),)]
     c, *got_near = call(
-        functools.partial(near_kernel, experts, slabs, near),
+        functools.partial(near_kernel, experts, slabs, near, split),
         (shape(rows, width), *[whole] * len(near)),
         *gate_up, *xs, *dys, *both[:-1], after(both[-1], *joined), *hid,
         cost=COSTS["near"],

time: 111 us -> 111 us (level)
  transfers between devices with their start and end apart: 20 -> 20, of which waited for: 12 -> 10; matrix products, arithmetic and copies ran while one was open for 2% -> 2% of each run, Pallas kernels for 12% -> 12%
where the time goes in v6:
time: 111 us; the launch traced here: 110 us
  waiting for transfers between devices  58.9 us (53%)
  starting transfers between devices  33.6 us (30%)
  Pallas kernels  15 us (14%)
  local copies, waits for them, and re-layouts  1.11 us (1%)
    ppermute x9, waiting for transfers between devices, onward(): return lax.ppermute(block, 'dp', ring_pairs(lax.axis_size('dp'), turns))  46.6 us
    ppermute x9, starting transfers between devices, onward(): return lax.ppermute(block, 'dp', ring_pairs(lax.axis_size('dp'), turns))  27.3 us
    pallas_call x9, Pallas kernels, call(): pl.pallas_call(kernel, out_shape=list(outs), in_specs=[pl.BlockSpec(memor...  13.3 us
    ppermute x11, waiting for transfers between devices, swapped(): lax.ppermute(block, 'expert', [(i, i ^ bit) for i in range(lax.axis_size(...  12.3 us
    ppermute x11, starting transfers between devices, swapped(): lax.ppermute(block, 'expert', [(i, i ^ bit) for i in range(lax.axis_size(...  6.22 us
  transfers between devices with their start and end apart: 20, of which 10 were waited for; matrix products, arithmetic and copies ran while one was open for 2% of the time, Pallas kernels for 12%

profile of v6, /device:TPU:0, one launch (start us, length us, event | category | flops | bytes accessed | tf_op | source)
XLA Modules:
  0.0 110.4 jit_solution(1882171889622850291)
XLA Ops:
  0.6 0.0 copy-start.1
  0.6 0.0 copy-start.2
  0.7 3.1 %collective-permute-start.6 = (bf16[128,2048]{1,0:T(8,128)(2,1)}, bf16[128,2048]{1,0:T(8,128)(2,1)S(1)}, u32[]{:S(2)}, u32[]{:S(2)}) collective-permute-start(bf16[128,2048]{1,0:T(8,128)(2,1)} %refs_4_.3), channel_id=1, source_target_pairs={{0,1},{1,3},{3,2},{2,0},{4,5},{5,7},{7,6},{6,4},{8,9},{9,11},{11,1... | collective-permute-start | bytes 1572872 | tf_op jit(solution)/shard_map/ppermute | solution.py:22
  3.7 0.8 fusion
  4.5 1.5 %collective-permute-start.1 = (bf16[192,2048]{1,0:T(8,128)(2,1)}, bf16[192,2048]{1,0:T(8,128)(2,1)S(1)}, u32[]{:S(2)}, u32[]{:S(2)}) collective-permute-start(bf16[192,2048]{1,0:T(8,128)(2,1)} %bitcast.12), channel_id=1, source_target_pairs={{0,8},{4,12},{8,0},{12,4},{1,9},{5,13},{9,1},{13,5},{2,10},{6,14},... | collective-permute-start | bytes 2359304 | tf_op jit(solution)/shard_map/ppermute | solution.py:26
  6.0 1.1 copy.15
  7.2 2.6 %collective-permute-start.7 = (bf16[1040,256]{1,0:T(8,128)(2,1)S(1)}, bf16[1040,256]{1,0:T(8,128)(2,1)S(1)}, u32[]{:S(2)}, u32[]{:S(2)}) collective-permute-start(bf16[1040,256]{1,0:T(8,128)(2,1)S(1)} %pad_maximum_fusion.refs_1_.refs_8_.refs_6_), channel_id=1, source_target_pairs={{0,1},{1,3},{3,2},{2,0},{4,5},{5,7},{7,6},{6,4},{8,9},{9,11},{11,1... | collective-permute-start | bytes 1597448 | tf_op jit(solution)/shard_map/ppermute | solution.py:22
  9.8 7.9 %collective-permute-done.6.refs_0_.refs_5_.refs_3_ = bf16[128,2048]{1,0:T(8,128)(2,1)S(1)} collective-permute-done((bf16[128,2048]{1,0:T(8,128)(2,1)}, bf16[128,2048]{1,0:T(8,128)(2,1)S(1)}, u32[]{:S(2)}, u32[]{:S(2)}) %collective-permute-start.6) | collective-permute-done | bytes 524320 | tf_op jit(solution)/shard_map/ppermute | solution.py:22
  17.7 1.3 %collective-permute-start.8 = (bf16[128,2048]{1,0:T(8,128)(2,1)S(1)}, bf16[128,2048]{1,0:T(8,128)(2,1)S(1)}, u32[]{:S(2)}, u32[]{:S(2)}) collective-permute-start(bf16[128,2048]{1,0:T(8,128)(2,1)S(1)} %collective-permute-done.6.refs_0_.refs_5_.refs_3_), channel_id=1, source_target_pairs={{0,1},{1,3},{3,2},{2,0},{4,5},{5,7},{7,6},{6,4},{8,9},{9,11},{11,1... | collective-permute-start | bytes 1572872 | tf_op jit(solution)/shard_map/ppermute | solution.py:22
  19.0 0.0 copy-done.1
  19.0 0.0 collective-permute-start
  19.0 4.7 %collective-permute-done.1.refs_4_.refs_3_.refs_2_ = bf16[192,2048]{1,0:T(8,128)(2,1)S(1)} collective-permute-done((bf16[192,2048]{1,0:T(8,128)(2,1)}, bf16[192,2048]{1,0:T(8,128)(2,1)S(1)}, u32[]{:S(2)}, u32[]{:S(2)}) %collective-permute-start.1) | collective-permute-done | bytes 786464 | tf_op jit(solution)/shard_map/ppermute | solution.py:26
  23.7 0.0 collective-permute-start.2
  23.7 5.4 %collective-permute-done.7.refs_1_.refs_9_.refs_7_ = bf16[1040,256]{1,0:T(8,128)(2,1)S(1)} collective-permute-done((bf16[1040,256]{1,0:T(8,128)(2,1)S(1)}, bf16[1040,256]{1,0:T(8,128)(2,1)S(1)}, u32[]{:S(2)}, u32[]{:S(2)}) %collective-permute-start.7) | collective-permute-done | bytes 532512 | tf_op jit(solution)/shard_map/ppermute | solution.py:22
  29.1 1.2 %collective-permute-start.10 = (bf16[1040,256]{1,0:T(8,128)(2,1)S(1)}, bf16[1040,256]{1,0:T(8,128)(2,1)S(1)}, u32[]{:S(2)}, u32[]{:S(2)}) collective-permute-start(bf16[1040,256]{1,0:T(8,128)(2,1)S(1)} %collective-permute-done.7.refs_1_.refs_9_.refs_7_), channel_id=1, source_target_pairs={{0,1},{1,3},{3,2},{2,0},{4,5},{5,7},{7,6},{6,4},{8,9},{9,11},{11,1... | collective-permute-start | bytes 1597448 | tf_op jit(solution)/shard_map/ppermute | solution.py:22
  30.3 10.1 %collective-permute-done.8.refs_0_.refs_6_.refs_4_ = bf16[128,2048]{1,0:T(8,128)(2,1)S(1)} collective-permute-done((bf16[128,2048]{1,0:T(8,128)(2,1)S(1)}, bf16[128,2048]{1,0:T(8,128)(2,1)S(1)}, u32[]{:S(2)}, u32[]{:S(2)}) %collective-permute-start.8) | collective-permute-done | bytes 524320 | tf_op jit(solution)/shard_map/ppermute | solution.py:22
  40.4 1.2 %collective-permute-start.9 = (bf16[128,2048]{1,0:T(8,128)(2,1)S(1)}, bf16[128,2048]{1,0:T(8,128)(2,1)S(1)}, u32[]{:S(2)}, u32[]{:S(2)}) collective-permute-start(bf16[128,2048]{1,0:T(8,128)(2,1)S(1)} %collective-permute-done.8.refs_0_.refs_6_.refs_4_), channel_id=1, source_target_pairs={{0,1},{1,3},{3,2},{2,0},{4,5},{5,7},{7,6},{6,4},{8,9},{9,11},{11,1... | collective-permute-start | bytes 1572872 | tf_op jit(solution)/shard_map/ppermute | solution.py:22
  41.5 0.0 copy-done.2
  41.5 1.5 %collective-permute-start.4 = (bf16[96,2048]{1,0:T(8,128)(2,1)S(1)}, bf16[96,2048]{1,0:T(8,128)(2,1)S(1)}, u32[]{:S(2)}, u32[]{:S(2)}) collective-permute-start(bf16[96,2048]{1,0:T(8,128)(2,1)S(1)} %bitcast.19), channel_id=1, source_target_pairs={{0,8},{4,12},{8,0},{12,4},{1,9},{5,13},{9,1},{13,5},{2,10},{6,14},... | collective-permute-start | bytes 1179656 | tf_op jit(solution)/shard_map/ppermute | solution.py:26
  43.0 7.0 %collective-permute-done.4.refs_8_.refs_3_ = bf16[96,2048]{1,0:T(8,128)(2,1)S(1)} collective-permute-done((bf16[96,2048]{1,0:T(8,128)(2,1)S(1)}, bf16[96,2048]{1,0:T(8,128)(2,1)S(1)}, u32[]{:S(2)}, u32[]{:S(2)}) %collective-permute-start.4) | collective-permute-done | bytes 393248 | tf_op jit(solution)/shard_map/ppermute | solution.py:26
  50.1 0.0 collective-permute-start.3
  50.1 0.0 collective-permute-done.refs_3_.refs_2_.refs_1_
  50.1 0.5 collective-permute-start.5
  50.6 1.2 %collective-permute-done.10.refs_1_.refs_10_.refs_8_ = bf16[1040,256]{1,0:T(8,128)(2,1)S(1)} collective-permute-done((bf16[1040,256]{1,0:T(8,128)(2,1)S(1)}, bf16[1040,256]{1,0:T(8,128)(2,1)S(1)}, u32[]{:S(2)}, u32[]{:S(2)}) %collective-permute-start.10) | collective-permute-done | bytes 532512 | tf_op jit(solution)/shard_map/ppermute | solution.py:22
  51.8 2.2 %collective-permute-start.11 = (bf16[1040,256]{1,0:T(8,128)(2,1)S(1)}, bf16[1040,256]{1,0:T(8,128)(2,1)S(1)}, u32[]{:S(2)}, u32[]{:S(2)}) collective-permute-start(bf16[1040,256]{1,0:T(8,128)(2,1)S(1)} %collective-permute-done.10.refs_1_.refs_10_.refs_8_), channel_id=1, source_target_pairs={{0,1},{1,3},{3,2},{2,0},{4,5},{5,7},{7,6},{6,4},{8,9},{9,11},{11,1... | collective-permute-start | bytes 1597448 | tf_op jit(solution)/shard_map/ppermute | solution.py:22
  54.0 9.0 %collective-permute-done.9.refs_0_.refs_7_.refs_5_ = bf16[128,2048]{1,0:T(8,128)(2,1)S(1)} collective-permute-done((bf16[128,2048]{1,0:T(8,128)(2,1)S(1)}, bf16[128,2048]{1,0:T(8,128)(2,1)S(1)}, u32[]{:S(2)}, u32[]{:S(2)}) %collective-permute-start.9) | collective-permute-done | bytes 524320 | tf_op jit(solution)/shard_map/ppermute | solution.py:22
  63.0 0.0 collective-permute-done.2.refs_5_.refs_4_.refs_3_
  63.0 1.0 shard_map.87.refs_0_
  64.0 0.0 collective-permute-done.3.refs_7_.refs_2_
  64.0 0.0 collective-permute-done.5.refs_9_.refs_1_
  64.0 2.2 %shard_map.88 = (bf16[768,128]{1,0:T(8,128)(2,1)S(1)}, bf16[384,128]{1,0:T(8,128)(2,1)S(1)}, bf16[128,2048]{1,0:T(8,128)(2,1)S(1)}) custom-call(bf16[128,2048]{1,0:T(8,128)(2,1)S(1)} %collective-permute-done.8.refs_0_.refs_6_.refs_4_, bf16[1040,256]{1,0:T(8,128)(2,1)S(1)} %collective-permute-done.10.refs_1_.refs_10_.refs_8_, bf16[192,2048]{1,0:T(8,128)(2,1)S(1)} %bitcast.15, ...), custom_call_target="tpu_custom_call" | custom-call | flops 2000000000 | tf_op jit(solution)/shard_map/pallas_call | solution.py:41
  66.2 0.0 copy-start
  66.2 1.2 %collective-permute-start.16 = (bf16[128,2048]{1,0:T(8,128)(2,1)S(1)}, bf16[128,2048]{1,0:T(8,128)(2,1)S(1)}, u32[]{:S(2)}, u32[]{:S(2)}) collective-permute-start(bf16[128,2048]{1,0:T(8,128)(2,1)S(1)} %get-tuple-element.58), channel_id=1, source_target_pairs={{0,1},{1,3},{3,2},{2,0},{4,5},{5,7},{7,6},{6,4},{8,9},{9,11},{11,1... | collective-permute-start | bytes 1572872 | tf_op jit(solution)/shard_map/ppermute | solution.py:22
  67.4 2.2 %shard_map.86 = (bf16[768,128]{1,0:T(8,128)(2,1)S(1)}, bf16[384,128]{1,0:T(8,128)(2,1)S(1)}, bf16[128,2048]{1,0:T(8,128)(2,1)S(1)}) custom-call(bf16[128,2048]{1,0:T(8,128)(2,1)S(1)} %collective-permute-done.6.refs_0_.refs_5_.refs_3_, bf16[1040,256]{1,0:T(8,128)(2,1)S(1)} %collective-permute-done.7.refs_1_.refs_9_.refs_7_, bf16[192,2048]{1,0:T(8,128)(2,1)S(1)} %bitcast.16, ...), custom_call_target="tpu_custom_call" | custom-call | flops 2000000000 | tf_op jit(solution)/shard_map/pallas_call | solution.py:41
  69.7 0.0 copy-done
  69.7 2.2 %shard_map.85 = (bf16[768,128]{1,0:T(8,128)(2,1)S(1)}, bf16[384,128]{1,0:T(8,128)(2,1)S(1)}, bf16[128,2048]{1,0:T(8,128)(2,1)S(1)}) custom-call(bf16[128,2048]{1,0:T(8,128)(2,1)S(1)} %copy-done, bf16[1040,256]{1,0:T(8,128)(2,1)S(1)} %pad_maximum_fusion.refs_1_.refs_8_.refs_6_, bf16[192,2048]{1,0:T(8,128)(2,1)S(1)} %bitcast.17, ...), custom_call_target="tpu_custom_call" | custom-call | flops 2000000000 | tf_op jit(solution)/shard_map/pallas_call | solution.py:41
  71.9 2.5 %collective-permute-done.11.refs_11_.refs_9_ = bf16[1040,256]{1,0:T(8,128)(2,1)S(1)} collective-permute-done((bf16[1040,256]{1,0:T(8,128)(2,1)S(1)}, bf16[1040,256]{1,0:T(8,128)(2,1)S(1)}, u32[]{:S(2)}, u32[]{:S(2)}) %collective-permute-start.11) | collective-permute-done | bytes 532512 | tf_op jit(solution)/shard_map/ppermute | solution.py:22
  74.4 1.3 %shard_map.90 = (bf16[192,128]{1,0:T(8,128)(2,1)S(1)}, bf16[96,128]{1,0:T(8,128)(2,1)S(1)}, bf16[96,2048]{1,0:T(8,128)(2,1)S(1)}, bf16[96,2048]{1,0:T(8,128)(2,1)S(1)}, bf16[96,2048]{1,0:T(8,128)(2,1)S(1)}) custom-call(f32[768,128]{1,0:T(8,128)S(1)} %shard_map.87.refs_0_, bf16[96,2048]{1,0:T(8,128)(2,1)S(1)} %collective-permute-done.5.refs_9_.refs_1_, ...), custom_call_target="tpu_custom_call" | custom-call | flops 1000000000 | tf_op jit(solution)/shard_map/pallas_call | solution.py:41
  75.8 0.1 collective-permute-start.12
  75.8 0.5 collective-permute-start.13
  76.3 0.1 collective-permute-start.14
  76.4 1.7 %shard_map.89 = (bf16[576,128]{1,0:T(8,128)(2,1)S(1)}, bf16[288,128]{1,0:T(8,128)(2,1)S(1)}, bf16[288,2048]{1,0:T(8,128)(2,1)S(1)}) custom-call(f32[768,128]{1,0:T(8,128)S(1)} %shard_map.87.refs_0_, bf16[96,2048]{1,0:T(8,128)(2,1)S(1)} %bitcast.24, bf16[96,2048]{1,0:T(8,128)(2,1)S(1)} %collective-permute-done.3.refs_7_.refs_2_, ...), custom_call_target="tpu_custom_call" | custom-call | flops 5000000000 | tf_op jit(solution)/shard_map/pallas_call | solution.py:41
  78.1 0.0 collective-permute-done.12.refs_1_
  78.1 0.0 collective-permute-done.13.refs_2_
  78.1 0.5 collective-permute-done.14.refs_3_
  78.7 0.3 shard_map.91
  78.9 1.9 %collective-permute-start.18 = (bf16[288,2048]{1,0:T(8,128)(2,1)S(1)}, bf16[288,2048]{1,0:T(8,128)(2,1)S(1)}, u32[]{:S(2)}, u32[]{:S(2)}) collective-permute-start(bf16[288,2048]{1,0:T(8,128)(2,1)S(1)} %shard_map.91), channel_id=1, source_target_pairs={{0,8},{4,12},{8,0},{12,4},{1,9},{5,13},{9,1},{13,5},{2,10},{6,14},... | collective-permute-start | bytes 3538952 | tf_op jit(solution)/shard_map/ppermute | solution.py:26
  80.9 1.7 %collective-permute-start.15 = (bf16[128,2048]{1,0:T(8,128)(2,1)S(1)}, bf16[128,2048]{1,0:T(8,128)(2,1)S(1)}, u32[]{:S(2)}, u32[]{:S(2)}) collective-permute-start(bf16[128,2048]{1,0:T(8,128)(2,1)S(1)} %get-tuple-element.56), channel_id=1, source_target_pairs={{0,2},{1,0},{3,1},{2,3},{4,6},{5,4},{7,5},{6,7},{8,10},{9,8},{11,9... | collective-permute-start | bytes 1572872 | tf_op jit(solution)/shard_map/ppermute | solution.py:22
  82.6 2.2 %shard_map.92 = (bf16[128,2048]{1,0:T(8,128)(2,1)S(1)}, bf16[288,2048]{1,0:T(8,128)(2,1)S(1)}, bf16[288,2048]{1,0:T(8,128)(2,1)S(1)}) custom-call(bf16[192,2048]{1,0:T(8,128)(2,1)S(1)} %bitcast.18, bf16[192,2048]{1,0:T(8,128)(2,1)S(1)} %collective-permute-done.refs_3_.refs_2_.refs_1_, bf16[192,2048]{1,0:T(8,128)(2,1)S(1)} %collective-permute-done.1.refs_4_.refs_3_.refs_2_, ...), custom_call_target="tpu_custom_call" | custom-call | flops 2000000000 | tf_op jit(solution)/shard_map/pallas_call | solution.py:41
  84.8 0.1 collective-permute-start.19
  84.9 0.0 collective-permute-done.16.refs_0_
  84.9 0.1 shard_map.93
  85.0 13.0 %collective-permute-start.17 = (bf16[128,2048]{1,0:T(8,128)(2,1)S(1)}, bf16[128,2048]{1,0:T(8,128)(2,1)S(1)}, u32[]{:S(2)}, u32[]{:S(2)}) collective-permute-start(bf16[128,2048]{1,0:T(8,128)(2,1)S(1)} %shard_map.93), channel_id=1, source_target_pairs={{0,1},{1,3},{3,2},{2,0},{4,5},{5,7},{7,6},{6,4},{8,9},{9,11},{11,1... | collective-permute-start | bytes 1572872 | tf_op jit(solution)/shard_map/ppermute | solution.py:22
  98.0 0.0 collective-permute-done.15.refs_1_
  98.0 10.4 %collective-permute-done.17.refs_2_ = bf16[128,2048]{1,0:T(8,128)(2,1)S(1)} collective-permute-done((bf16[128,2048]{1,0:T(8,128)(2,1)S(1)}, bf16[128,2048]{1,0:T(8,128)(2,1)S(1)}, u32[]{:S(2)}, u32[]{:S(2)}) %collective-permute-start.17) | collective-permute-done | bytes 524320 | tf_op jit(solution)/shard_map/ppermute | solution.py:22
  108.5 0.0 collective-permute-done.19.refs_5_
  108.5 0.0 collective-permute-done.18.refs_4_
  108.5 1.8 %shard_map.94 = (bf16[128,2048]{1,0:T(8,128)(2,1)}, f32[192,2048]{1,0:T(8,128)}, f32[96,2048]{1,0:T(8,128)}) custom-call(bf16[128,2048]{1,0:T(8,128)(2,1)S(1)} %get-tuple-element.44.refs_0_, bf16[128,2048]{1,0:T(8,128)(2,1)S(1)} %collective-permute-done.15.refs_1_, bf16[128,2048]{1,0:T(8,128)(2,1)S(1)} %collective-permute-done.17.refs_2_, ...), custom_call_target="tpu_custom_call" | custom-call | flops 2000000000 | tf_op jit(solution)/shard_map/pallas_call | solution.py:167
  (4 shorter events, 0.1 us)
Async XLA Ops:
  0.6 18.3 %copy-start.1 = (bf16[1,2,96,2048]{3,2,1,0:T(8,128)(2,1)S(1)}, bf16[1,2,96,2048]{3,2,1,0:T(8,128)(2,1)}, u32[]{:S(2)}) copy-start(bf16[1,2,96,2048]{3,2,1,0:T(8,128)(2,1)} %param.12) | copy-start | bytes 2359300
  0.6 40.9 %copy-start.2 = (bf16[1,96,2048]{2,1,0:T(8,128)(2,1)S(1)}, bf16[1,96,2048]{2,1,0:T(8,128)(2,1)}, u32[]{:S(2)}) copy-start(bf16[1,96,2048]{2,1,0:T(8,128)(2,1)} %param.13) | copy-start | bytes 1179652
  0.7 17.1 %collective-permute-start.6 = (bf16[128,2048]{1,0:T(8,128)(2,1)}, bf16[128,2048]{1,0:T(8,128)(2,1)S(1)}, u32[]{:S(2)}, u32[]{:S(2)}) collective-permute-start(bf16[128,2048]{1,0:T(8,128)(2,1)} %refs_4_.3), channel_id=1, source_target_pairs={{0,1},{1,3},{3,2},{2,0},{4,5},{5,7},{7,6},{6,4},{8,9},{9,11},{11,1... | collective-permute-start | bytes 1572872 | tf_op jit(solution)/shard_map/ppermute | solution.py:22
  4.5 19.2 %collective-permute-start.1 = (bf16[192,2048]{1,0:T(8,128)(2,1)}, bf16[192,2048]{1,0:T(8,128)(2,1)S(1)}, u32[]{:S(2)}, u32[]{:S(2)}) collective-permute-start(bf16[192,2048]{1,0:T(8,128)(2,1)} %bitcast.12), channel_id=1, source_target_pairs={{0,8},{4,12},{8,0},{12,4},{1,9},{5,13},{9,1},{13,5},{2,10},{6,14},... | collective-permute-start | bytes 2359304 | tf_op jit(solution)/shard_map/ppermute | solution.py:26
  7.2 22.0 %collective-permute-start.7 = (bf16[1040,256]{1,0:T(8,128)(2,1)S(1)}, bf16[1040,256]{1,0:T(8,128)(2,1)S(1)}, u32[]{:S(2)}, u32[]{:S(2)}) collective-permute-start(bf16[1040,256]{1,0:T(8,128)(2,1)S(1)} %pad_maximum_fusion.refs_1_.refs_8_.refs_6_), channel_id=1, source_target_pairs={{0,1},{1,3},{3,2},{2,0},{4,5},{5,7},{7,6},{6,4},{8,9},{9,11},{11,1... | collective-permute-start | bytes 1597448 | tf_op jit(solution)/shard_map/ppermute | solution.py:22
  17.7 22.6 %collective-permute-start.8 = (bf16[128,2048]{1,0:T(8,128)(2,1)S(1)}, bf16[128,2048]{1,0:T(8,128)(2,1)S(1)}, u32[]{:S(2)}, u32[]{:S(2)}) collective-permute-start(bf16[128,2048]{1,0:T(8,128)(2,1)S(1)} %collective-permute-done.6.refs_0_.refs_5_.refs_3_), channel_id=1, source_target_pairs={{0,1},{1,3},{3,2},{2,0},{4,5},{5,7},{7,6},{6,4},{8,9},{9,11},{11,1... | collective-permute-start | bytes 1572872 | tf_op jit(solution)/shard_map/ppermute | solution.py:22
  19.0 31.1 %collective-permute-start = (bf16[192,2048]{1,0:T(8,128)(2,1)S(1)}, bf16[192,2048]{1,0:T(8,128)(2,1)S(1)}, u32[]{:S(2)}, u32[]{:S(2)}) collective-permute-start(bf16[192,2048]{1,0:T(8,128)(2,1)S(1)} %bitcast.13), channel_id=1, source_target_pairs={{0,4},{4,0},{8,12},{12,8},{1,5},{5,1},{9,13},{13,9},{2,6},{6,2},{1... | collective-permute-start | bytes 2359304 | tf_op jit(solution)/shard_map/ppermute | solution.py:26
  23.7 39.3 %collective-permute-start.2 = (bf16[192,2048]{1,0:T(8,128)(2,1)S(1)}, bf16[192,2048]{1,0:T(8,128)(2,1)S(1)}, u32[]{:S(2)}, u32[]{:S(2)}) collective-permute-start(bf16[192,2048]{1,0:T(8,128)(2,1)S(1)} %collective-permute-done.1.refs_4_.refs_3_.refs_2_), channel_id=1, source_target_pairs={{0,4},{4,0},{8,12},{12,8},{1,5},{5,1},{9,13},{13,9},{2,6},{6,2},{1... | collective-permute-start | bytes 2359304 | tf_op jit(solution)/shard_map/ppermute | solution.py:26
  29.1 22.6 %collective-permute-start.10 = (bf16[1040,256]{1,0:T(8,128)(2,1)S(1)}, bf16[1040,256]{1,0:T(8,128)(2,1)S(1)}, u32[]{:S(2)}, u32[]{:S(2)}) collective-permute-start(bf16[1040,256]{1,0:T(8,128)(2,1)S(1)} %collective-permute-done.7.refs_1_.refs_9_.refs_7_), channel_id=1, source_target_pairs={{0,1},{1,3},{3,2},{2,0},{4,5},{5,7},{7,6},{6,4},{8,9},{9,11},{11,1... | collective-permute-start | bytes 1597448 | tf_op jit(solution)/shard_map/ppermute | solution.py:22
  40.4 22.6 %collective-permute-start.9 = (bf16[128,2048]{1,0:T(8,128)(2,1)S(1)}, bf16[128,2048]{1,0:T(8,128)(2,1)S(1)}, u32[]{:S(2)}, u32[]{:S(2)}) collective-permute-start(bf16[128,2048]{1,0:T(8,128)(2,1)S(1)} %collective-permute-done.8.refs_0_.refs_6_.refs_4_), channel_id=1, source_target_pairs={{0,1},{1,3},{3,2},{2,0},{4,5},{5,7},{7,6},{6,4},{8,9},{9,11},{11,1... | collective-permute-start | bytes 1572872 | tf_op jit(solution)/shard_map/ppermute | solution.py:22
  41.5 8.6 %collective-permute-start.4 = (bf16[96,2048]{1,0:T(8,128)(2,1)S(1)}, bf16[96,2048]{1,0:T(8,128)(2,1)S(1)}, u32[]{:S(2)}, u32[]{:S(2)}) collective-permute-start(bf16[96,2048]{1,0:T(8,128)(2,1)S(1)} %bitcast.19), channel_id=1, source_target_pairs={{0,8},{4,12},{8,0},{12,4},{1,9},{5,13},{9,1},{13,5},{2,10},{6,14},... | collective-permute-start | bytes 1179656 | tf_op jit(solution)/shard_map/ppermute | solution.py:26
  50.1 13.9 %collective-permute-start.3 = (bf16[96,2048]{1,0:T(8,128)(2,1)S(1)}, bf16[96,2048]{1,0:T(8,128)(2,1)S(1)}, u32[]{:S(2)}, u32[]{:S(2)}) collective-permute-start(bf16[96,2048]{1,0:T(8,128)(2,1)S(1)} %bitcast.20), channel_id=1, source_target_pairs={{0,4},{4,0},{8,12},{12,8},{1,5},{5,1},{9,13},{13,9},{2,6},{6,2},{1... | collective-permute-start | bytes 1179656 | tf_op jit(solution)/shard_map/ppermute | solution.py:26
  50.1 13.9 %collective-permute-start.5 = (bf16[96,2048]{1,0:T(8,128)(2,1)S(1)}, bf16[96,2048]{1,0:T(8,128)(2,1)S(1)}, u32[]{:S(2)}, u32[]{:S(2)}) collective-permute-start(bf16[96,2048]{1,0:T(8,128)(2,1)S(1)} %collective-permute-done.4.refs_8_.refs_3_), channel_id=1, source_target_pairs={{0,4},{4,0},{8,12},{12,8},{1,5},{5,1},{9,13},{13,9},{2,6},{6,2},{1... | collective-permute-start | bytes 1179656 | tf_op jit(solution)/shard_map/ppermute | solution.py:26
  51.8 22.6 %collective-permute-start.11 = (bf16[1040,256]{1,0:T(8,128)(2,1)S(1)}, bf16[1040,256]{1,0:T(8,128)(2,1)S(1)}, u32[]{:S(2)}, u32[]{:S(2)}) collective-permute-start(bf16[1040,256]{1,0:T(8,128)(2,1)S(1)} %collective-permute-done.10.refs_1_.refs_10_.refs_8_), channel_id=1, source_target_pairs={{0,1},{1,3},{3,2},{2,0},{4,5},{5,7},{7,6},{6,4},{8,9},{9,11},{11,1... | collective-permute-start | bytes 1597448 | tf_op jit(solution)/shard_map/ppermute | solution.py:22
  66.2 3.5 %copy-start = (bf16[128,2048]{1,0:T(8,128)(2,1)S(1)}, bf16[128,2048]{1,0:T(8,128)(2,1)}, u32[]{:S(2)}) copy-start(bf16[128,2048]{1,0:T(8,128)(2,1)} %refs_4_.3) | copy-start | bytes 1572868
  66.2 18.7 %collective-permute-start.16 = (bf16[128,2048]{1,0:T(8,128)(2,1)S(1)}, bf16[128,2048]{1,0:T(8,128)(2,1)S(1)}, u32[]{:S(2)}, u32[]{:S(2)}) collective-permute-start(bf16[128,2048]{1,0:T(8,128)(2,1)S(1)} %get-tuple-element.58), channel_id=1, source_target_pairs={{0,1},{1,3},{3,2},{2,0},{4,5},{5,7},{7,6},{6,4},{8,9},{9,11},{11,1... | collective-permute-start | bytes 1572872 | tf_op jit(solution)/shard_map/ppermute | solution.py:22
  75.8 2.3 %collective-permute-start.12 = (bf16[96,2048]{1,0:T(8,128)(2,1)S(1)}, bf16[96,2048]{1,0:T(8,128)(2,1)S(1)}, u32[]{:S(2)}, u32[]{:S(2)}) collective-permute-start(bf16[96,2048]{1,0:T(8,128)(2,1)S(1)} %get-tuple-element.53), channel_id=1, source_target_pairs={{0,4},{4,0},{8,12},{12,8},{1,5},{5,1},{9,13},{13,9},{2,6},{6,2},{1... | collective-permute-start | bytes 1179656 | tf_op jit(solution)/shard_map/ppermute | solution.py:26
  75.8 2.3 %collective-permute-start.13 = (bf16[96,2048]{1,0:T(8,128)(2,1)S(1)}, bf16[96,2048]{1,0:T(8,128)(2,1)S(1)}, u32[]{:S(2)}, u32[]{:S(2)}) collective-permute-start(bf16[96,2048]{1,0:T(8,128)(2,1)S(1)} %get-tuple-element.54), channel_id=1, source_target_pairs={{0,4},{4,0},{8,12},{12,8},{1,5},{5,1},{9,13},{13,9},{2,6},{6,2},{1... | collective-permute-start | bytes 1179656 | tf_op jit(solution)/shard_map/ppermute | solution.py:26
  76.3 2.3 %collective-permute-start.14 = (bf16[96,2048]{1,0:T(8,128)(2,1)S(1)}, bf16[96,2048]{1,0:T(8,128)(2,1)S(1)}, u32[]{:S(2)}, u32[]{:S(2)}) collective-permute-start(bf16[96,2048]{1,0:T(8,128)(2,1)S(1)} %get-tuple-element.55), channel_id=1, source_target_pairs={{0,4},{4,0},{8,12},{12,8},{1,5},{5,1},{9,13},{13,9},{2,6},{6,2},{1... | collective-permute-start | bytes 1179656 | tf_op jit(solution)/shard_map/ppermute | solution.py:26
  78.9 29.5 %collective-permute-start.18 = (bf16[288,2048]{1,0:T(8,128)(2,1)S(1)}, bf16[288,2048]{1,0:T(8,128)(2,1)S(1)}, u32[]{:S(2)}, u32[]{:S(2)}) collective-permute-start(bf16[288,2048]{1,0:T(8,128)(2,1)S(1)} %shard_map.91), channel_id=1, source_target_pairs={{0,8},{4,12},{8,0},{12,4},{1,9},{5,13},{9,1},{13,5},{2,10},{6,14},... | collective-permute-start | bytes 3538952 | tf_op jit(solution)/shard_map/ppermute | solution.py:26
  80.9 17.1 %collective-permute-start.15 = (bf16[128,2048]{1,0:T(8,128)(2,1)S(1)}, bf16[128,2048]{1,0:T(8,128)(2,1)S(1)}, u32[]{:S(2)}, u32[]{:S(2)}) collective-permute-start(bf16[128,2048]{1,0:T(8,128)(2,1)S(1)} %get-tuple-element.56), channel_id=1, source_target_pairs={{0,2},{1,0},{3,1},{2,3},{4,6},{5,4},{7,5},{6,7},{8,10},{9,8},{11,9... | collective-permute-start | bytes 1572872 | tf_op jit(solution)/shard_map/ppermute | solution.py:22
  84.8 23.6 %collective-permute-start.19 = (bf16[288,2048]{1,0:T(8,128)(2,1)S(1)}, bf16[288,2048]{1,0:T(8,128)(2,1)S(1)}, u32[]{:S(2)}, u32[]{:S(2)}) collective-permute-start(bf16[288,2048]{1,0:T(8,128)(2,1)S(1)} %get-tuple-element.67), channel_id=1, source_target_pairs={{0,4},{4,0},{8,12},{12,8},{1,5},{5,1},{9,13},{13,9},{2,6},{6,2},{1... | collective-permute-start | bytes 3538952 | tf_op jit(solution)/shard_map/ppermute | solution.py:26
  85.0 23.4 %collective-permute-start.17 = (bf16[128,2048]{1,0:T(8,128)(2,1)S(1)}, bf16[128,2048]{1,0:T(8,128)(2,1)S(1)}, u32[]{:S(2)}, u32[]{:S(2)}) collective-permute-start(bf16[128,2048]{1,0:T(8,128)(2,1)S(1)} %shard_map.93), channel_id=1, source_target_pairs={{0,1},{1,3},{3,2},{2,0},{4,5},{5,7},{7,6},{6,4},{8,9},{9,11},{11,1... | collective-permute-start | bytes 1572872 | tf_op jit(solution)/shard_map/ppermute | solution.py:22
